TPU v7x, 32 devices: a whole 2x2x4 slice. The times are simulated.
32 devices in a mesh: groups: 2 (over x), seq: 2 (over core), tp: 8 (over z, y).
Axes of the slice: x: 2, y: 2, z: 4, core: 2. Of those that a mesh axis runs over, the one named last changes fastest.
Arguments:
- loaded: bfloat16 [3072, 4096], P(('groups', 'seq'), 'tp'), parts along dimension 0, may hold values from -6 to 6
- block_counts: int32 [8], P(('groups', 'seq')), parts along dimension 0, may hold values from 1 to 3, 8 in all
- seq_order: int32 [16], P('groups'), parts along dimension 0, may hold values from 0 to 7, each once
- gate_weight: bfloat16 [4096, 14336], P(None, 'tp'), may hold values from -0.09375 to 0.09375
- up_weight: bfloat16 [4096, 14336], P(None, 'tp'), may hold values from -0.09375 to 0.09375
- down_weight: bfloat16 [14336, 4096], P('tp'), may hold values from -0.0625 to 0.0625
Outputs:
- ffn_output: bfloat16 [2048, 4096], P(('groups', 'seq'), 'tp'), parts along dimension 0
There are 2 independent parts, one for each index of `groups`. A program takes and returns all parts, laid end to end along the dimension named above; an argument that names none is the same for every part. Nothing has to cross between parts.
Inputs may be any that keep to these rules, and one draw needn't show every extreme that they name: A loader's live blocks are its first block_counts slots; the counts sum to 8 and the largest is exactly 3. `seq_order`: each of the 8 block positions appears once.
All inputs are finite; a program needn't handle non-finite values.
Results may differ from a plain program's by a relative error of at most 0.013.
Values may be sent and summed in bfloat16 or wider, within the bound.
No kernel may reach another device: no remote copies, remote signals or barrier semaphores. Data moves between devices by JAX's collectives and lax.ppermute only.
A program may use at most 128 MiB of HBM per device.

v0:
```python
import jax
import jax.numpy as jnp
from jax import lax
from jax.sharding import PartitionSpec as P

BLOCK = 128


def redistribute(slot_rows, block_counts, seq_order):
    dev_slots = slot_rows.shape[0] // BLOCK
    local_loaders = block_counts.shape[0]
    loader_slots = dev_slots // local_loaders
    row_width = slot_rows.shape[1]
    all_blocks = seq_order.shape[0]
    seq_ways = lax.axis_size("seq")
    own_slots = all_blocks // seq_ways
    flat_rows = slot_rows.reshape(dev_slots, BLOCK * row_width)
    block_ids = jnp.arange(all_blocks, dtype=jnp.int32)
    every_row, every_count = (
        lax.all_gather(flat_rows, "seq", axis=0, tiled=True),
        lax.all_gather(block_counts, "seq", axis=0, tiled=True),
    )
    offsets = jnp.cumsum(every_count) - every_count
    positions = lax.axis_index("seq") * own_slots + jnp.arange(own_slots, dtype=jnp.int32)
    matches = seq_order[None, :] == positions[:, None]
    source = jnp.sum(jnp.where(matches, block_ids[None, :], 0), axis=1)
    inside = (source[:, None] >= offsets[None, :]) & (
        source[:, None] < (offsets + every_count)[None, :]
    )
    loader_ids = jnp.arange(every_count.shape[0], dtype=jnp.int32)
    row_ids = jnp.sum(
        jnp.where(
            inside, loader_ids[None, :] * loader_slots + source[:, None] - offsets[None, :], 0
        ),
        axis=1,
    )
    merged = jnp.take(every_row, row_ids, axis=0)
    return merged.reshape(own_slots * BLOCK, row_width)


def feed_forward(row_data, gate_weight, up_weight, down_weight):
    part_cols = lax.all_gather(row_data, "tp", axis=1, tiled=True)
    gate_proj = jnp.dot(part_cols, gate_weight, preferred_element_type=jnp.float32)
    up_proj = jnp.dot(part_cols, up_weight, preferred_element_type=jnp.float32)
    hidden = (jax.nn.silu(gate_proj) * up_proj).astype(jnp.bfloat16)
    partial_value = jnp.dot(hidden, down_weight, preferred_element_type=jnp.float32)
    return lax.psum_scatter(
        partial_value.astype(jnp.bfloat16), "tp", scatter_dimension=1, tiled=True
    )


def body(loaded, block_counts, seq_order, gate_weight, up_weight, down_weight):
    computed = feed_forward(loaded, gate_weight, up_weight, down_weight)
    return redistribute(computed, block_counts, seq_order)


def solution(mesh):
    return jax.shard_map(
        body,
        mesh=mesh,
        in_specs=(
            P(("groups", "seq"), "tp"),
            P(("groups", "seq")),
            P("groups"),
            P(None, "tp"),
            P(None, "tp"),
            P("tp", None),
        ),
        out_specs=P(("groups", "seq"), "tp"),
        check_vma=False,
    )
```

profile of v0, /device:TPU:0, one launch (start us, length us, event | category | flops | bytes accessed | tf_op | source)
XLA Modules:
  0.0 307.9 jit_solution(6651016675551678369)
XLA Ops:
  6.5 0.0 all-gather.4.cloned.1.call-start
  6.5 0.7 all-gather.4.cloned.1.call-update
  7.3 0.0 reduce-scatter.2.cloned.1.call-start
  7.3 104.8 %all-gather.4.cloned.1.call-done = bf16[768,4096]{1,0:T(8,128)(2,1)} async-done(((bf16[768,512]{1,0:T(8,128)(2,1)}), bf16[768,4096]{1,0:T(8,128)(2,1)}) %all-gather.4.cloned.1.call-update) | async-done | bytes 6291472 | tf_op jit(solution)/shard_map/all_gather | solution.py:42
  112.1 18.1 %fusion.2 = f32[768,1792]{1,0:T(8,128)} fusion(bf16[768,4096]{1,0:T(8,128)(2,1)} %all-gather.4.cloned.1.call-done, bf16[4096,1792]{1,0:T(8,128)(2,1)} %param.9), kind=kOutput, calls=%fused_computation.16 | convolution fusion | flops 11274289152 | bytes 26476544 | tf_op jit(solution)/shard_map/dot_general | solution.py:43
  130.2 37.0 %convolution_convert_fusion = bf16[768,4096]{1,0:T(8,128)(2,1)} fusion(bf16[1792,4096]{1,0:T(8,128)(2,1)} %param.11, f32[768,1792]{1,0:T(8,128)} %fusion.2, bf16[768,4096]{1,0:T(8,128)(2,1)} %all-gather.4.cloned.1.call-done, bf16[4096,1792]{1,0:T(8,128)(2,1)} %param.10), kind=kOutput, calls=%fused_computation.1 | convolution fusion | flops 22559981568 | bytes 47448064 | tf_op jit(solution)/shard_map/dot_general | solution.py:46
  167.1 0.0 reduce-scatter.2.cloned.1.call-update
  167.2 0.2 all-gather.6.cloned.1.call-start
  167.4 116.5 %reduce-scatter.2.cloned.1.call-done = bf16[768,512]{1,0:T(8,128)(2,1)} async-done(((bf16[768,4096]{1,0:T(8,128)(2,1)}), bf16[768,512]{1,0:T(8,128)(2,1)}) %reduce-scatter.2.cloned.1.call-update) | async-done | bytes 786448 | tf_op jit(solution)/shard_map/reduce_scatter | solution.py:47
  283.9 3.0 reshape.73
  286.9 0.0 all-gather.6.cloned.1.call-update
  286.9 0.6 dynamic-slice
  288.2 0.0 copy-done
  288.2 0.2 dynamic-update-slice
  288.4 1.8 all-reduce
  290.2 0.2 reduce-window.8
  290.4 0.2 select_reduce_fusion.1
  290.6 0.2 select_reduce_fusion
  290.8 0.1 broadcast_bitcast_fusion
  290.9 5.9 %all-gather.6.cloned.1.call-done = bf16[2,6,65536]{2,1,0:T(8,128)(2,1)} async-done(((bf16[1,6,65536]{2,1,0:T(8,128)(2,1)}), bf16[2,6,65536]{2,1,0:T(8,128)(2,1)}) %all-gather.6.cloned.1.call-update) | async-done | bytes 1572880 | tf_op jit(solution)/shard_map/all_gather | solution.py:20
  296.8 2.1 reshape.74
  298.9 1.1 gather_fusion
  300.0 0.4 gather.7
  300.4 0.9 broadcast_select_fusion
  (12 shorter events, 0.0 us)
Async XLA Ops:
  6.5 105.5 %all-gather.4.cloned.1.call-start = ((), (), s32[]{:S(2)}) async-start(), calls=%async_computation.1 | async-start | bytes 7077888 | tf_op jit(solution)/shard_map/all_gather | solution.py:42
  7.3 276.6 %reduce-scatter.2.cloned.1.call-start = ((), (), s32[]{:S(2)}) async-start(), calls=%async_computation.2 | async-start | bytes 7077888 | tf_op jit(solution)/shard_map/reduce_scatter | solution.py:47
  167.1 119.8 %copy-start.2 = (u32[32]{0:T(128)S(1)}, u32[32]{0:T(128)}, u32[]{:S(2)}) copy-start(u32[32]{0:T(128)} %constant.36) | copy-start | bytes 388
  167.1 121.1 %copy-start = (s32[2]{0:T(128)S(1)}, s32[2]{0:T(128)}, u32[]{:S(2)}) copy-start(s32[2]{0:T(128)} %param.7) | copy-start | bytes 28
  167.1 123.3 %copy-start.1 = (s32[8]{0:T(128)S(1)}, s32[8]{0:T(128)}, u32[]{:S(2)}) copy-start(s32[8]{0:T(128)} %param.8) | copy-start | bytes 100
  167.2 129.6 %all-gather.6.cloned.1.call-start = ((), (), s32[]{:S(2)}) async-start(), calls=%async_computation.3 | async-start | bytes 3145728 | tf_op jit(solution)/shard_map/all_gather | solution.py:20
Sparse Core Ops, SparseCore 0:
  9.4 102.6 all-gather.3
  167.3 116.5 reduce-scatter.1
  287.0 9.7 all-gather.5
where the time goes:
time: 308 us
  waiting for transfers between devices  228 us (74%)
  matrix products  55.1 us (18%)
  between operations  13.8 us (4%)
  local copies, waits for them, and re-layouts  7.56 us (2%)
    reduce_scatter x1, waiting for transfers between devices, feed_forward(): lax.psum_scatter(partial_value.astype(jnp.bfloat16), 'tp', scatter_dimens...  116 us
    all_gather x1, waiting for transfers between devices, feed_forward(): part_cols = lax.all_gather(row_data, 'tp', axis=1, tiled=True)  105 us
    dot_general x1, matrix products, feed_forward(): jnp.dot(hidden, down_weight, preferred_element_type=jnp.float32)  37 us
    dot_general x1, matrix products, feed_forward(): jnp.dot(part_cols, gate_weight, preferred_element_type=jnp.float32)  18.1 us
  transfers between devices with their start and end apart: 3, of which 3 were waited for; matrix products, arithmetic and copies ran while one was open for 0% of the time, Pallas kernels for 0%

commit v1 on v0

v1 whole, which is shorter than its diff:
```python
import functools

import jax
import jax.numpy as jnp
from jax import lax
from jax.experimental import pallas as pl
from jax.experimental.pallas import tpu as pltpu
from jax.sharding import PartitionSpec as P

BLOCK = 128
F32 = jnp.float32
BF16 = jnp.bfloat16
MIB = 1024 * 1024


def ring_order(n):
    if n == 8:
        return list(range(0, n, 2)) + list(range(n - 1, 0, -2))
    return list(range(n))


def shift(order, step):
    n = len(order)
    return [(order[i], order[(i + step) % n]) for i in range(n)]


def pack_kernel(mine_c, other_c, order, seq_at, mine, other, out, sems):
    loaders = mine_c.shape[0]
    blocks = order.shape[0]
    slots = mine.shape[0] // BLOCK // loaders
    own = out.shape[0] // BLOCK
    me = seq_at[0]

    first = [jnp.where(me == 0, mine_c[i], other_c[i]) for i in range(loaders)]
    second = [jnp.where(me == 0, other_c[i], mine_c[i]) for i in range(loaders)]
    counts = first + second
    copies = []
    for i in range(own):
        place = me * own + i
        source = jnp.int32(0)
        for b in range(blocks):
            source = jnp.where(order[b] == place, b, source)
        offset = jnp.int32(0)
        row = jnp.int32(0)
        for s in range(2 * loaders):
            inside = (source >= offset) & (source < offset + counts[s])
            row = jnp.where(inside, s * slots + source - offset, row)
            offset = offset + counts[s]
        holder = jnp.where(row >= loaders * slots, 1, 0)
        row = row - holder * (loaders * slots)
        start = pl.multiple_of(row * BLOCK, BLOCK)

        @pl.when(holder == me)
        def _(start=start, i=i):
            pltpu.make_async_copy(
                mine.at[pl.ds(start, BLOCK)], out.at[pl.ds(i * BLOCK, BLOCK)], sems.at[i]
            ).start()

        @pl.when(holder != me)
        def _(start=start, i=i):
            pltpu.make_async_copy(
                other.at[pl.ds(start, BLOCK)], out.at[pl.ds(i * BLOCK, BLOCK)], sems.at[i]
            ).start()

    for i in range(own):
        pltpu.make_async_copy(
            mine.at[pl.ds(0, BLOCK)], out.at[pl.ds(i * BLOCK, BLOCK)], sems.at[i]
        ).wait()


def pack(loaded, block_counts, seq_order):
    swap = [(0, 1), (1, 0)]
    other = lax.ppermute(loaded, "seq", swap)
    other_counts = lax.ppermute(block_counts, "seq", swap)
    own = seq_order.shape[0] // 2
    width = loaded.shape[1]
    seq_at = lax.axis_index("seq").astype(jnp.int32).reshape(1)
    any_spec = pl.BlockSpec(memory_space=pl.ANY)
    return pl.pallas_call(
        pack_kernel,
        out_shape=jax.ShapeDtypeStruct((own * BLOCK, width), loaded.dtype),
        grid_spec=pltpu.PrefetchScalarGridSpec(
            num_scalar_prefetch=4,
            grid=(1,),
            in_specs=[any_spec, any_spec],
            out_specs=any_spec,
            scratch_shapes=[pltpu.SemaphoreType.DMA((own,))],
        ),
    )(block_counts, other_counts, seq_order, seq_at, loaded, other)


def stage_kernel(pieces, has_acc, last, *refs):
    refs = list(refs[1:])
    xs = [(refs.pop(0), refs.pop(0)) for _ in range(pieces)]
    gws = [refs.pop(0) for _ in range(pieces)]
    uws = [refs.pop(0) for _ in range(pieces)]
    acc = [refs.pop(0), refs.pop(0)] if has_acc else None
    half = xs[0][0].shape[0]
    for c in range(2):
        rows = pl.ds(c * half, half)
        sums = []
        for k, ws in enumerate((gws, uws)):
            total = acc[k][rows, :] if has_acc else None
            for p in range(pieces):
                term = jnp.dot(xs[p][c][...], ws[p][...], preferred_element_type=F32)
                total = term if total is None else total + term
            sums.append(total)
        if last:
            gate, up = sums
            refs[0][rows, :] = (gate / (1.0 + jnp.exp(-gate)) * up).astype(BF16)
        else:
            refs[0][rows, :] = sums[0]
            refs[1][rows, :] = sums[1]


def stage(xs, owners, gate_weight, up_weight, acc, last, tile):
    pieces = len(xs)
    half, width = xs[0][0].shape
    hid = gate_weight.shape[1]
    x_spec = pl.BlockSpec((half, width), lambda i, own: (0, 0))
    w_specs = [
        pl.BlockSpec((width, tile), functools.partial(lambda p, i, own: (own[p], i), p))
        for p in range(pieces)
    ]
    full = pl.BlockSpec((2 * half, tile), lambda i, own: (0, i))
    operands = [x for pair in xs for x in pair] + [gate_weight] * pieces + [up_weight] * pieces
    in_specs = [x_spec] * (2 * pieces) + w_specs * 2
    aliases = {}
    if acc is not None:
        if not last:
            aliases = {1 + len(operands): 0, 2 + len(operands): 1}
        operands += list(acc)
        in_specs += [full, full]
    if last:
        out_shape = jax.ShapeDtypeStruct((2 * half, hid), BF16)
        out_specs = full
    else:
        out_shape = [jax.ShapeDtypeStruct((2 * half, hid), F32)] * 2
        out_specs = [full, full]
    return pl.pallas_call(
        functools.partial(stage_kernel, pieces, acc is not None, last),
        out_shape=out_shape,
        grid_spec=pltpu.PrefetchScalarGridSpec(
            num_scalar_prefetch=1,
            grid=(hid // tile,),
            in_specs=in_specs,
            out_specs=out_specs,
        ),
        input_output_aliases=aliases,
        compiler_params=pltpu.CompilerParams(vmem_limit_bytes=48 * MIB),
        cost_estimate=pl.CostEstimate(
            flops=2 * 2 * half * width * pieces * hid * 2,
            bytes_accessed=2 * width * pieces * hid * 2 + 2 * 2 * 2 * half * hid * 4,
            transcendentals=0,
        ),
    )(owners, *operands)


def body(loaded, block_counts, seq_order, gate_weight, up_weight, down_weight):
    n = lax.axis_size("tp")
    order = ring_order(n)
    table = jnp.array(order, jnp.int32)
    where = jnp.array([order.index(i) for i in range(n)], jnp.int32)
    at = where[lax.axis_index("tp")]
    fwd, bwd = shift(order, 1), shift(order, -1)
    far = n // 2

    def owner(step):
        return table[lax.rem(at + step + n, n)]

    packed = pack(loaded, block_counts, seq_order)
    half = packed.shape[0] // 2
    width = packed.shape[1]

    a_f = a_b = packed[:half]
    b_f = b_b = packed[half:]
    fresh = [((a_f, b_f), owner(0))]
    acc = None
    for step in range(1, far):
        a_f = lax.ppermute(a_f, "tp", fwd)
        a_b = lax.ppermute(a_b, "tp", bwd)
        b_f = lax.ppermute(b_f, "tp", fwd)
        b_b = lax.ppermute(b_b, "tp", bwd)
        fresh += [((a_f, b_f), owner(-step)), ((a_b, b_b), owner(step))]
        acc = stage(
            [x for x, _ in fresh],
            jnp.stack([o for _, o in fresh]),
            gate_weight, up_weight, acc, False, 256,
        )
        fresh = []
    a_f = lax.ppermute(a_f, "tp", fwd)
    b_b = lax.ppermute(b_b, "tp", bwd)
    hidden = stage([(a_f, b_b)], owner(far).reshape(1), gate_weight, up_weight, acc, True, 256)

    def term(rows, step):
        cols = lax.dynamic_slice_in_dim(down_weight, owner(step) * width, width, axis=1)
        return jnp.dot(rows, cols, preferred_element_type=F32)

    h_a, h_b = hidden[:half], hidden[half:]
    a_f = term(h_a, far).astype(BF16)
    b_b = term(h_b, far).astype(BF16)
    a_b = b_f = None
    for step in range(far - 1, 0, -1):
        a_f = lax.ppermute(a_f, "tp", fwd)
        b_b = lax.ppermute(b_b, "tp", bwd)
        if a_b is not None:
            a_b = lax.ppermute(a_b, "tp", bwd)
            b_f = lax.ppermute(b_f, "tp", fwd)
        a_f = (term(h_a, step) + a_f.astype(F32)).astype(BF16)
        b_b = (term(h_b, -step) + b_b.astype(F32)).astype(BF16)
        t_ab, t_bf = term(h_a, -step), term(h_b, step)
        a_b = (t_ab if a_b is None else t_ab + a_b.astype(F32)).astype(BF16)
        b_f = (t_bf if b_f is None else t_bf + b_f.astype(F32)).astype(BF16)
    a_f = lax.ppermute(a_f, "tp", fwd)
    b_b = lax.ppermute(b_b, "tp", bwd)
    a_b = lax.ppermute(a_b, "tp", bwd)
    b_f = lax.ppermute(b_f, "tp", fwd)
    out_a = term(h_a, 0) + a_f.astype(F32) + a_b.astype(F32)
    out_b = term(h_b, 0) + b_f.astype(F32) + b_b.astype(F32)
    return jnp.concatenate([out_a.astype(BF16), out_b.astype(BF16)], axis=0)


def solution(mesh):
    return jax.shard_map(
        body,
        mesh=mesh,
        in_specs=(
            P(("groups", "seq"), "tp"),
            P(("groups", "seq")),
            P("groups"),
            P(None, "tp"),
            P(None, "tp"),
            P("tp", None),
        ),
        out_specs=P(("groups", "seq"), "tp"),
        check_vma=False,
    )
```

time: 308 us -> 148 us (0.48)
  waiting for transfers between devices: 228 us -> 17.3 us
  Pallas kernels: 0 us -> 59.3 us
  matrix products: 55.1 us -> 16.6 us
  starting transfers between devices: 0.26 us -> 32.7 us
  other arithmetic: 1.51 us -> 5.31 us
  between operations: 13.8 us -> 10.5 us
    reduce_scatter x1 -> x0, waiting for transfers between devices: 116 us -> none  [feed_forward(): lax.psum_scatter(partial_value.astype(jnp.bfloat16), 'tp', scatter_dimens...]
    all_gather x2 -> x0, waiting for transfers between devices: 111 us -> none  [the longest x1 105 us: feed_forward(): part_cols = lax.all_gather(row_data, 'tp', axis=1, tiled=True)]
    pallas_call x0 -> x5, Pallas kernels: none -> 59.3 us  [the longest x4 41.5 us: stage(): pl.pallas_call(functools.partial(stage_kernel, pieces, acc is not None, l...]
    dot_general x2 -> x16, matrix products: 55.1 us -> 16.6 us  [term(): return jnp.dot(rows, cols, preferred_element_type=F32)]
    ppermute x0 -> x30, starting transfers between devices: none -> 32.7 us  [the longest x8 12.3 us: body(): b_b = lax.ppermute(b_b, 'tp', bwd)]
    ppermute x0 -> x30, waiting for transfers between devices: none -> 17.3 us  [the longest x8 8.58 us: body(): b_b = lax.ppermute(b_b, 'tp', bwd)]
    unnamed x11 -> x12, local copies, waits for them, and re-layouts: 6 us -> 0.92 us
    another operation x1 -> x3, other arithmetic: 0.18 us -> 4.48 us  [body(): jnp.stack([o for _, o in fresh])]
  transfers between devices with their start and end apart: 3 -> 30, of which waited for: 3 -> 10; matrix products, arithmetic and copies ran while one was open for 0% -> 13% of each run, Pallas kernels for 0% -> 22%
where the time goes in v1:
time: 148 us; the launch traced here: 147 us
  Pallas kernels  59.3 us (40%)
  starting transfers between devices  32.7 us (22%)
  waiting for transfers between devices  17.3 us (12%)
  matrix products  16.6 us (11%)
  between operations  10.5 us (7%)
  other arithmetic  5.31 us (4%)
  local copies, waits for them, and re-layouts  4.88 us (3%)
    pallas_call x4, Pallas kernels, stage(): pl.pallas_call(functools.partial(stage_kernel, pieces, acc is not None, l...  41.5 us
    pallas_call x1, Pallas kernels, pack(): pl.pallas_call(pack_kernel, out_shape=jax.ShapeDtypeStruct((own * BLOCK,...  17.7 us
    dot_general x16, matrix products, term(): return jnp.dot(rows, cols, preferred_element_type=F32)  16.6 us
    ppermute x8, starting transfers between devices, body(): b_b = lax.ppermute(b_b, 'tp', bwd)  12.3 us
    ppermute x6, starting transfers between devices, body(): a_b = lax.ppermute(a_b, 'tp', bwd)  11.4 us
    ppermute x8, waiting for transfers between devices, body(): b_b = lax.ppermute(b_b, 'tp', bwd)  8.58 us
    ppermute x6, starting transfers between devices, body(): b_f = lax.ppermute(b_f, 'tp', fwd)  5.44 us
    another operation x3, other arithmetic, body(): jnp.stack([o for _, o in fresh])  4.48 us
  transfers between devices with their start and end apart: 30, of which 10 were waited for; matrix products, arithmetic and copies ran while one was open for 13% of the time, Pallas kernels for 22%

profile of v1, /device:TPU:0, one launch (start us, length us, event | category | flops | bytes accessed | tf_op | source)
XLA Modules:
  0.0 146.5 jit_solution(7012699257924825525)
XLA Ops:
  9.6 17.7 %shard_map.82 = bf16[512,512]{1,0:T(8,128)(2,1)} custom-call(s32[2]{0:T(128)} %mine_c.1, s32[2]{0:T(128)} %copy-done.1, s32[8]{0:T(128)} %order.1, s32[1]{0:T(128)} %bitcast.1.seq_at, bf16[768,512]{1,0:T(8,128)(2,1)} %mine.1, bf16[768,512]{1,0:T(8,128)(2,1)} %copy-done), custom_call_target="tpu_custom_call" | custom-call | tf_op jit(solution)/shard_map/pallas_call | solution.py:79
  28.4 3.0 %collective-permute-start.13 = (bf16[256,512]{1,0:T(8,128)(2,1)S(1)}, bf16[256,512]{1,0:T(8,128)(2,1)S(1)}, u32[]{:S(2)}, u32[]{:S(2)}) collective-permute-start(bf16[256,512]{1,0:T(8,128)(2,1)S(1)} %get-tuple-element.18.refs_1_), channel_id=1, source_target_pairs={{0,1},{2,0},{4,2},{6,4},{7,6},{5,7},{3,5},{1,3},{8,9},{10,8},{12,1... | collective-permute-start | bytes 786440 | tf_op jit(solution)/shard_map/ppermute | solution.py:181
  31.5 2.0 %collective-permute-start.10 = (bf16[256,512]{1,0:T(8,128)(2,1)S(1)}, bf16[256,512]{1,0:T(8,128)(2,1)S(1)}, u32[]{:S(2)}, u32[]{:S(2)}) collective-permute-start(bf16[256,512]{1,0:T(8,128)(2,1)S(1)} %get-tuple-element.17.refs_2_), channel_id=1, source_target_pairs={{0,2},{2,4},{4,6},{6,7},{7,5},{5,3},{3,1},{1,0},{8,10},{10,12},{12... | collective-permute-start | bytes 786440 | tf_op jit(solution)/shard_map/ppermute | solution.py:182
  33.6 2.0 %pad_add_fusion.2.refs_0_ = s32[3]{0:T(128)S(1)} fusion(s32[1]{0:T(128)} %get-tuple-element.19, s32[1]{0:T(128)} %get-tuple-element.26, s32[1]{0:T(128)} %get-tuple-element.20), kind=kLoop, calls=%fused_computation.97 | loop fusion | flops 6 | bytes 24 | tf_op jit(solution)/shard_map/stack | solution.py:187
  43.0 1.9 %collective-permute-done.10.refs_4_ = bf16[256,512]{1,0:T(8,128)(2,1)S(1)} collective-permute-done((bf16[256,512]{1,0:T(8,128)(2,1)S(1)}, bf16[256,512]{1,0:T(8,128)(2,1)S(1)}, u32[]{:S(2)}, u32[]{:S(2)}) %collective-permute-start.10) | collective-permute-done | bytes 262176 | tf_op jit(solution)/shard_map/ppermute | solution.py:182
  49.0 11.6 %shard_map.83 = (f32[512,1792]{1,0:T(8,128)S(1)}, f32[512,1792]{1,0:T(8,128)}) custom-call(s32[3]{0:T(128)S(1)} %pad_add_fusion.2.refs_0_, bf16[256,512]{1,0:T(8,128)(2,1)S(1)} %get-tuple-element.18.refs_1_, bf16[256,512]{1,0:T(8,128)(2,1)S(1)} %get-tuple-element.17.refs_2_, bf16[256,512]{1,0:T(8,128)(2,1)S(1)} %collective-permute-done.2.refs_3_, ...), custom_call_target="tpu_custom_call" | custom-call | flops 5637144576 | bytes 25690112 | tf_op jit(solution)/shard_map/pallas_call | solution.py:140
  64.7 10.6 %shard_map.84 = (f32[512,1792]{1,0:T(8,128)S(1)}, f32[512,1792]{1,0:T(8,128)}) custom-call(s32[2]{0:T(128)S(1)} %pad_add_fusion.1.refs_0_, bf16[256,512]{1,0:T(8,128)(2,1)S(1)} %collective-permute-done.3.refs_1_, bf16[256,512]{1,0:T(8,128)(2,1)S(1)} %collective-permute-done.11.refs_2_, ...), custom_call_target="tpu_custom_call", output_to_operand_aliasing={{0}: (9, {}), {1}: (10, {})} | custom-call | flops 3758096384 | bytes 22020096 | tf_op jit(solution)/shard_map/pallas_call | solution.py:140
  77.3 10.6 %shard_map.85 = (f32[512,1792]{1,0:T(8,128)S(1)}, f32[512,1792]{1,0:T(8,128)}) custom-call(s32[2]{0:T(128)S(1)} %pad_add_fusion.refs_0_, bf16[256,512]{1,0:T(8,128)(2,1)S(1)} %collective-permute-done.4.refs_1_, bf16[256,512]{1,0:T(8,128)(2,1)S(1)} %collective-permute-done.12.refs_2_, ...), custom_call_target="tpu_custom_call", output_to_operand_aliasing={{0}: (9, {}), {1}: (10, {})} | custom-call | flops 3758096384 | bytes 22020096 | tf_op jit(solution)/shard_map/pallas_call | solution.py:140
  88.0 8.8 %shard_map.86 = bf16[512,1792]{1,0:T(8,128)(2,1)S(1)} custom-call(s32[1]{0:T(128)} %get-tuple-element.25.refs_0_, bf16[256,512]{1,0:T(8,128)(2,1)S(1)} %collective-permute-done.5.refs_1_, bf16[256,512]{1,0:T(8,128)(2,1)S(1)} %collective-permute-done.9.refs_2_, bf16[4096,1792]{1,0:T(8,128)(2,1)} %refs_3_.1, bf16[4096,1792]{1,0:T(8,128)(2,1)} %refs_4_.1, ...), custom_call_target="tpu_custom_call" | custom-call | flops 1879048192 | bytes 18350080 | tf_op jit(solution)/shard_map/pallas_call | solution.py:140
  96.8 2.3 %fusion.113 = bf16[256,512]{1,0:T(8,128)(2,1)S(1)} fusion(bf16[1792,4096]{1,0:T(8,128)(2,1)} %param.13, s32[]{:T(128)S(6)} %select_n.88, bf16[512,1792]{1,0:T(8,128)(2,1)S(1)} %shard_map.86), kind=kOutput, calls=%fused_computation.59 | convolution fusion | flops 469893120 | bytes 3014660 | tf_op jit(solution)/shard_map/dot_general | solution.py:197
  99.1 2.1 %fusion.116 = bf16[256,512]{1,0:T(8,128)(2,1)S(1)} fusion(bf16[1792,4096]{1,0:T(8,128)(2,1)} %param.13, s32[]{:T(128)S(6)} %select_n.88, bf16[512,1792]{1,0:T(8,128)(2,1)S(1)} %shard_map.86), kind=kOutput, calls=%fused_computation.60 | convolution fusion | flops 469893120 | bytes 3014660 | tf_op jit(solution)/shard_map/dot_general | solution.py:197
  101.7 2.1 %fusion.119 = bf16[256,512]{1,0:T(8,128)(2,1)S(1)} fusion(bf16[1792,4096]{1,0:T(8,128)(2,1)} %param.13, s32[]{:T(128)S(6)} %select_n.91, bf16[512,1792]{1,0:T(8,128)(2,1)S(1)} %shard_map.86), kind=kOutput, calls=%fused_computation.61 | convolution fusion | flops 469893120 | bytes 3014660 | tf_op jit(solution)/shard_map/dot_general | solution.py:197
  103.8 1.7 %collective-permute-start.20 = (bf16[256,512]{1,0:T(8,128)(2,1)S(1)}, bf16[256,512]{1,0:T(8,128)(2,1)S(1)}, u32[]{:S(2)}, u32[]{:S(2)}) collective-permute-start(bf16[256,512]{1,0:T(8,128)(2,1)S(1)} %fusion.119), channel_id=1, source_target_pairs={{0,1},{2,0},{4,2},{6,4},{7,6},{5,7},{3,5},{1,3},{8,9},{10,8},{12,1... | collective-permute-start | bytes 786440 | tf_op jit(solution)/shard_map/ppermute | solution.py:207
  105.5 2.1 %fusion.110 = bf16[256,512]{1,0:T(8,128)(2,1)S(1)} fusion(bf16[1792,4096]{1,0:T(8,128)(2,1)} %param.13, s32[]{:T(128)S(6)} %select_n.87, bf16[512,1792]{1,0:T(8,128)(2,1)S(1)} %shard_map.86), kind=kOutput, calls=%fused_computation.58 | convolution fusion | flops 469893120 | bytes 3014660 | tf_op jit(solution)/shard_map/dot_general | solution.py:197
  110.9 2.2 %collective-permute-done.20 = bf16[256,512]{1,0:T(8,128)(2,1)S(1)} collective-permute-done((bf16[256,512]{1,0:T(8,128)(2,1)S(1)}, bf16[256,512]{1,0:T(8,128)(2,1)S(1)}, u32[]{:S(2)}, u32[]{:S(2)}) %collective-permute-start.20) | collective-permute-done | bytes 262176 | tf_op jit(solution)/shard_map/ppermute | solution.py:207
  113.8 1.7 %collective-permute-start.21 = (bf16[256,512]{1,0:T(8,128)(2,1)S(1)}, bf16[256,512]{1,0:T(8,128)(2,1)S(1)}, u32[]{:S(2)}, u32[]{:S(2)}) collective-permute-start(bf16[256,512]{1,0:T(8,128)(2,1)S(1)} %fusion.86), channel_id=1, source_target_pairs={{0,1},{2,0},{4,2},{6,4},{7,6},{5,7},{3,5},{1,3},{8,9},{10,8},{12,1... | collective-permute-start | bytes 786440 | tf_op jit(solution)/shard_map/ppermute | solution.py:207
  119.4 1.7 %collective-permute-start.27 = (bf16[256,512]{1,0:T(8,128)(2,1)S(1)}, bf16[256,512]{1,0:T(8,128)(2,1)S(1)}, u32[]{:S(2)}, u32[]{:S(2)}) collective-permute-start(bf16[256,512]{1,0:T(8,128)(2,1)S(1)} %fusion.80), channel_id=1, source_target_pairs={{0,1},{2,0},{4,2},{6,4},{7,6},{5,7},{3,5},{1,3},{8,9},{10,8},{12,1... | collective-permute-start | bytes 786440 | tf_op jit(solution)/shard_map/ppermute | solution.py:205
  125.0 1.7 %collective-permute-start.22 = (bf16[256,512]{1,0:T(8,128)(2,1)S(1)}, bf16[256,512]{1,0:T(8,128)(2,1)S(1)}, u32[]{:S(2)}, u32[]{:S(2)}) collective-permute-start(bf16[256,512]{1,0:T(8,128)(2,1)S(1)} %fusion.92), channel_id=1, source_target_pairs={{0,1},{2,0},{4,2},{6,4},{7,6},{5,7},{3,5},{1,3},{8,9},{10,8},{12,1... | collective-permute-start | bytes 786440 | tf_op jit(solution)/shard_map/ppermute | solution.py:216
  126.7 3.2 %collective-permute-done.27 = bf16[256,512]{1,0:T(8,128)(2,1)S(1)} collective-permute-done((bf16[256,512]{1,0:T(8,128)(2,1)S(1)}, bf16[256,512]{1,0:T(8,128)(2,1)S(1)}, u32[]{:S(2)}, u32[]{:S(2)}) %collective-permute-start.27) | collective-permute-done | bytes 262176 | tf_op jit(solution)/shard_map/ppermute | solution.py:205
  130.6 1.7 %collective-permute-start.28 = (bf16[256,512]{1,0:T(8,128)(2,1)S(1)}, bf16[256,512]{1,0:T(8,128)(2,1)S(1)}, u32[]{:S(2)}, u32[]{:S(2)}) collective-permute-start(bf16[256,512]{1,0:T(8,128)(2,1)S(1)} %fusion.83), channel_id=1, source_target_pairs={{0,1},{2,0},{4,2},{6,4},{7,6},{5,7},{3,5},{1,3},{8,9},{10,8},{12,1... | collective-permute-start | bytes 786440 | tf_op jit(solution)/shard_map/ppermute | solution.py:205
  134.1 1.8 %collective-permute-start.25 = (bf16[256,512]{1,0:T(8,128)(2,1)S(1)}, bf16[256,512]{1,0:T(8,128)(2,1)S(1)}, u32[]{:S(2)}, u32[]{:S(2)}) collective-permute-start(bf16[256,512]{1,0:T(8,128)(2,1)S(1)} %fusion.104), channel_id=1, source_target_pairs={{0,2},{2,4},{4,6},{6,7},{7,5},{5,3},{3,1},{1,0},{8,10},{10,12},{12... | collective-permute-start | bytes 786440 | tf_op jit(solution)/shard_map/ppermute | solution.py:217
  135.8 1.9 %collective-permute-done.28 = bf16[256,512]{1,0:T(8,128)(2,1)S(1)} collective-permute-done((bf16[256,512]{1,0:T(8,128)(2,1)S(1)}, bf16[256,512]{1,0:T(8,128)(2,1)S(1)}, u32[]{:S(2)}, u32[]{:S(2)}) %collective-permute-start.28) | collective-permute-done | bytes 262176 | tf_op jit(solution)/shard_map/ppermute | solution.py:205
  138.4 2.3 %collective-permute-start.29 = (bf16[256,512]{1,0:T(8,128)(2,1)S(1)}, bf16[256,512]{1,0:T(8,128)(2,1)S(1)}, u32[]{:S(2)}, u32[]{:S(2)}) collective-permute-start(bf16[256,512]{1,0:T(8,128)(2,1)S(1)} %fusion.89), channel_id=1, source_target_pairs={{0,1},{2,0},{4,2},{6,4},{7,6},{5,7},{3,5},{1,3},{8,9},{10,8},{12,1... | collective-permute-start | bytes 786440 | tf_op jit(solution)/shard_map/ppermute | solution.py:215
  142.2 2.8 %collective-permute-done.29 = bf16[256,512]{1,0:T(8,128)(2,1)S(1)} collective-permute-done((bf16[256,512]{1,0:T(8,128)(2,1)S(1)}, bf16[256,512]{1,0:T(8,128)(2,1)S(1)}, u32[]{:S(2)}, u32[]{:S(2)}) %collective-permute-start.29) | collective-permute-done | bytes 262176 | tf_op jit(solution)/shard_map/ppermute | solution.py:215
  (77 shorter events, 36.5 us)
Async XLA Ops:
  0.0 8.7 %collective-permute-start.1 = (bf16[768,512]{1,0:T(8,128)(2,1)}, bf16[768,512]{1,0:T(8,128)(2,1)S(1)}, u32[]{:S(2)}, u32[]{:S(2)}) collective-permute-start(bf16[768,512]{1,0:T(8,128)(2,1)} %mine.1), channel_id=1, source_target_pairs={{0,8},{8,0},{1,9},{9,1},{2,10},{10,2},{3,11},{11,3},{4,12},{12,4},... | collective-permute-start | bytes 2359304 | tf_op jit(solution)/shard_map/ppermute | solution.py:73
  28.4 17.0 %collective-permute-start.13 = (bf16[256,512]{1,0:T(8,128)(2,1)S(1)}, bf16[256,512]{1,0:T(8,128)(2,1)S(1)}, u32[]{:S(2)}, u32[]{:S(2)}) collective-permute-start(bf16[256,512]{1,0:T(8,128)(2,1)S(1)} %get-tuple-element.18.refs_1_), channel_id=1, source_target_pairs={{0,1},{2,0},{4,2},{6,4},{7,6},{5,7},{3,5},{1,3},{8,9},{10,8},{12,1... | collective-permute-start | bytes 786440 | tf_op jit(solution)/shard_map/ppermute | solution.py:181
  31.4 15.6 %collective-permute-start.2 = (bf16[256,512]{1,0:T(8,128)(2,1)S(1)}, bf16[256,512]{1,0:T(8,128)(2,1)S(1)}, u32[]{:S(2)}, u32[]{:S(2)}) collective-permute-start(bf16[256,512]{1,0:T(8,128)(2,1)S(1)} %get-tuple-element.18.refs_1_), channel_id=1, source_target_pairs={{0,2},{2,4},{4,6},{6,7},{7,5},{5,3},{3,1},{1,0},{8,10},{10,12},{12... | collective-permute-start | bytes 786440 | tf_op jit(solution)/shard_map/ppermute | solution.py:180
  31.5 13.4 %collective-permute-start.10 = (bf16[256,512]{1,0:T(8,128)(2,1)S(1)}, bf16[256,512]{1,0:T(8,128)(2,1)S(1)}, u32[]{:S(2)}, u32[]{:S(2)}) collective-permute-start(bf16[256,512]{1,0:T(8,128)(2,1)S(1)} %get-tuple-element.17.refs_2_), channel_id=1, source_target_pairs={{0,2},{2,4},{4,6},{6,7},{7,5},{5,3},{3,1},{1,0},{8,10},{10,12},{12... | collective-permute-start | bytes 786440 | tf_op jit(solution)/shard_map/ppermute | solution.py:182
  33.5 13.9 %collective-permute-start.6 = (bf16[256,512]{1,0:T(8,128)(2,1)S(1)}, bf16[256,512]{1,0:T(8,128)(2,1)S(1)}, u32[]{:S(2)}, u32[]{:S(2)}) collective-permute-start(bf16[256,512]{1,0:T(8,128)(2,1)S(1)} %get-tuple-element.17.refs_2_), channel_id=1, source_target_pairs={{0,1},{2,0},{4,2},{6,4},{7,6},{5,7},{3,5},{1,3},{8,9},{10,8},{12,1... | collective-permute-start | bytes 786440 | tf_op jit(solution)/shard_map/ppermute | solution.py:183
  45.0 17.7 %collective-permute-start.11 = (bf16[256,512]{1,0:T(8,128)(2,1)S(1)}, bf16[256,512]{1,0:T(8,128)(2,1)S(1)}, u32[]{:S(2)}, u32[]{:S(2)}) collective-permute-start(bf16[256,512]{1,0:T(8,128)(2,1)S(1)} %collective-permute-done.10.refs_4_), channel_id=1, source_target_pairs={{0,2},{2,4},{4,6},{6,7},{7,5},{5,3},{3,1},{1,0},{8,10},{10,12},{12... | collective-permute-start | bytes 786440 | tf_op jit(solution)/shard_map/ppermute | solution.py:182
  45.4 17.7 %collective-permute-start.14 = (bf16[256,512]{1,0:T(8,128)(2,1)S(1)}, bf16[256,512]{1,0:T(8,128)(2,1)S(1)}, u32[]{:S(2)}, u32[]{:S(2)}) collective-permute-start(bf16[256,512]{1,0:T(8,128)(2,1)S(1)} %collective-permute-done.13.refs_5_), channel_id=1, source_target_pairs={{0,1},{2,0},{4,2},{6,4},{7,6},{5,7},{3,5},{1,3},{8,9},{10,8},{12,1... | collective-permute-start | bytes 786440 | tf_op jit(solution)/shard_map/ppermute | solution.py:181
  47.0 13.6 %collective-permute-start.3 = (bf16[256,512]{1,0:T(8,128)(2,1)S(1)}, bf16[256,512]{1,0:T(8,128)(2,1)S(1)}, u32[]{:S(2)}, u32[]{:S(2)}) collective-permute-start(bf16[256,512]{1,0:T(8,128)(2,1)S(1)} %collective-permute-done.2.refs_3_), channel_id=1, source_target_pairs={{0,2},{2,4},{4,6},{6,7},{7,5},{5,3},{3,1},{1,0},{8,10},{10,12},{12... | collective-permute-start | bytes 786440 | tf_op jit(solution)/shard_map/ppermute | solution.py:180
  47.4 13.6 %collective-permute-start.7 = (bf16[256,512]{1,0:T(8,128)(2,1)S(1)}, bf16[256,512]{1,0:T(8,128)(2,1)S(1)}, u32[]{:S(2)}, u32[]{:S(2)}) collective-permute-start(bf16[256,512]{1,0:T(8,128)(2,1)S(1)} %collective-permute-done.6.refs_6_), channel_id=1, source_target_pairs={{0,1},{2,0},{4,2},{6,4},{7,6},{5,7},{3,5},{1,3},{8,9},{10,8},{12,1... | collective-permute-start | bytes 786440 | tf_op jit(solution)/shard_map/ppermute | solution.py:183
  60.6 14.7 %collective-permute-start.4 = (bf16[256,512]{1,0:T(8,128)(2,1)S(1)}, bf16[256,512]{1,0:T(8,128)(2,1)S(1)}, u32[]{:S(2)}, u32[]{:S(2)}) collective-permute-start(bf16[256,512]{1,0:T(8,128)(2,1)S(1)} %collective-permute-done.3.refs_1_), channel_id=1, source_target_pairs={{0,2},{2,4},{4,6},{6,7},{7,5},{5,3},{3,1},{1,0},{8,10},{10,12},{12... | collective-permute-start | bytes 786440 | tf_op jit(solution)/shard_map/ppermute | solution.py:180
  61.0 14.7 %collective-permute-start.8 = (bf16[256,512]{1,0:T(8,128)(2,1)S(1)}, bf16[256,512]{1,0:T(8,128)(2,1)S(1)}, u32[]{:S(2)}, u32[]{:S(2)}) collective-permute-start(bf16[256,512]{1,0:T(8,128)(2,1)S(1)} %collective-permute-done.7.refs_4_), channel_id=1, source_target_pairs={{0,1},{2,0},{4,2},{6,4},{7,6},{5,7},{3,5},{1,3},{8,9},{10,8},{12,1... | collective-permute-start | bytes 786440 | tf_op jit(solution)/shard_map/ppermute | solution.py:183
  62.7 14.7 %collective-permute-start.12 = (bf16[256,512]{1,0:T(8,128)(2,1)S(1)}, bf16[256,512]{1,0:T(8,128)(2,1)S(1)}, u32[]{:S(2)}, u32[]{:S(2)}) collective-permute-start(bf16[256,512]{1,0:T(8,128)(2,1)S(1)} %collective-permute-done.11.refs_2_), channel_id=1, source_target_pairs={{0,2},{2,4},{4,6},{6,7},{7,5},{5,3},{3,1},{1,0},{8,10},{10,12},{12... | collective-permute-start | bytes 786440 | tf_op jit(solution)/shard_map/ppermute | solution.py:182
  63.1 14.2 %collective-permute-start.15 = (bf16[256,512]{1,0:T(8,128)(2,1)S(1)}, bf16[256,512]{1,0:T(8,128)(2,1)S(1)}, u32[]{:S(2)}, u32[]{:S(2)}) collective-permute-start(bf16[256,512]{1,0:T(8,128)(2,1)S(1)} %collective-permute-done.14.refs_3_), channel_id=1, source_target_pairs={{0,1},{2,0},{4,2},{6,4},{7,6},{5,7},{3,5},{1,3},{8,9},{10,8},{12,1... | collective-permute-start | bytes 786440 | tf_op jit(solution)/shard_map/ppermute | solution.py:181
  75.3 12.6 %collective-permute-start.5 = (bf16[256,512]{1,0:T(8,128)(2,1)S(1)}, bf16[256,512]{1,0:T(8,128)(2,1)S(1)}, u32[]{:S(2)}, u32[]{:S(2)}) collective-permute-start(bf16[256,512]{1,0:T(8,128)(2,1)S(1)} %collective-permute-done.4.refs_1_), channel_id=1, source_target_pairs={{0,2},{2,4},{4,6},{6,7},{7,5},{5,3},{3,1},{1,0},{8,10},{10,12},{12... | collective-permute-start | bytes 786440 | tf_op jit(solution)/shard_map/ppermute | solution.py:191
  75.7 12.2 %collective-permute-start.9 = (bf16[256,512]{1,0:T(8,128)(2,1)S(1)}, bf16[256,512]{1,0:T(8,128)(2,1)S(1)}, u32[]{:S(2)}, u32[]{:S(2)}) collective-permute-start(bf16[256,512]{1,0:T(8,128)(2,1)S(1)} %collective-permute-done.8.refs_4_), channel_id=1, source_target_pairs={{0,1},{2,0},{4,2},{6,4},{7,6},{5,7},{3,5},{1,3},{8,9},{10,8},{12,1... | collective-permute-start | bytes 786440 | tf_op jit(solution)/shard_map/ppermute | solution.py:192
  103.8 9.3 %collective-permute-start.20 = (bf16[256,512]{1,0:T(8,128)(2,1)S(1)}, bf16[256,512]{1,0:T(8,128)(2,1)S(1)}, u32[]{:S(2)}, u32[]{:S(2)}) collective-permute-start(bf16[256,512]{1,0:T(8,128)(2,1)S(1)} %fusion.119), channel_id=1, source_target_pairs={{0,1},{2,0},{4,2},{6,4},{7,6},{5,7},{3,5},{1,3},{8,9},{10,8},{12,1... | collective-permute-start | bytes 786440 | tf_op jit(solution)/shard_map/ppermute | solution.py:207
  107.6 9.3 %collective-permute-start.23 = (bf16[256,512]{1,0:T(8,128)(2,1)S(1)}, bf16[256,512]{1,0:T(8,128)(2,1)S(1)}, u32[]{:S(2)}, u32[]{:S(2)}) collective-permute-start(bf16[256,512]{1,0:T(8,128)(2,1)S(1)} %fusion.110), channel_id=1, source_target_pairs={{0,2},{2,4},{4,6},{6,7},{7,5},{5,3},{3,1},{1,0},{8,10},{10,12},{12... | collective-permute-start | bytes 786440 | tf_op jit(solution)/shard_map/ppermute | solution.py:208
  108.1 10.6 %collective-permute-start.26 = (bf16[256,512]{1,0:T(8,128)(2,1)S(1)}, bf16[256,512]{1,0:T(8,128)(2,1)S(1)}, u32[]{:S(2)}, u32[]{:S(2)}) collective-permute-start(bf16[256,512]{1,0:T(8,128)(2,1)S(1)} %fusion.116), channel_id=1, source_target_pairs={{0,1},{2,0},{4,2},{6,4},{7,6},{5,7},{3,5},{1,3},{8,9},{10,8},{12,1... | collective-permute-start | bytes 786440 | tf_op jit(solution)/shard_map/ppermute | solution.py:205
  110.4 12.1 %collective-permute-start.17 = (bf16[256,512]{1,0:T(8,128)(2,1)S(1)}, bf16[256,512]{1,0:T(8,128)(2,1)S(1)}, u32[]{:S(2)}, u32[]{:S(2)}) collective-permute-start(bf16[256,512]{1,0:T(8,128)(2,1)S(1)} %fusion.95), channel_id=1, source_target_pairs={{0,2},{2,4},{4,6},{6,7},{7,5},{5,3},{3,1},{1,0},{8,10},{10,12},{12... | collective-permute-start | bytes 786440 | tf_op jit(solution)/shard_map/ppermute | solution.py:204
  113.8 10.6 %collective-permute-start.21 = (bf16[256,512]{1,0:T(8,128)(2,1)S(1)}, bf16[256,512]{1,0:T(8,128)(2,1)S(1)}, u32[]{:S(2)}, u32[]{:S(2)}) collective-permute-start(bf16[256,512]{1,0:T(8,128)(2,1)S(1)} %fusion.86), channel_id=1, source_target_pairs={{0,1},{2,0},{4,2},{6,4},{7,6},{5,7},{3,5},{1,3},{8,9},{10,8},{12,1... | collective-permute-start | bytes 786440 | tf_op jit(solution)/shard_map/ppermute | solution.py:207
  117.6 15.8 %collective-permute-start.24 = (bf16[256,512]{1,0:T(8,128)(2,1)S(1)}, bf16[256,512]{1,0:T(8,128)(2,1)S(1)}, u32[]{:S(2)}, u32[]{:S(2)}) collective-permute-start(bf16[256,512]{1,0:T(8,128)(2,1)S(1)} %fusion.98), channel_id=1, source_target_pairs={{0,2},{2,4},{4,6},{6,7},{7,5},{5,3},{3,1},{1,0},{8,10},{10,12},{12... | collective-permute-start | bytes 786440 | tf_op jit(solution)/shard_map/ppermute | solution.py:208
  119.4 10.6 %collective-permute-start.27 = (bf16[256,512]{1,0:T(8,128)(2,1)S(1)}, bf16[256,512]{1,0:T(8,128)(2,1)S(1)}, u32[]{:S(2)}, u32[]{:S(2)}) collective-permute-start(bf16[256,512]{1,0:T(8,128)(2,1)S(1)} %fusion.80), channel_id=1, source_target_pairs={{0,1},{2,0},{4,2},{6,4},{7,6},{5,7},{3,5},{1,3},{8,9},{10,8},{12,1... | collective-permute-start | bytes 786440 | tf_op jit(solution)/shard_map/ppermute | solution.py:205
  123.2 9.1 %collective-permute-start.18 = (bf16[256,512]{1,0:T(8,128)(2,1)S(1)}, bf16[256,512]{1,0:T(8,128)(2,1)S(1)}, u32[]{:S(2)}, u32[]{:S(2)}) collective-permute-start(bf16[256,512]{1,0:T(8,128)(2,1)S(1)} %fusion.101), channel_id=1, source_target_pairs={{0,2},{2,4},{4,6},{6,7},{7,5},{5,3},{3,1},{1,0},{8,10},{10,12},{12... | collective-permute-start | bytes 786440 | tf_op jit(solution)/shard_map/ppermute | solution.py:204
  125.0 15.6 %collective-permute-start.22 = (bf16[256,512]{1,0:T(8,128)(2,1)S(1)}, bf16[256,512]{1,0:T(8,128)(2,1)S(1)}, u32[]{:S(2)}, u32[]{:S(2)}) collective-permute-start(bf16[256,512]{1,0:T(8,128)(2,1)S(1)} %fusion.92), channel_id=1, source_target_pairs={{0,1},{2,0},{4,2},{6,4},{7,6},{5,7},{3,5},{1,3},{8,9},{10,8},{12,1... | collective-permute-start | bytes 786440 | tf_op jit(solution)/shard_map/ppermute | solution.py:216
  (12 other events, 126.2 us)

commit v2 on v1

--- a/solution.py
+++ b/solution.py
@@ -11,6 +11,7 @@
 F32 = jnp.float32
 BF16 = jnp.bfloat16
 MIB = 1024 * 1024
+VMEM = 32 * MIB
 
 
 def ring_order(n):
@@ -19,17 +20,27 @@
     return list(range(n))
 
 
+def owner_at(step, n):
+    here = lax.axis_index("tp")
+    if n != 8:
+        return (here + (step + n)) & (n - 1) if n & (n - 1) == 0 else lax.rem(here + (step + n), n)
+    place = jnp.where((here & 1) == 0, here >> 1, n - 1 - (here >> 1))
+    there = (place + (step + n)) & (n - 1)
+    return jnp.where(there < n // 2, there * 2, 2 * n - 1 - 2 * there)
+
+
 def shift(order, step):
     n = len(order)
     return [(order[i], order[(i + step) % n]) for i in range(n)]
 
 
-def pack_kernel(mine_c, other_c, order, seq_at, mine, other, out, sems):
+def pack_kernel(mine_c, other_c, order, mine, other, first_half, second_half, sems):
     loaders = mine_c.shape[0]
     blocks = order.shape[0]
     slots = mine.shape[0] // BLOCK // loaders
-    own = out.shape[0] // BLOCK
-    me = seq_at[0]
+    half = first_half.shape[0] // BLOCK
+    own = 2 * half
+    me = lax.axis_index("seq")
 
     first = [jnp.where(me == 0, mine_c[i], other_c[i]) for i in range(loaders)]
     second = [jnp.where(me == 0, other_c[i], mine_c[i]) for i in range(loaders)]
@@ -49,22 +60,25 @@
         holder = jnp.where(row >= loaders * slots, 1, 0)
         row = row - holder * (loaders * slots)
         start = pl.multiple_of(row * BLOCK, BLOCK)
+        out = first_half if i < half else second_half
+        at = pl.ds(i % half * BLOCK, BLOCK)
 
         @pl.when(holder == me)
-        def _(start=start, i=i):
+        def _(start=start, i=i, out=out, at=at):
             pltpu.make_async_copy(
-                mine.at[pl.ds(start, BLOCK)], out.at[pl.ds(i * BLOCK, BLOCK)], sems.at[i]
+                mine.at[pl.ds(start, BLOCK)], out.at[at], sems.at[i]
             ).start()
 
         @pl.when(holder != me)
-        def _(start=start, i=i):
+        def _(start=start, i=i, out=out, at=at):
             pltpu.make_async_copy(
-                other.at[pl.ds(start, BLOCK)], out.at[pl.ds(i * BLOCK, BLOCK)], sems.at[i]
+                other.at[pl.ds(start, BLOCK)], out.at[at], sems.at[i]
             ).start()
 
     for i in range(own):
+        out = first_half if i < half else second_half
         pltpu.make_async_copy(
-            mine.at[pl.ds(0, BLOCK)], out.at[pl.ds(i * BLOCK, BLOCK)], sems.at[i]
+            mine.at[pl.ds(0, BLOCK)], out.at[pl.ds(i % half * BLOCK, BLOCK)], sems.at[i]
         ).wait()
 
 
@@ -74,23 +88,25 @@
     other_counts = lax.ppermute(block_counts, "seq", swap)
     own = seq_order.shape[0] // 2
     width = loaded.shape[1]
-    seq_at = lax.axis_index("seq").astype(jnp.int32).reshape(1)
+    rows = own // 2 * BLOCK
     any_spec = pl.BlockSpec(memory_space=pl.ANY)
+    whole = pl.BlockSpec((rows, width), lambda i, *_: (0, 0))
     return pl.pallas_call(
         pack_kernel,
-        out_shape=jax.ShapeDtypeStruct((own * BLOCK, width), loaded.dtype),
+        out_shape=[jax.ShapeDtypeStruct((rows, width), loaded.dtype)] * 2,
         grid_spec=pltpu.PrefetchScalarGridSpec(
-            num_scalar_prefetch=4,
+            num_scalar_prefetch=3,
             grid=(1,),
             in_specs=[any_spec, any_spec],
-            out_specs=any_spec,
+            out_specs=[whole, whole],
             scratch_shapes=[pltpu.SemaphoreType.DMA((own,))],
         ),
-    )(block_counts, other_counts, seq_order, seq_at, loaded, other)
+        compiler_params=pltpu.CompilerParams(vmem_limit_bytes=8 * MIB),
+    )(block_counts, other_counts, seq_order, loaded, other)
 
 
 def stage_kernel(pieces, has_acc, last, *refs):
-    refs = list(refs[1:])
+    refs = list(refs)
     xs = [(refs.pop(0), refs.pop(0)) for _ in range(pieces)]
     gws = [refs.pop(0) for _ in range(pieces)]
     uws = [refs.pop(0) for _ in range(pieces)]
@@ -113,22 +129,23 @@
             refs[1][rows, :] = sums[1]
 
 
-def stage(xs, owners, gate_weight, up_weight, acc, last, tile):
+def stage(xs, steps, gate_weight, up_weight, acc, last, tile):
+    n = lax.axis_size("tp")
     pieces = len(xs)
     half, width = xs[0][0].shape
     hid = gate_weight.shape[1]
-    x_spec = pl.BlockSpec((half, width), lambda i, own: (0, 0))
+    x_spec = pl.BlockSpec((half, width), lambda i: (0, 0))
     w_specs = [
-        pl.BlockSpec((width, tile), functools.partial(lambda p, i, own: (own[p], i), p))
-        for p in range(pieces)
+        pl.BlockSpec((width, tile), functools.partial(lambda s, i: (owner_at(s, n), i), s))
+        for s in steps
     ]
-    full = pl.BlockSpec((2 * half, tile), lambda i, own: (0, i))
+    full = pl.BlockSpec((2 * half, tile), lambda i: (0, i))
     operands = [x for pair in xs for x in pair] + [gate_weight] * pieces + [up_weight] * pieces
     in_specs = [x_spec] * (2 * pieces) + w_specs * 2
     aliases = {}
     if acc is not None:
         if not last:
-            aliases = {1 + len(operands): 0, 2 + len(operands): 1}
+            aliases = {len(operands): 0, 1 + len(operands): 1}
         operands += list(acc)
         in_specs += [full, full]
     if last:
@@ -140,60 +157,50 @@
     return pl.pallas_call(
         functools.partial(stage_kernel, pieces, acc is not None, last),
         out_shape=out_shape,
-        grid_spec=pltpu.PrefetchScalarGridSpec(
-            num_scalar_prefetch=1,
-            grid=(hid // tile,),
-            in_specs=in_specs,
-            out_specs=out_specs,
-        ),
+        grid=(hid // tile,),
+        in_specs=in_specs,
+        out_specs=out_specs,
         input_output_aliases=aliases,
-        compiler_params=pltpu.CompilerParams(vmem_limit_bytes=48 * MIB),
+        compiler_params=pltpu.CompilerParams(vmem_limit_bytes=VMEM),
         cost_estimate=pl.CostEstimate(
             flops=2 * 2 * half * width * pieces * hid * 2,
             bytes_accessed=2 * width * pieces * hid * 2 + 2 * 2 * 2 * half * hid * 4,
             transcendentals=0,
         ),
-    )(owners, *operands)
+    )(*operands)
 
 
 def body(loaded, block_counts, seq_order, gate_weight, up_weight, down_weight):
     n = lax.axis_size("tp")
     order = ring_order(n)
-    table = jnp.array(order, jnp.int32)
-    where = jnp.array([order.index(i) for i in range(n)], jnp.int32)
-    at = where[lax.axis_index("tp")]
     fwd, bwd = shift(order, 1), shift(order, -1)
     far = n // 2
 
-    def owner(step):
-        return table[lax.rem(at + step + n, n)]
-
-    packed = pack(loaded, block_counts, seq_order)
-    half = packed.shape[0] // 2
-    width = packed.shape[1]
-
-    a_f = a_b = packed[:half]
-    b_f = b_b = packed[half:]
-    fresh = [((a_f, b_f), owner(0))]
+    own_a, own_b = pack(loaded, block_counts, seq_order)
+    half, width = own_a.shape
+
+    a_f = a_b = own_a
+    b_f = b_b = own_b
+    fresh = [((a_f, b_f), 0)]
     acc = None
     for step in range(1, far):
         a_f = lax.ppermute(a_f, "tp", fwd)
         a_b = lax.ppermute(a_b, "tp", bwd)
         b_f = lax.ppermute(b_f, "tp", fwd)
         b_b = lax.ppermute(b_b, "tp", bwd)
-        fresh += [((a_f, b_f), owner(-step)), ((a_b, b_b), owner(step))]
+        fresh += [((a_f, b_f), -step), ((a_b, b_b), step)]
         acc = stage(
             [x for x, _ in fresh],
-            jnp.stack([o for _, o in fresh]),
-            gate_weight, up_weight, acc, False, 256,
+            [o for _, o in fresh],
+            gate_weight, up_weight, acc, False, 896,
         )
         fresh = []
     a_f = lax.ppermute(a_f, "tp", fwd)
     b_b = lax.ppermute(b_b, "tp", bwd)
-    hidden = stage([(a_f, b_b)], owner(far).reshape(1), gate_weight, up_weight, acc, True, 256)
+    hidden = stage([(a_f, b_b)], [far], gate_weight, up_weight, acc, True, 896)
 
     def term(rows, step):
-        cols = lax.dynamic_slice_in_dim(down_weight, owner(step) * width, width, axis=1)
+        cols = lax.dynamic_slice_in_dim(down_weight, owner_at(step, n) * width, width, axis=1)
         return jnp.dot(rows, cols, preferred_element_type=F32)
 
     h_a, h_b = hidden[:half], hidden[half:]

time: 148 us -> 109 us (0.74)
  Pallas kernels: 59.3 us -> 30.7 us
  waiting for transfers between devices: 17.3 us -> 32.6 us
  between operations: 10.5 us -> 0.28 us
  matrix products: 16.6 us -> 10.5 us
  other arithmetic: 5.31 us -> 0.83 us
  local copies, waits for them, and re-layouts: 4.88 us -> 2.46 us
    pallas_call x1, Pallas kernels: 17.7 us -> 1.37 us  [pack(): pl.pallas_call(pack_kernel, out_shape=[jax.ShapeDtypeStruct((rows, width)...]
    pallas_call x4, Pallas kernels: 41.5 us -> 29.4 us  [stage(): pl.pallas_call(functools.partial(stage_kernel, pieces, acc is not None, l...]
    ppermute x8, starting transfers between devices: 3.15 us -> 14.8 us  [body(): a_f = lax.ppermute(a_f, 'tp', fwd)]
    ppermute x8, starting transfers between devices: 12.3 us -> 2.36 us  [body(): b_b = lax.ppermute(b_b, 'tp', bwd)]
    ppermute x6, starting transfers between devices: 11.4 us -> 1.55 us  [body(): a_b = lax.ppermute(a_b, 'tp', bwd)]
    ppermute x8, waiting for transfers between devices: 1.5 us -> 9.95 us  [body(): a_f = lax.ppermute(a_f, 'tp', fwd)]
    ppermute x6, starting transfers between devices: 5.44 us -> 12 us  [body(): b_f = lax.ppermute(b_f, 'tp', fwd)]
    dot_general x16, matrix products: 16.6 us -> 10.5 us  [term(): return jnp.dot(rows, cols, preferred_element_type=F32)]
  transfers between devices with their start and end apart: 30 -> 30, of which waited for: 10 -> 12; matrix products, arithmetic and copies ran while one was open for 13% -> 8% of each run, Pallas kernels for 22% -> 23%
where the time goes in v2:
time: 109 us
  waiting for transfers between devices  32.6 us (30%)
  starting transfers between devices  31.3 us (29%)
  Pallas kernels  30.7 us (28%)
  matrix products  10.5 us (10%)
  local copies, waits for them, and re-layouts  2.46 us (2%)
    pallas_call x4, Pallas kernels, stage(): pl.pallas_call(functools.partial(stage_kernel, pieces, acc is not None, l...  29.4 us
    ppermute x8, starting transfers between devices, body(): a_f = lax.ppermute(a_f, 'tp', fwd)  14.8 us
    ppermute x8, waiting for transfers between devices, body(): b_b = lax.ppermute(b_b, 'tp', bwd)  12.6 us
    ppermute x6, starting transfers between devices, body(): b_f = lax.ppermute(b_f, 'tp', fwd)  12 us
    dot_general x16, matrix products, term(): return jnp.dot(rows, cols, preferred_element_type=F32)  10.5 us
    ppermute x8, waiting for transfers between devices, body(): a_f = lax.ppermute(a_f, 'tp', fwd)  9.95 us
    ppermute x6, waiting for transfers between devices, body(): b_f = lax.ppermute(b_f, 'tp', fwd)  7.22 us
    unnamed x14, local copies, waits for them, and re-layouts  2.46 us
  transfers between devices with their start and end apart: 30, of which 12 were waited for; matrix products, arithmetic and copies ran while one was open for 8% of the time, Pallas kernels for 23%

profile of v2, /device:TPU:0, one launch (start us, length us, event | category | flops | bytes accessed | tf_op | source)
XLA Modules:
  0.0 108.7 jit_solution(11673906325688582436)
XLA Ops:
  0.5 2.1 %collective-permute-done.other_c = s32[2]{0:T(128)S(1)} collective-permute-done((s32[2]{0:T(128)}, s32[2]{0:T(128)S(1)}, u32[]{:S(2)}, u32[]{:S(2)}) %collective-permute-start) | collective-permute-done | bytes 40 | tf_op jit(solution)/shard_map/ppermute | solution.py:88
  6.4 3.0 %collective-permute-start.10 = (bf16[256,512]{1,0:T(8,128)(2,1)S(1)}, bf16[256,512]{1,0:T(8,128)(2,1)S(1)}, u32[]{:S(2)}, u32[]{:S(2)}) collective-permute-start(bf16[256,512]{1,0:T(8,128)(2,1)S(1)} %get-tuple-element.14.refs_1_), channel_id=1, source_target_pairs={{0,2},{2,4},{4,6},{6,7},{7,5},{5,3},{3,1},{1,0},{8,10},{10,12},{12... | collective-permute-start | bytes 786440 | tf_op jit(solution)/shard_map/ppermute | solution.py:189
  9.4 2.0 %collective-permute-start.2 = (bf16[256,512]{1,0:T(8,128)(2,1)S(1)}, bf16[256,512]{1,0:T(8,128)(2,1)S(1)}, u32[]{:S(2)}, u32[]{:S(2)}) collective-permute-start(bf16[256,512]{1,0:T(8,128)(2,1)S(1)} %get-tuple-element.13.refs_0_), channel_id=1, source_target_pairs={{0,2},{2,4},{4,6},{6,7},{7,5},{5,3},{3,1},{1,0},{8,10},{10,12},{12... | collective-permute-start | bytes 786440 | tf_op jit(solution)/shard_map/ppermute | solution.py:187
  11.4 5.0 %collective-permute-done.10.refs_3_ = bf16[256,512]{1,0:T(8,128)(2,1)S(1)} collective-permute-done((bf16[256,512]{1,0:T(8,128)(2,1)S(1)}, bf16[256,512]{1,0:T(8,128)(2,1)S(1)}, u32[]{:S(2)}, u32[]{:S(2)}) %collective-permute-start.10) | collective-permute-done | bytes 262176 | tf_op jit(solution)/shard_map/ppermute | solution.py:189
  16.4 2.1 %collective-permute-start.11 = (bf16[256,512]{1,0:T(8,128)(2,1)S(1)}, bf16[256,512]{1,0:T(8,128)(2,1)S(1)}, u32[]{:S(2)}, u32[]{:S(2)}) collective-permute-start(bf16[256,512]{1,0:T(8,128)(2,1)S(1)} %collective-permute-done.10.refs_3_), channel_id=1, source_target_pairs={{0,2},{2,4},{4,6},{6,7},{7,5},{5,3},{3,1},{1,0},{8,10},{10,12},{12... | collective-permute-start | bytes 786440 | tf_op jit(solution)/shard_map/ppermute | solution.py:189
  18.6 3.5 %collective-permute-done.2.refs_2_ = bf16[256,512]{1,0:T(8,128)(2,1)S(1)} collective-permute-done((bf16[256,512]{1,0:T(8,128)(2,1)S(1)}, bf16[256,512]{1,0:T(8,128)(2,1)S(1)}, u32[]{:S(2)}, u32[]{:S(2)}) %collective-permute-start.2) | collective-permute-done | bytes 262176 | tf_op jit(solution)/shard_map/ppermute | solution.py:187
  22.1 2.1 %collective-permute-start.3 = (bf16[256,512]{1,0:T(8,128)(2,1)S(1)}, bf16[256,512]{1,0:T(8,128)(2,1)S(1)}, u32[]{:S(2)}, u32[]{:S(2)}) collective-permute-start(bf16[256,512]{1,0:T(8,128)(2,1)S(1)} %collective-permute-done.2.refs_2_), channel_id=1, source_target_pairs={{0,2},{2,4},{4,6},{6,7},{7,5},{5,3},{3,1},{1,0},{8,10},{10,12},{12... | collective-permute-start | bytes 786440 | tf_op jit(solution)/shard_map/ppermute | solution.py:187
  24.2 10.1 %shard_map.65 = (f32[512,1792]{1,0:T(8,128)S(1)}, f32[512,1792]{1,0:T(8,128)S(1)}) custom-call(bf16[256,512]{1,0:T(8,128)(2,1)S(1)} %get-tuple-element.13.refs_0_, bf16[256,512]{1,0:T(8,128)(2,1)S(1)} %get-tuple-element.14.refs_1_, bf16[256,512]{1,0:T(8,128)(2,1)S(1)} %collective-permute-done.2.refs_2_, ...), custom_call_target="tpu_custom_call" | custom-call | flops 5637144576 | bytes 25690112 | tf_op jit(solution)/shard_map/pallas_call | solution.py:157
  34.4 2.0 %collective-permute-start.4 = (bf16[256,512]{1,0:T(8,128)(2,1)S(1)}, bf16[256,512]{1,0:T(8,128)(2,1)S(1)}, u32[]{:S(2)}, u32[]{:S(2)}) collective-permute-start(bf16[256,512]{1,0:T(8,128)(2,1)S(1)} %collective-permute-done.3.refs_0_), channel_id=1, source_target_pairs={{0,2},{2,4},{4,6},{6,7},{7,5},{5,3},{3,1},{1,0},{8,10},{10,12},{12... | collective-permute-start | bytes 786440 | tf_op jit(solution)/shard_map/ppermute | solution.py:187
  36.4 2.0 %collective-permute-start.12 = (bf16[256,512]{1,0:T(8,128)(2,1)S(1)}, bf16[256,512]{1,0:T(8,128)(2,1)S(1)}, u32[]{:S(2)}, u32[]{:S(2)}) collective-permute-start(bf16[256,512]{1,0:T(8,128)(2,1)S(1)} %collective-permute-done.11.refs_1_), channel_id=1, source_target_pairs={{0,2},{2,4},{4,6},{6,7},{7,5},{5,3},{3,1},{1,0},{8,10},{10,12},{12... | collective-permute-start | bytes 786440 | tf_op jit(solution)/shard_map/ppermute | solution.py:189
  38.5 7.3 %shard_map.66 = (f32[512,1792]{1,0:T(8,128)S(1)}, f32[512,1792]{1,0:T(8,128)S(1)}) custom-call(bf16[256,512]{1,0:T(8,128)(2,1)S(1)} %collective-permute-done.3.refs_0_, bf16[256,512]{1,0:T(8,128)(2,1)S(1)} %collective-permute-done.11.refs_1_, bf16[256,512]{1,0:T(8,128)(2,1)S(1)} %collective-permute-done.14.refs_2_, ...), custom_call_target="tpu_custom_call", output_to_operand_aliasing={{0}: (8, {}), {1}: (9, {})} | custom-call | flops 3758096384 | bytes 22020096 | tf_op jit(solution)/shard_map/pallas_call | solution.py:157
  45.8 2.0 %collective-permute-start.5 = (bf16[256,512]{1,0:T(8,128)(2,1)S(1)}, bf16[256,512]{1,0:T(8,128)(2,1)S(1)}, u32[]{:S(2)}, u32[]{:S(2)}) collective-permute-start(bf16[256,512]{1,0:T(8,128)(2,1)S(1)} %collective-permute-done.4.refs_0_), channel_id=1, source_target_pairs={{0,2},{2,4},{4,6},{6,7},{7,5},{5,3},{3,1},{1,0},{8,10},{10,12},{12... | collective-permute-start | bytes 786440 | tf_op jit(solution)/shard_map/ppermute | solution.py:198
  48.7 7.5 %shard_map.67 = (f32[512,1792]{1,0:T(8,128)S(1)}, f32[512,1792]{1,0:T(8,128)S(1)}) custom-call(bf16[256,512]{1,0:T(8,128)(2,1)S(1)} %collective-permute-done.4.refs_0_, bf16[256,512]{1,0:T(8,128)(2,1)S(1)} %collective-permute-done.12.refs_1_, bf16[256,512]{1,0:T(8,128)(2,1)S(1)} %collective-permute-done.15.refs_2_, ...), custom_call_target="tpu_custom_call", output_to_operand_aliasing={{0}: (8, {}), {1}: (9, {})} | custom-call | flops 3758096384 | bytes 22020096 | tf_op jit(solution)/shard_map/pallas_call | solution.py:157
  56.2 4.5 %shard_map.68 = bf16[512,1792]{1,0:T(8,128)(2,1)S(1)} custom-call(bf16[256,512]{1,0:T(8,128)(2,1)S(1)} %collective-permute-done.5.refs_0_, bf16[256,512]{1,0:T(8,128)(2,1)S(1)} %collective-permute-done.9.refs_1_, bf16[4096,1792]{1,0:T(8,128)(2,1)} %refs_2_.1, bf16[4096,1792]{1,0:T(8,128)(2,1)} %refs_3_.1, f32[512,1792]{1,0:T(8,128)S(1)} %get-tuple-element.19.refs_4_, ...), custom_call_target="tpu_custom_call" | custom-call | flops 1879048192 | bytes 18350080 | tf_op jit(solution)/shard_map/pallas_call | solution.py:157
  65.6 1.7 %collective-permute-start.23 = (bf16[256,512]{1,0:T(8,128)(2,1)S(1)}, bf16[256,512]{1,0:T(8,128)(2,1)S(1)}, u32[]{:S(2)}, u32[]{:S(2)}) collective-permute-start(bf16[256,512]{1,0:T(8,128)(2,1)S(1)} %fusion.110), channel_id=1, source_target_pairs={{0,2},{2,4},{4,6},{6,7},{7,5},{5,3},{3,1},{1,0},{8,10},{10,12},{12... | collective-permute-start | bytes 786440 | tf_op jit(solution)/shard_map/ppermute | solution.py:215
  67.7 3.8 %collective-permute-done.16 = bf16[256,512]{1,0:T(8,128)(2,1)S(1)} collective-permute-done((bf16[256,512]{1,0:T(8,128)(2,1)S(1)}, bf16[256,512]{1,0:T(8,128)(2,1)S(1)}, u32[]{:S(2)}, u32[]{:S(2)}) %collective-permute-start.16) | collective-permute-done | bytes 262176 | tf_op jit(solution)/shard_map/ppermute | solution.py:211
  72.1 1.7 %collective-permute-start.17 = (bf16[256,512]{1,0:T(8,128)(2,1)S(1)}, bf16[256,512]{1,0:T(8,128)(2,1)S(1)}, u32[]{:S(2)}, u32[]{:S(2)}) collective-permute-start(bf16[256,512]{1,0:T(8,128)(2,1)S(1)} %fusion.95), channel_id=1, source_target_pairs={{0,2},{2,4},{4,6},{6,7},{7,5},{5,3},{3,1},{1,0},{8,10},{10,12},{12... | collective-permute-start | bytes 786440 | tf_op jit(solution)/shard_map/ppermute | solution.py:211
  74.9 2.2 %collective-permute-done.23 = bf16[256,512]{1,0:T(8,128)(2,1)S(1)} collective-permute-done((bf16[256,512]{1,0:T(8,128)(2,1)S(1)}, bf16[256,512]{1,0:T(8,128)(2,1)S(1)}, u32[]{:S(2)}, u32[]{:S(2)}) %collective-permute-start.23) | collective-permute-done | bytes 262176 | tf_op jit(solution)/shard_map/ppermute | solution.py:215
  80.5 2.2 %collective-permute-done.17 = bf16[256,512]{1,0:T(8,128)(2,1)S(1)} collective-permute-done((bf16[256,512]{1,0:T(8,128)(2,1)S(1)}, bf16[256,512]{1,0:T(8,128)(2,1)S(1)}, u32[]{:S(2)}, u32[]{:S(2)}) %collective-permute-start.17) | collective-permute-done | bytes 262176 | tf_op jit(solution)/shard_map/ppermute | solution.py:211
  86.1 4.3 %collective-permute-done.27 = bf16[256,512]{1,0:T(8,128)(2,1)S(1)} collective-permute-done((bf16[256,512]{1,0:T(8,128)(2,1)S(1)}, bf16[256,512]{1,0:T(8,128)(2,1)S(1)}, u32[]{:S(2)}, u32[]{:S(2)}) %collective-permute-start.27) | collective-permute-done | bytes 262176 | tf_op jit(solution)/shard_map/ppermute | solution.py:212
  92.9 1.8 %collective-permute-start.19 = (bf16[256,512]{1,0:T(8,128)(2,1)S(1)}, bf16[256,512]{1,0:T(8,128)(2,1)S(1)}, u32[]{:S(2)}, u32[]{:S(2)}) collective-permute-start(bf16[256,512]{1,0:T(8,128)(2,1)S(1)} %fusion.107), channel_id=1, source_target_pairs={{0,2},{2,4},{4,6},{6,7},{7,5},{5,3},{3,1},{1,0},{8,10},{10,12},{12... | collective-permute-start | bytes 786440 | tf_op jit(solution)/shard_map/ppermute | solution.py:221
  95.3 1.7 %collective-permute-start.25 = (bf16[256,512]{1,0:T(8,128)(2,1)S(1)}, bf16[256,512]{1,0:T(8,128)(2,1)S(1)}, u32[]{:S(2)}, u32[]{:S(2)}) collective-permute-start(bf16[256,512]{1,0:T(8,128)(2,1)S(1)} %fusion.104), channel_id=1, source_target_pairs={{0,2},{2,4},{4,6},{6,7},{7,5},{5,3},{3,1},{1,0},{8,10},{10,12},{12... | collective-permute-start | bytes 786440 | tf_op jit(solution)/shard_map/ppermute | solution.py:224
  97.0 3.1 %collective-permute-done.28 = bf16[256,512]{1,0:T(8,128)(2,1)S(1)} collective-permute-done((bf16[256,512]{1,0:T(8,128)(2,1)S(1)}, bf16[256,512]{1,0:T(8,128)(2,1)S(1)}, u32[]{:S(2)}, u32[]{:S(2)}) %collective-permute-start.28) | collective-permute-done | bytes 262176 | tf_op jit(solution)/shard_map/ppermute | solution.py:212
  102.1 5.1 %collective-permute-done.29 = bf16[256,512]{1,0:T(8,128)(2,1)S(1)} collective-permute-done((bf16[256,512]{1,0:T(8,128)(2,1)S(1)}, bf16[256,512]{1,0:T(8,128)(2,1)S(1)}, u32[]{:S(2)}, u32[]{:S(2)}) %collective-permute-start.29) | collective-permute-done | bytes 262176 | tf_op jit(solution)/shard_map/ppermute | solution.py:222
  (73 shorter events, 25.9 us)
Async XLA Ops:
  6.4 10.0 %collective-permute-start.10 = (bf16[256,512]{1,0:T(8,128)(2,1)S(1)}, bf16[256,512]{1,0:T(8,128)(2,1)S(1)}, u32[]{:S(2)}, u32[]{:S(2)}) collective-permute-start(bf16[256,512]{1,0:T(8,128)(2,1)S(1)} %get-tuple-element.14.refs_1_), channel_id=1, source_target_pairs={{0,2},{2,4},{4,6},{6,7},{7,5},{5,3},{3,1},{1,0},{8,10},{10,12},{12... | collective-permute-start | bytes 786440 | tf_op jit(solution)/shard_map/ppermute | solution.py:189
  9.4 9.2 %collective-permute-start.13 = (bf16[256,512]{1,0:T(8,128)(2,1)S(1)}, bf16[256,512]{1,0:T(8,128)(2,1)S(1)}, u32[]{:S(2)}, u32[]{:S(2)}) collective-permute-start(bf16[256,512]{1,0:T(8,128)(2,1)S(1)} %get-tuple-element.13.refs_0_), channel_id=1, source_target_pairs={{0,1},{2,0},{4,2},{6,4},{7,6},{5,7},{3,5},{1,3},{8,9},{10,8},{12,1... | collective-permute-start | bytes 786440 | tf_op jit(solution)/shard_map/ppermute | solution.py:188
  9.4 12.6 %collective-permute-start.2 = (bf16[256,512]{1,0:T(8,128)(2,1)S(1)}, bf16[256,512]{1,0:T(8,128)(2,1)S(1)}, u32[]{:S(2)}, u32[]{:S(2)}) collective-permute-start(bf16[256,512]{1,0:T(8,128)(2,1)S(1)} %get-tuple-element.13.refs_0_), channel_id=1, source_target_pairs={{0,2},{2,4},{4,6},{6,7},{7,5},{5,3},{3,1},{1,0},{8,10},{10,12},{12... | collective-permute-start | bytes 786440 | tf_op jit(solution)/shard_map/ppermute | solution.py:187
  11.4 12.8 %collective-permute-start.6 = (bf16[256,512]{1,0:T(8,128)(2,1)S(1)}, bf16[256,512]{1,0:T(8,128)(2,1)S(1)}, u32[]{:S(2)}, u32[]{:S(2)}) collective-permute-start(bf16[256,512]{1,0:T(8,128)(2,1)S(1)} %get-tuple-element.14.refs_1_), channel_id=1, source_target_pairs={{0,1},{2,0},{4,2},{6,4},{7,6},{5,7},{3,5},{1,3},{8,9},{10,8},{12,1... | collective-permute-start | bytes 786440 | tf_op jit(solution)/shard_map/ppermute | solution.py:190
  16.4 20.0 %collective-permute-start.11 = (bf16[256,512]{1,0:T(8,128)(2,1)S(1)}, bf16[256,512]{1,0:T(8,128)(2,1)S(1)}, u32[]{:S(2)}, u32[]{:S(2)}) collective-permute-start(bf16[256,512]{1,0:T(8,128)(2,1)S(1)} %collective-permute-done.10.refs_3_), channel_id=1, source_target_pairs={{0,2},{2,4},{4,6},{6,7},{7,5},{5,3},{3,1},{1,0},{8,10},{10,12},{12... | collective-permute-start | bytes 786440 | tf_op jit(solution)/shard_map/ppermute | solution.py:189
  18.6 19.8 %collective-permute-start.14 = (bf16[256,512]{1,0:T(8,128)(2,1)S(1)}, bf16[256,512]{1,0:T(8,128)(2,1)S(1)}, u32[]{:S(2)}, u32[]{:S(2)}) collective-permute-start(bf16[256,512]{1,0:T(8,128)(2,1)S(1)} %collective-permute-done.13.refs_4_), channel_id=1, source_target_pairs={{0,1},{2,0},{4,2},{6,4},{7,6},{5,7},{3,5},{1,3},{8,9},{10,8},{12,1... | collective-permute-start | bytes 786440 | tf_op jit(solution)/shard_map/ppermute | solution.py:188
  22.1 12.3 %collective-permute-start.3 = (bf16[256,512]{1,0:T(8,128)(2,1)S(1)}, bf16[256,512]{1,0:T(8,128)(2,1)S(1)}, u32[]{:S(2)}, u32[]{:S(2)}) collective-permute-start(bf16[256,512]{1,0:T(8,128)(2,1)S(1)} %collective-permute-done.2.refs_2_), channel_id=1, source_target_pairs={{0,2},{2,4},{4,6},{6,7},{7,5},{5,3},{3,1},{1,0},{8,10},{10,12},{12... | collective-permute-start | bytes 786440 | tf_op jit(solution)/shard_map/ppermute | solution.py:187
  24.2 12.2 %collective-permute-start.7 = (bf16[256,512]{1,0:T(8,128)(2,1)S(1)}, bf16[256,512]{1,0:T(8,128)(2,1)S(1)}, u32[]{:S(2)}, u32[]{:S(2)}) collective-permute-start(bf16[256,512]{1,0:T(8,128)(2,1)S(1)} %collective-permute-done.6.refs_5_), channel_id=1, source_target_pairs={{0,1},{2,0},{4,2},{6,4},{7,6},{5,7},{3,5},{1,3},{8,9},{10,8},{12,1... | collective-permute-start | bytes 786440 | tf_op jit(solution)/shard_map/ppermute | solution.py:190
  34.4 11.4 %collective-permute-start.4 = (bf16[256,512]{1,0:T(8,128)(2,1)S(1)}, bf16[256,512]{1,0:T(8,128)(2,1)S(1)}, u32[]{:S(2)}, u32[]{:S(2)}) collective-permute-start(bf16[256,512]{1,0:T(8,128)(2,1)S(1)} %collective-permute-done.3.refs_0_), channel_id=1, source_target_pairs={{0,2},{2,4},{4,6},{6,7},{7,5},{5,3},{3,1},{1,0},{8,10},{10,12},{12... | collective-permute-start | bytes 786440 | tf_op jit(solution)/shard_map/ppermute | solution.py:187
  36.4 11.4 %collective-permute-start.8 = (bf16[256,512]{1,0:T(8,128)(2,1)S(1)}, bf16[256,512]{1,0:T(8,128)(2,1)S(1)}, u32[]{:S(2)}, u32[]{:S(2)}) collective-permute-start(bf16[256,512]{1,0:T(8,128)(2,1)S(1)} %collective-permute-done.7.refs_3_), channel_id=1, source_target_pairs={{0,1},{2,0},{4,2},{6,4},{7,6},{5,7},{3,5},{1,3},{8,9},{10,8},{12,1... | collective-permute-start | bytes 786440 | tf_op jit(solution)/shard_map/ppermute | solution.py:190
  36.4 11.5 %collective-permute-start.12 = (bf16[256,512]{1,0:T(8,128)(2,1)S(1)}, bf16[256,512]{1,0:T(8,128)(2,1)S(1)}, u32[]{:S(2)}, u32[]{:S(2)}) collective-permute-start(bf16[256,512]{1,0:T(8,128)(2,1)S(1)} %collective-permute-done.11.refs_1_), channel_id=1, source_target_pairs={{0,2},{2,4},{4,6},{6,7},{7,5},{5,3},{3,1},{1,0},{8,10},{10,12},{12... | collective-permute-start | bytes 786440 | tf_op jit(solution)/shard_map/ppermute | solution.py:189
  38.4 10.3 %collective-permute-start.15 = (bf16[256,512]{1,0:T(8,128)(2,1)S(1)}, bf16[256,512]{1,0:T(8,128)(2,1)S(1)}, u32[]{:S(2)}, u32[]{:S(2)}) collective-permute-start(bf16[256,512]{1,0:T(8,128)(2,1)S(1)} %collective-permute-done.14.refs_2_), channel_id=1, source_target_pairs={{0,1},{2,0},{4,2},{6,4},{7,6},{5,7},{3,5},{1,3},{8,9},{10,8},{12,1... | collective-permute-start | bytes 786440 | tf_op jit(solution)/shard_map/ppermute | solution.py:188
  45.8 10.4 %collective-permute-start.5 = (bf16[256,512]{1,0:T(8,128)(2,1)S(1)}, bf16[256,512]{1,0:T(8,128)(2,1)S(1)}, u32[]{:S(2)}, u32[]{:S(2)}) collective-permute-start(bf16[256,512]{1,0:T(8,128)(2,1)S(1)} %collective-permute-done.4.refs_0_), channel_id=1, source_target_pairs={{0,2},{2,4},{4,6},{6,7},{7,5},{5,3},{3,1},{1,0},{8,10},{10,12},{12... | collective-permute-start | bytes 786440 | tf_op jit(solution)/shard_map/ppermute | solution.py:198
  62.1 9.3 %collective-permute-start.16 = (bf16[256,512]{1,0:T(8,128)(2,1)S(1)}, bf16[256,512]{1,0:T(8,128)(2,1)S(1)}, u32[]{:S(2)}, u32[]{:S(2)}) collective-permute-start(bf16[256,512]{1,0:T(8,128)(2,1)S(1)} %fusion.113), channel_id=1, source_target_pairs={{0,2},{2,4},{4,6},{6,7},{7,5},{5,3},{3,1},{1,0},{8,10},{10,12},{12... | collective-permute-start | bytes 786440 | tf_op jit(solution)/shard_map/ppermute | solution.py:211
  64.4 9.3 %collective-permute-start.20 = (bf16[256,512]{1,0:T(8,128)(2,1)S(1)}, bf16[256,512]{1,0:T(8,128)(2,1)S(1)}, u32[]{:S(2)}, u32[]{:S(2)}) collective-permute-start(bf16[256,512]{1,0:T(8,128)(2,1)S(1)} %fusion.119), channel_id=1, source_target_pairs={{0,1},{2,0},{4,2},{6,4},{7,6},{5,7},{3,5},{1,3},{8,9},{10,8},{12,1... | collective-permute-start | bytes 786440 | tf_op jit(solution)/shard_map/ppermute | solution.py:214
  65.6 11.5 %collective-permute-start.23 = (bf16[256,512]{1,0:T(8,128)(2,1)S(1)}, bf16[256,512]{1,0:T(8,128)(2,1)S(1)}, u32[]{:S(2)}, u32[]{:S(2)}) collective-permute-start(bf16[256,512]{1,0:T(8,128)(2,1)S(1)} %fusion.110), channel_id=1, source_target_pairs={{0,2},{2,4},{4,6},{6,7},{7,5},{5,3},{3,1},{1,0},{8,10},{10,12},{12... | collective-permute-start | bytes 786440 | tf_op jit(solution)/shard_map/ppermute | solution.py:215
  67.2 12.1 %collective-permute-start.26 = (bf16[256,512]{1,0:T(8,128)(2,1)S(1)}, bf16[256,512]{1,0:T(8,128)(2,1)S(1)}, u32[]{:S(2)}, u32[]{:S(2)}) collective-permute-start(bf16[256,512]{1,0:T(8,128)(2,1)S(1)} %fusion.116), channel_id=1, source_target_pairs={{0,1},{2,0},{4,2},{6,4},{7,6},{5,7},{3,5},{1,3},{8,9},{10,8},{12,1... | collective-permute-start | bytes 786440 | tf_op jit(solution)/shard_map/ppermute | solution.py:212
  72.1 10.6 %collective-permute-start.17 = (bf16[256,512]{1,0:T(8,128)(2,1)S(1)}, bf16[256,512]{1,0:T(8,128)(2,1)S(1)}, u32[]{:S(2)}, u32[]{:S(2)}) collective-permute-start(bf16[256,512]{1,0:T(8,128)(2,1)S(1)} %fusion.95), channel_id=1, source_target_pairs={{0,2},{2,4},{4,6},{6,7},{7,5},{5,3},{3,1},{1,0},{8,10},{10,12},{12... | collective-permute-start | bytes 786440 | tf_op jit(solution)/shard_map/ppermute | solution.py:211
  74.4 10.5 %collective-permute-start.21 = (bf16[256,512]{1,0:T(8,128)(2,1)S(1)}, bf16[256,512]{1,0:T(8,128)(2,1)S(1)}, u32[]{:S(2)}, u32[]{:S(2)}) collective-permute-start(bf16[256,512]{1,0:T(8,128)(2,1)S(1)} %fusion.86), channel_id=1, source_target_pairs={{0,1},{2,0},{4,2},{6,4},{7,6},{5,7},{3,5},{1,3},{8,9},{10,8},{12,1... | collective-permute-start | bytes 786440 | tf_op jit(solution)/shard_map/ppermute | solution.py:214
  77.7 16.9 %collective-permute-start.24 = (bf16[256,512]{1,0:T(8,128)(2,1)S(1)}, bf16[256,512]{1,0:T(8,128)(2,1)S(1)}, u32[]{:S(2)}, u32[]{:S(2)}) collective-permute-start(bf16[256,512]{1,0:T(8,128)(2,1)S(1)} %fusion.98), channel_id=1, source_target_pairs={{0,2},{2,4},{4,6},{6,7},{7,5},{5,3},{3,1},{1,0},{8,10},{10,12},{12... | collective-permute-start | bytes 786440 | tf_op jit(solution)/shard_map/ppermute | solution.py:215
  80.0 10.4 %collective-permute-start.27 = (bf16[256,512]{1,0:T(8,128)(2,1)S(1)}, bf16[256,512]{1,0:T(8,128)(2,1)S(1)}, u32[]{:S(2)}, u32[]{:S(2)}) collective-permute-start(bf16[256,512]{1,0:T(8,128)(2,1)S(1)} %fusion.80), channel_id=1, source_target_pairs={{0,1},{2,0},{4,2},{6,4},{7,6},{5,7},{3,5},{1,3},{8,9},{10,8},{12,1... | collective-permute-start | bytes 786440 | tf_op jit(solution)/shard_map/ppermute | solution.py:212
  83.3 8.9 %collective-permute-start.18 = (bf16[256,512]{1,0:T(8,128)(2,1)S(1)}, bf16[256,512]{1,0:T(8,128)(2,1)S(1)}, u32[]{:S(2)}, u32[]{:S(2)}) collective-permute-start(bf16[256,512]{1,0:T(8,128)(2,1)S(1)} %fusion.101), channel_id=1, source_target_pairs={{0,2},{2,4},{4,6},{6,7},{7,5},{5,3},{3,1},{1,0},{8,10},{10,12},{12... | collective-permute-start | bytes 786440 | tf_op jit(solution)/shard_map/ppermute | solution.py:211
  85.6 15.7 %collective-permute-start.22 = (bf16[256,512]{1,0:T(8,128)(2,1)S(1)}, bf16[256,512]{1,0:T(8,128)(2,1)S(1)}, u32[]{:S(2)}, u32[]{:S(2)}) collective-permute-start(bf16[256,512]{1,0:T(8,128)(2,1)S(1)} %fusion.92), channel_id=1, source_target_pairs={{0,1},{2,0},{4,2},{6,4},{7,6},{5,7},{3,5},{1,3},{8,9},{10,8},{12,1... | collective-permute-start | bytes 786440 | tf_op jit(solution)/shard_map/ppermute | solution.py:223
  91.1 9.1 %collective-permute-start.28 = (bf16[256,512]{1,0:T(8,128)(2,1)S(1)}, bf16[256,512]{1,0:T(8,128)(2,1)S(1)}, u32[]{:S(2)}, u32[]{:S(2)}) collective-permute-start(bf16[256,512]{1,0:T(8,128)(2,1)S(1)} %fusion.83), channel_id=1, source_target_pairs={{0,1},{2,0},{4,2},{6,4},{7,6},{5,7},{3,5},{1,3},{8,9},{10,8},{12,1... | collective-permute-start | bytes 786440 | tf_op jit(solution)/shard_map/ppermute | solution.py:212
  (13 other events, 78.0 us)

commit v3 on v2

v3 whole, which is shorter than its diff:
```python
import functools

import jax
import jax.numpy as jnp
from jax import lax
from jax.experimental import pallas as pl
from jax.experimental.pallas import tpu as pltpu
from jax.sharding import PartitionSpec as P

BLOCK = 128
F32 = jnp.float32
BF16 = jnp.bfloat16
MIB = 1024 * 1024
IN_VMEM = pl.BlockSpec(memory_space=pltpu.VMEM)


def ring_order(n):
    if n == 8:
        return list(range(0, n, 2)) + list(range(n - 1, 0, -2))
    return list(range(n))


def owner_at(step, n):
    here = lax.axis_index("tp")
    if n != 8:
        return (here + (step + n)) & (n - 1) if n & (n - 1) == 0 else lax.rem(here + (step + n), n)
    place = jnp.where((here & 1) == 0, here >> 1, n - 1 - (here >> 1))
    there = (place + (step + n)) & (n - 1)
    return jnp.where(there < n // 2, there * 2, 2 * n - 1 - 2 * there)


def shift(order, step):
    n = len(order)
    return [(order[i], order[(i + step) % n]) for i in range(n)]


def in_hbm(x):
    return pltpu.with_memory_space_constraint(x, pltpu.HBM)


def pack_kernel(mine_c, other_c, order, mine, other, _, first_half, second_half, sems):
    loaders = mine_c.shape[0]
    blocks = order.shape[0]
    slots = mine.shape[0] // BLOCK // loaders
    half = first_half.shape[0] // BLOCK
    own = 2 * half
    me = lax.axis_index("seq")

    first = [jnp.where(me == 0, mine_c[i], other_c[i]) for i in range(loaders)]
    second = [jnp.where(me == 0, other_c[i], mine_c[i]) for i in range(loaders)]
    counts = first + second
    copies = []
    for i in range(own):
        place = me * own + i
        source = jnp.int32(0)
        for b in range(blocks):
            source = jnp.where(order[b] == place, b, source)
        offset = jnp.int32(0)
        row = jnp.int32(0)
        for s in range(2 * loaders):
            inside = (source >= offset) & (source < offset + counts[s])
            row = jnp.where(inside, s * slots + source - offset, row)
            offset = offset + counts[s]
        holder = jnp.where(row >= loaders * slots, 1, 0)
        row = row - holder * (loaders * slots)
        start = pl.multiple_of(row * BLOCK, BLOCK)
        out = first_half if i < half else second_half
        at = pl.ds(i % half * BLOCK, BLOCK)

        @pl.when(holder == me)
        def _(start=start, i=i, out=out, at=at):
            pltpu.make_async_copy(
                mine.at[pl.ds(start, BLOCK)], out.at[at], sems.at[i]
            ).start()

        @pl.when(holder != me)
        def _(start=start, i=i, out=out, at=at):
            pltpu.make_async_copy(
                other.at[pl.ds(start, BLOCK)], out.at[at], sems.at[i]
            ).start()

    for i in range(own):
        out = first_half if i < half else second_half
        pltpu.make_async_copy(
            mine.at[pl.ds(0, BLOCK)], out.at[pl.ds(i % half * BLOCK, BLOCK)], sems.at[i]
        ).wait()


def pack(loaded, block_counts, seq_order, after):
    swap = [(0, 1), (1, 0)]
    other = lax.ppermute(loaded, "seq", swap)
    other_counts = lax.ppermute(block_counts, "seq", swap)
    own = seq_order.shape[0] // 2
    width = loaded.shape[1]
    rows = own // 2 * BLOCK
    any_spec = pl.BlockSpec(memory_space=pl.ANY)
    whole = pl.BlockSpec((rows, width), lambda i, *_: (0, 0))
    return pl.pallas_call(
        pack_kernel,
        out_shape=[jax.ShapeDtypeStruct((rows, width), loaded.dtype)] * 2,
        grid_spec=pltpu.PrefetchScalarGridSpec(
            num_scalar_prefetch=3,
            grid=(1,),
            in_specs=[any_spec, any_spec, IN_VMEM],
            out_specs=[whole, whole],
            scratch_shapes=[pltpu.SemaphoreType.DMA((own,))],
        ),
        compiler_params=pltpu.CompilerParams(vmem_limit_bytes=8 * MIB),
    )(in_hbm(block_counts), other_counts, in_hbm(seq_order), in_hbm(loaded), other, after)


GATE, UP, DOWN = range(3)


def bring_start(bring, n, sources, targets, sems):
    copies = []
    for i, (which, step) in enumerate(bring):
        rows, cols = targets[i].shape
        source = sources[which]
        if which == DOWN:
            piece = source.at[:, pl.ds(pl.multiple_of(owner_at(step, n) * cols, cols), cols)]
        else:
            piece = source.at[pl.ds(pl.multiple_of(owner_at(step, n) * rows, rows), rows)]
        copies.append(pltpu.make_async_copy(piece, targets[i], sems.at[i]))
        copies[-1].start()
    return copies


def brought(bring, sources, n):
    shapes = []
    for which, _ in bring:
        rows, cols = sources[which].shape
        shape = (rows, cols // n) if which == DOWN else (rows // n, cols)
        shapes.append(pltpu.VMEM(shape, sources[which].dtype))
    return shapes


def fetch_kernel(bring, n, has_after, *refs):
    first = 3 + has_after
    for copy in bring_start(bring, n, refs[:3], refs[first:-1], refs[-1]):
        copy.wait()


def fetch(sources, bring, after=None):
    n = lax.axis_size("tp")
    outs = brought(bring, sources, n)
    any_spec = pl.BlockSpec(memory_space=pl.ANY)
    more = [] if after is None else [after]
    out = pl.pallas_call(
        functools.partial(fetch_kernel, bring, n, len(more)),
        out_shape=outs,
        in_specs=[any_spec] * 3 + [IN_VMEM] * len(more),
        out_specs=[IN_VMEM] * len(outs),
        scratch_shapes=[pltpu.SemaphoreType.DMA((len(bring),))],
        compiler_params=pltpu.CompilerParams(vmem_limit_bytes=MIB),
        cost_estimate=pl.CostEstimate(
            flops=0, bytes_accessed=len(bring) * 4 * MIB, transcendentals=0
        ),
    )(*sources, *more)
    return dict(zip(bring, out))


def stage_kernel(pieces, has_acc, last, bring, n, *refs):
    refs = list(refs)
    if bring:
        sems = refs.pop()
        sources = [refs.pop(0) for _ in range(3)]
        targets = refs[-len(bring) :]
        bring_start(bring, n, sources, targets, sems)
    xs = [refs.pop(0) for _ in range(pieces)]
    weights = [[refs.pop(0) for _ in range(pieces)] for _ in range(2)]
    acc = [refs.pop(0), refs.pop(0)] if has_acc else None

    def columns(start, tile):
        cols = pl.ds(start, tile)
        sums = []
        for k in range(2):
            total = acc[k][:, cols] if has_acc else None
            for x, weight in zip(xs, weights[k]):
                term = jnp.dot(x[...], weight[:, cols], preferred_element_type=F32)
                total = term if total is None else total + term
            sums.append(total)
        if last:
            gate, up = sums
            refs[0][:, cols] = (gate / (1.0 + jnp.exp(-gate)) * up).astype(BF16)
        else:
            refs[0][:, cols] = sums[0]
            refs[1][:, cols] = sums[1]

    lanes = weights[0][0].shape[1] // 128
    if bring:
        count = next(c for c in range(2, lanes + 1) if lanes % c == 0)
        tile = lanes // count * 128
        pl.loop(0, count)(lambda i: columns(pl.multiple_of(i * tile, tile), tile))
    else:
        tile = 256 if lanes % 2 == 0 else 128
        for i in range(lanes * 128 // tile):
            columns(i * tile, tile)
    if bring:
        for i, target in enumerate(targets):
            pltpu.make_async_copy(target, target, sems.at[i]).wait()


def stage(held, sources, xs, steps, acc=(), last=False, bring=()):
    n = lax.axis_size("tp")
    rows, width = xs[0].shape
    hid = sources[GATE].shape[1]
    operands = [*xs, *[held[which, step] for which in (GATE, UP) for step in steps], *acc]
    if last:
        out_shape = [pltpu.VMEM((rows, hid), BF16)]
    else:
        out_shape = [pltpu.VMEM((rows, hid), F32)] * 2
    outs = len(out_shape)
    in_specs = [IN_VMEM] * len(operands)
    scratch = []
    if bring:
        operands = [*sources, *operands]
        in_specs = [pl.BlockSpec(memory_space=pl.ANY)] * 3 + in_specs
        out_shape += brought(bring, sources, n)
        scratch = [pltpu.SemaphoreType.DMA((len(bring),))]
    aliases = {len(operands) - 2: 0, len(operands) - 1: 1} if acc and not last else {}
    out = pl.pallas_call(
        functools.partial(stage_kernel, len(xs), bool(acc), last, bring, n),
        out_shape=out_shape,
        in_specs=in_specs,
        out_specs=[IN_VMEM] * len(out_shape),
        scratch_shapes=scratch,
        input_output_aliases=aliases,
        compiler_params=pltpu.CompilerParams(vmem_limit_bytes=4 * MIB),
        cost_estimate=pl.CostEstimate(
            flops=4 * rows * width * len(xs) * hid, bytes_accessed=0, transcendentals=0
        ),
    )(*operands)
    held.update(zip(bring, out[outs:]))
    return out[:outs]


def down_kernel(h, weight, *refs):
    total = jnp.dot(h[...], weight[...], preferred_element_type=F32)
    for other in refs[:-1]:
        total = total + other[...].astype(F32)
    refs[-1][...] = total.astype(refs[-1].dtype)


def down(h, weight, *arrived, dtype=BF16):
    operands = [h, weight, *arrived]
    return pl.pallas_call(
        down_kernel,
        out_shape=jax.ShapeDtypeStruct((h.shape[0], weight.shape[1]), dtype),
        in_specs=[IN_VMEM] * len(operands),
        out_specs=IN_VMEM,
        compiler_params=pltpu.CompilerParams(vmem_limit_bytes=4 * MIB),
        cost_estimate=pl.CostEstimate(
            flops=2 * h.size * weight.shape[1], bytes_accessed=0, transcendentals=0
        ),
    )(*operands)


def finish_kernel(own_a, own_b, a_f, a_b, b_f, b_b, out):
    half = own_a.shape[0]
    for i, (own, f, b) in enumerate(((own_a, a_f, a_b), (own_b, b_f, b_b))):
        total = own[...] + f[...].astype(F32) + b[...].astype(F32)
        out[i * half : (i + 1) * half, :] = total.astype(BF16)


def finish(own_a, own_b, arrived_a, arrived_b):
    rows, width = own_a.shape
    return pl.pallas_call(
        finish_kernel,
        out_shape=jax.ShapeDtypeStruct((2 * rows, width), BF16),
        in_specs=[IN_VMEM] * 6,
        out_specs=IN_VMEM,
        compiler_params=pltpu.CompilerParams(vmem_limit_bytes=8 * MIB),
    )(own_a, own_b, *arrived_a, *arrived_b)


def both(*steps):
    return tuple((which, step) for step in steps for which in (GATE, UP))


def body(loaded, block_counts, seq_order, gate_weight, up_weight, down_weight):
    n = lax.axis_size("tp")
    order = ring_order(n)
    fwd, bwd = shift(order, 1), shift(order, -1)
    far = n // 2
    sources = [in_hbm(w) for w in (gate_weight, up_weight, down_weight)]

    later = [slot for step in range(3, far) for slot in both(step, -step)] + list(both(far))
    later += [(DOWN, far)]
    for step in range(far - 1, 0, -1):
        later += [(DOWN, step), (DOWN, -step)]
    later += [(DOWN, 0)]
    stages = 2 * (far - 1)
    shares = [
        tuple(later[i * len(later) // stages : (i + 1) * len(later) // stages])
        for i in range(stages)
    ]

    held = fetch(sources, both(0))
    own_a, own_b = pack(loaded, block_counts, seq_order, held[GATE, 0])
    run = functools.partial(stage, held, sources)

    a_f = a_b = own_a
    b_f = b_b = own_b
    acc_a = run([own_a], [0], bring=both(1))
    acc_b = run([own_b], [0], bring=both(-1))
    held |= fetch(sources, both(2, -2), acc_b[0])
    for step in range(1, far):
        a_f = lax.ppermute(a_f, "tp", fwd)
        a_b = lax.ppermute(a_b, "tp", bwd)
        b_f = lax.ppermute(b_f, "tp", fwd)
        b_b = lax.ppermute(b_b, "tp", bwd)
        acc_a = run([a_f, a_b], [-step, step], acc_a, bring=shares[2 * step - 2])
        acc_b = run([b_f, b_b], [-step, step], acc_b, bring=shares[2 * step - 1])
    a_f = lax.ppermute(a_f, "tp", fwd)
    b_b = lax.ppermute(b_b, "tp", bwd)
    (h_a,) = run([a_f], [far], acc_a, last=True)
    (h_b,) = run([b_b], [far], acc_b, last=True)

    def term_a(step, *arrived):
        return down(h_a, held[DOWN, step], *arrived)

    def term_b(step, *arrived):
        return down(h_b, held[DOWN, step], *arrived)

    a_f, b_b = term_a(far), term_b(far)
    a_b, b_f = term_a(1 - far), term_b(far - 1)
    for step in range(far - 1, 0, -1):
        a_f = term_a(step, lax.ppermute(a_f, "tp", fwd))
        b_b = term_b(-step, lax.ppermute(b_b, "tp", bwd))
        if step > 1:
            a_b = term_a(1 - step, lax.ppermute(a_b, "tp", bwd))
            b_f = term_b(step - 1, lax.ppermute(b_f, "tp", fwd))
    last = held[DOWN, 0]
    own = down(h_a, last, dtype=F32), down(h_b, last, dtype=F32)
    return finish(
        *own,
        (lax.ppermute(a_f, "tp", fwd), lax.ppermute(a_b, "tp", bwd)),
        (lax.ppermute(b_f, "tp", fwd), lax.ppermute(b_b, "tp", bwd)),
    )


def solution(mesh):
    return jax.shard_map(
        body,
        mesh=mesh,
        in_specs=(
            P(("groups", "seq"), "tp"),
            P(("groups", "seq")),
            P("groups"),
            P(None, "tp"),
            P(None, "tp"),
            P("tp", None),
        ),
        out_specs=P(("groups", "seq"), "tp"),
        check_vma=False,
    )
```

time: 109 us -> 96 us (0.88)
  matrix products: 10.5 us -> 0 us
  waiting for transfers between devices: 32.6 us -> 22.1 us
  Pallas kernels: 30.7 us -> 40.8 us
  local copies, waits for them, and re-layouts: 2.46 us -> 0 us
  starting transfers between devices: 31.3 us -> 32.6 us
    ppermute x0 -> x14, waiting for transfers between devices: none -> 17.6 us  [the longest x2 8.71 us: body(): b_f = term_b(step - 1, lax.ppermute(b_f, 'tp', fwd))]
    ppermute x0 -> x14, starting transfers between devices: none -> 15.2 us  [the longest x3 4.86 us: body(): b_b = term_b(-step, lax.ppermute(b_b, 'tp', bwd))]
    ppermute x8 -> x4, starting transfers between devices: 14.8 us -> 2.39 us  [body(): a_f = lax.ppermute(a_f, 'tp', fwd)]
    ppermute x6 -> x3, starting transfers between devices: 12 us -> 0.56 us  [body(): b_f = lax.ppermute(b_f, 'tp', fwd)]
    dot_general x16 -> x0, matrix products: 10.5 us -> none  [term(): return jnp.dot(rows, cols, preferred_element_type=F32)]
    ppermute x8 -> x4, waiting for transfers between devices: 9.95 us -> 0.18 us  [body(): a_f = lax.ppermute(a_f, 'tp', fwd)]
    pallas_call x4 -> x29, Pallas kernels: 29.4 us -> 38.7 us  [the longest x10 22.3 us: stage(): pl.pallas_call(functools.partial(stage_kernel, len(xs), bool(acc), last,...]
    ppermute x8 -> x4, waiting for transfers between devices: 12.6 us -> 4.24 us  [body(): b_b = lax.ppermute(b_b, 'tp', bwd)]
  transfers between devices with their start and end apart: 30 -> 30, of which waited for: 12 -> 10; matrix products, arithmetic and copies ran while one was open for 8% -> 0% of each run, Pallas kernels for 23% -> 39%
where the time goes in v3:
time: 96 us; the launch traced here: 95.8 us
  Pallas kernels  40.8 us (42%)
  starting transfers between devices  32.6 us (34%)
  waiting for transfers between devices  22.1 us (23%)
    pallas_call x10, Pallas kernels, stage(): pl.pallas_call(functools.partial(stage_kernel, len(xs), bool(acc), last,...  22.3 us
    pallas_call x16, Pallas kernels, down(): pl.pallas_call(down_kernel, out_shape=jax.ShapeDtypeStruct((h.shape[0], w...  10.2 us
    ppermute x2, waiting for transfers between devices, body(): b_f = term_b(step - 1, lax.ppermute(b_f, 'tp', fwd))  8.71 us
    ppermute x4, starting transfers between devices, body(): b_b = lax.ppermute(b_b, 'tp', bwd)  7.22 us
    ppermute x3, starting transfers between devices, body(): a_b = lax.ppermute(a_b, 'tp', bwd)  6.75 us
    pallas_call x2, Pallas kernels, fetch(): pl.pallas_call(functools.partial(fetch_kernel, bring, n, len(more)), out_...  5.27 us
    ppermute x3, starting transfers between devices, body(): b_b = term_b(-step, lax.ppermute(b_b, 'tp', bwd))  4.86 us
    ppermute x4, waiting for transfers between devices, body(): b_b = lax.ppermute(b_b, 'tp', bwd)  4.24 us
  transfers between devices with their start and end apart: 30, of which 10 were waited for; matrix products, arithmetic and copies ran while one was open for 0% of the time, Pallas kernels for 39%

profile of v3, /device:TPU:0, one launch (start us, length us, event | category | flops | bytes accessed | tf_op | source)
XLA Modules:
  0.0 95.8 jit_solution(10165851429229313702)
XLA Ops:
  0.5 2.1 %shard_map.64 = (bf16[512,1792]{1,0:T(8,128)(2,1)S(1)}, bf16[512,1792]{1,0:T(8,128)(2,1)S(1)}) custom-call(bf16[4096,1792]{1,0:T(8,128)(2,1)} %refs_0_.19, bf16[4096,1792]{1,0:T(8,128)(2,1)} %refs_1_.19, bf16[1792,4096]{1,0:T(8,128)(2,1)} %refs_2_.19), custom_call_target="tpu_custom_call" | custom-call | bytes 8388608 | tf_op jit(solution)/shard_map/pallas_call | solution.py:149
  2.6 2.1 %shard_map.65 = (bf16[256,512]{1,0:T(8,128)(2,1)S(1)}, bf16[256,512]{1,0:T(8,128)(2,1)S(1)}) custom-call(s32[2]{0:T(128)} %mine_c.1, s32[2]{0:T(128)S(1)} %collective-permute-done.other_c, s32[8]{0:T(128)} %order.1, bf16[768,512]{1,0:T(8,128)(2,1)} %mine.1, bf16[768,512]{1,0:T(8,128)(2,1)S(1)} %collective-permute-done.1.other, ...), custom_call_target="tpu_custom_call" | custom-call | tf_op jit(solution)/shard_map/pallas_call | solution.py:98
  4.7 3.0 %collective-permute-start.6 = (bf16[256,512]{1,0:T(8,128)(2,1)S(1)}, bf16[256,512]{1,0:T(8,128)(2,1)S(1)}, u32[]{:S(2)}, u32[]{:S(2)}) collective-permute-start(bf16[256,512]{1,0:T(8,128)(2,1)S(1)} %get-tuple-element.48.refs_3_), channel_id=1, source_target_pairs={{0,1},{2,0},{4,2},{6,4},{7,6},{5,7},{3,5},{1,3},{8,9},{10,8},{12,1... | collective-permute-start | bytes 786440 | tf_op jit(solution)/shard_map/ppermute | solution.py:310
  7.8 1.9 %collective-permute-start.10 = (bf16[256,512]{1,0:T(8,128)(2,1)S(1)}, bf16[256,512]{1,0:T(8,128)(2,1)S(1)}, u32[]{:S(2)}, u32[]{:S(2)}) collective-permute-start(bf16[256,512]{1,0:T(8,128)(2,1)S(1)} %get-tuple-element.49.refs_3_), channel_id=1, source_target_pairs={{0,1},{2,0},{4,2},{6,4},{7,6},{5,7},{3,5},{1,3},{8,9},{10,8},{12,1... | collective-permute-start | bytes 786440 | tf_op jit(solution)/shard_map/ppermute | solution.py:312
  9.8 2.1 %shard_map.66 = (f32[256,1792]{1,0:T(8,128)S(1)}, f32[256,1792]{1,0:T(8,128)S(1)}, bf16[512,1792]{1,0:T(8,128)(2,1)S(1)}, bf16[512,1792]{1,0:T(8,128)(2,1)S(1)}) custom-call(bf16[4096,1792]{1,0:T(8,128)(2,1)} %refs_0_.19, bf16[4096,1792]{1,0:T(8,128)(2,1)} %refs_1_.19, bf16[1792,4096]{1,0:T(8,128)(2,1)} %refs_2_.19, ...), custom_call_target="tpu_custom_call" | custom-call | flops 939524096 | tf_op jit(solution)/shard_map/pallas_call | solution.py:222
  11.9 3.2 %shard_map.67 = (bf16[512,1792]{1,0:T(8,128)(2,1)S(1)}, bf16[512,1792]{1,0:T(8,128)(2,1)S(1)}, bf16[512,1792]{1,0:T(8,128)(2,1)S(1)}, bf16[512,1792]{1,0:T(8,128)(2,1)S(1)}) custom-call(bf16[4096,1792]{1,0:T(8,128)(2,1)} %refs_0_.19, bf16[4096,1792]{1,0:T(8,128)(2,1)} %refs_1_.19, bf16[1792,4096]{1,0:T(8,128)(2,1)} %refs_2_.19, ...), custom_call_target="tpu_custom_call" | custom-call | bytes 16777216 | tf_op jit(solution)/shard_map/pallas_call | solution.py:149
  15.1 2.1 %shard_map.68 = (f32[256,1792]{1,0:T(8,128)S(1)}, f32[256,1792]{1,0:T(8,128)S(1)}, bf16[512,1792]{1,0:T(8,128)(2,1)S(1)}, bf16[512,1792]{1,0:T(8,128)(2,1)S(1)}) custom-call(bf16[4096,1792]{1,0:T(8,128)(2,1)} %refs_0_.19, bf16[4096,1792]{1,0:T(8,128)(2,1)} %refs_1_.19, bf16[1792,4096]{1,0:T(8,128)(2,1)} %refs_2_.19, ...), custom_call_target="tpu_custom_call" | custom-call | flops 939524096 | tf_op jit(solution)/shard_map/pallas_call | solution.py:222
  17.2 2.0 %collective-permute-start.7 = (bf16[256,512]{1,0:T(8,128)(2,1)S(1)}, bf16[256,512]{1,0:T(8,128)(2,1)S(1)}, u32[]{:S(2)}, u32[]{:S(2)}) collective-permute-start(bf16[256,512]{1,0:T(8,128)(2,1)S(1)} %collective-permute-done.6.refs_4_), channel_id=1, source_target_pairs={{0,1},{2,0},{4,2},{6,4},{7,6},{5,7},{3,5},{1,3},{8,9},{10,8},{12,1... | collective-permute-start | bytes 786440 | tf_op jit(solution)/shard_map/ppermute | solution.py:310
  20.5 1.7 %collective-permute-start.13 = (bf16[256,512]{1,0:T(8,128)(2,1)S(1)}, bf16[256,512]{1,0:T(8,128)(2,1)S(1)}, u32[]{:S(2)}, u32[]{:S(2)}) collective-permute-start(bf16[256,512]{1,0:T(8,128)(2,1)S(1)} %collective-permute-done.10.refs_4_), channel_id=1, source_target_pairs={{0,1},{2,0},{4,2},{6,4},{7,6},{5,7},{3,5},{1,3},{8,9},{10,8},{12,1... | collective-permute-start | bytes 786440 | tf_op jit(solution)/shard_map/ppermute | solution.py:312
  22.5 2.6 %shard_map.69 = (f32[256,1792]{1,0:T(8,128)S(1)}, f32[256,1792]{1,0:T(8,128)S(1)}, bf16[512,1792]{1,0:T(8,128)(2,1)S(1)}, bf16[512,1792]{1,0:T(8,128)(2,1)S(1)}) custom-call(bf16[4096,1792]{1,0:T(8,128)(2,1)} %refs_0_.19, bf16[4096,1792]{1,0:T(8,128)(2,1)} %refs_1_.19, bf16[1792,4096]{1,0:T(8,128)(2,1)} %refs_2_.19, ...), custom_call_target="tpu_custom_call", output_to_operand_aliasing={{0}: (9, {}), {1}: (10, {})} | custom-call | flops 1879048192 | tf_op jit(solution)/shard_map/pallas_call | solution.py:222
  25.2 2.6 %shard_map.71 = (f32[256,1792]{1,0:T(8,128)S(1)}, f32[256,1792]{1,0:T(8,128)S(1)}, bf16[512,1792]{1,0:T(8,128)(2,1)S(1)}, bf16[512,1792]{1,0:T(8,128)(2,1)S(1)}) custom-call(bf16[4096,1792]{1,0:T(8,128)(2,1)} %refs_0_.19, bf16[4096,1792]{1,0:T(8,128)(2,1)} %refs_1_.19, bf16[1792,4096]{1,0:T(8,128)(2,1)} %refs_2_.19, ...), custom_call_target="tpu_custom_call", output_to_operand_aliasing={{0}: (9, {}), {1}: (10, {})} | custom-call | flops 1879048192 | tf_op jit(solution)/shard_map/pallas_call | solution.py:222
  27.8 1.8 %collective-permute-start.8 = (bf16[256,512]{1,0:T(8,128)(2,1)S(1)}, bf16[256,512]{1,0:T(8,128)(2,1)S(1)}, u32[]{:S(2)}, u32[]{:S(2)}) collective-permute-start(bf16[256,512]{1,0:T(8,128)(2,1)S(1)} %collective-permute-done.7.refs_4_), channel_id=1, source_target_pairs={{0,1},{2,0},{4,2},{6,4},{7,6},{5,7},{3,5},{1,3},{8,9},{10,8},{12,1... | collective-permute-start | bytes 786440 | tf_op jit(solution)/shard_map/ppermute | solution.py:310
  29.9 2.2 %collective-permute-done.13.refs_4_ = bf16[256,512]{1,0:T(8,128)(2,1)S(1)} collective-permute-done((bf16[256,512]{1,0:T(8,128)(2,1)S(1)}, bf16[256,512]{1,0:T(8,128)(2,1)S(1)}, u32[]{:S(2)}, u32[]{:S(2)}) %collective-permute-start.13) | collective-permute-done | bytes 262176 | tf_op jit(solution)/shard_map/ppermute | solution.py:312
  32.2 1.9 %collective-permute-start.14 = (bf16[256,512]{1,0:T(8,128)(2,1)S(1)}, bf16[256,512]{1,0:T(8,128)(2,1)S(1)}, u32[]{:S(2)}, u32[]{:S(2)}) collective-permute-start(bf16[256,512]{1,0:T(8,128)(2,1)S(1)} %collective-permute-done.13.refs_4_), channel_id=1, source_target_pairs={{0,1},{2,0},{4,2},{6,4},{7,6},{5,7},{3,5},{1,3},{8,9},{10,8},{12,1... | collective-permute-start | bytes 786440 | tf_op jit(solution)/shard_map/ppermute | solution.py:312
  34.2 2.6 %shard_map.74 = (f32[256,1792]{1,0:T(8,128)S(1)}, f32[256,1792]{1,0:T(8,128)S(1)}, bf16[1792,512]{1,0:T(8,128)(2,1)S(1)}, bf16[1792,512]{1,0:T(8,128)(2,1)S(1)}) custom-call(bf16[4096,1792]{1,0:T(8,128)(2,1)} %refs_0_.19, bf16[4096,1792]{1,0:T(8,128)(2,1)} %refs_1_.19, bf16[1792,4096]{1,0:T(8,128)(2,1)} %refs_2_.19, ...), custom_call_target="tpu_custom_call", output_to_operand_aliasing={{0}: (9, {}), {1}: (10, {})} | custom-call | flops 1879048192 | tf_op jit(solution)/shard_map/pallas_call | solution.py:222
  36.8 2.7 %shard_map.70 = (f32[256,1792]{1,0:T(8,128)S(1)}, f32[256,1792]{1,0:T(8,128)S(1)}, bf16[512,1792]{1,0:T(8,128)(2,1)S(1)}, bf16[512,1792]{1,0:T(8,128)(2,1)S(1)}, bf16[1792,512]{1,0:T(8,128)(2,1)S(1)}) custom-call(bf16[4096,1792]{1,0:T(8,128)(2,1)} %refs_0_.19, bf16[4096,1792]{1,0:T(8,128)(2,1)} %refs_1_.19, ...), custom_call_target="tpu_custom_call", output_to_operand_aliasing={{0}: (9, {}), {1}: (10, {})} | custom-call | flops 1879048192 | tf_op jit(solution)/shard_map/pallas_call | solution.py:222
  39.7 1.8 %collective-permute-start.5 = (bf16[256,512]{1,0:T(8,128)(2,1)S(1)}, bf16[256,512]{1,0:T(8,128)(2,1)S(1)}, u32[]{:S(2)}, u32[]{:S(2)}) collective-permute-start(bf16[256,512]{1,0:T(8,128)(2,1)S(1)} %collective-permute-done.4.refs_3_), channel_id=1, source_target_pairs={{0,2},{2,4},{4,6},{6,7},{7,5},{5,3},{3,1},{1,0},{8,10},{10,12},{12... | collective-permute-start | bytes 786440 | tf_op jit(solution)/shard_map/ppermute | solution.py:315
  43.9 2.6 %shard_map.72 = (f32[256,1792]{1,0:T(8,128)S(1)}, f32[256,1792]{1,0:T(8,128)S(1)}, bf16[1792,512]{1,0:T(8,128)(2,1)S(1)}, bf16[1792,512]{1,0:T(8,128)(2,1)S(1)}) custom-call(bf16[4096,1792]{1,0:T(8,128)(2,1)} %refs_0_.19, bf16[4096,1792]{1,0:T(8,128)(2,1)} %refs_1_.19, bf16[1792,4096]{1,0:T(8,128)(2,1)} %refs_2_.19, ...), custom_call_target="tpu_custom_call", output_to_operand_aliasing={{0}: (9, {}), {1}: (10, {})} | custom-call | flops 1879048192 | tf_op jit(solution)/shard_map/pallas_call | solution.py:222
  46.5 2.7 %shard_map.75 = (f32[256,1792]{1,0:T(8,128)S(1)}, f32[256,1792]{1,0:T(8,128)S(1)}, bf16[1792,512]{1,0:T(8,128)(2,1)S(1)}, bf16[1792,512]{1,0:T(8,128)(2,1)S(1)}, bf16[1792,512]{1,0:T(8,128)(2,1)S(1)}) custom-call(bf16[4096,1792]{1,0:T(8,128)(2,1)} %refs_0_.19, bf16[4096,1792]{1,0:T(8,128)(2,1)} %refs_1_.19, ...), custom_call_target="tpu_custom_call", output_to_operand_aliasing={{0}: (9, {}), {1}: (10, {})} | custom-call | flops 1879048192 | tf_op jit(solution)/shard_map/pallas_call | solution.py:222
  60.9 3.1 %collective-permute-done.16.refs_0_ = bf16[256,512]{1,0:T(8,128)(2,1)S(1)} collective-permute-done((bf16[256,512]{1,0:T(8,128)(2,1)S(1)}, bf16[256,512]{1,0:T(8,128)(2,1)S(1)}, u32[]{:S(2)}, u32[]{:S(2)}) %collective-permute-start.16) | collective-permute-done | bytes 262176 | tf_op jit(solution)/shard_map/ppermute | solution.py:329
  65.2 4.4 %collective-permute-done.23.refs_0_ = bf16[256,512]{1,0:T(8,128)(2,1)S(1)} collective-permute-done((bf16[256,512]{1,0:T(8,128)(2,1)S(1)}, bf16[256,512]{1,0:T(8,128)(2,1)S(1)}, u32[]{:S(2)}, u32[]{:S(2)}) %collective-permute-start.23) | collective-permute-done | bytes 262176 | tf_op jit(solution)/shard_map/ppermute | solution.py:333
  76.5 4.4 %collective-permute-done.24.refs_0_ = bf16[256,512]{1,0:T(8,128)(2,1)S(1)} collective-permute-done((bf16[256,512]{1,0:T(8,128)(2,1)S(1)}, bf16[256,512]{1,0:T(8,128)(2,1)S(1)}, u32[]{:S(2)}, u32[]{:S(2)}) %collective-permute-start.24) | collective-permute-done | bytes 262176 | tf_op jit(solution)/shard_map/ppermute | solution.py:333
  89.0 3.0 %collective-permute-done.25.b_f = bf16[256,512]{1,0:T(8,128)(2,1)S(1)} collective-permute-done((bf16[256,512]{1,0:T(8,128)(2,1)S(1)}, bf16[256,512]{1,0:T(8,128)(2,1)S(1)}, u32[]{:S(2)}, u32[]{:S(2)}) %collective-permute-start.25) | collective-permute-done | bytes 262176 | tf_op jit(solution)/shard_map/ppermute | solution.py:339
  92.0 2.8 %collective-permute-done.19.a_f = bf16[256,512]{1,0:T(8,128)(2,1)S(1)} collective-permute-done((bf16[256,512]{1,0:T(8,128)(2,1)S(1)}, bf16[256,512]{1,0:T(8,128)(2,1)S(1)}, u32[]{:S(2)}, u32[]{:S(2)}) %collective-permute-start.19) | collective-permute-done | bytes 262176 | tf_op jit(solution)/shard_map/ppermute | solution.py:338
  (66 shorter events, 34.1 us)
Async XLA Ops:
  4.7 12.6 %collective-permute-start.6 = (bf16[256,512]{1,0:T(8,128)(2,1)S(1)}, bf16[256,512]{1,0:T(8,128)(2,1)S(1)}, u32[]{:S(2)}, u32[]{:S(2)}) collective-permute-start(bf16[256,512]{1,0:T(8,128)(2,1)S(1)} %get-tuple-element.48.refs_3_), channel_id=1, source_target_pairs={{0,1},{2,0},{4,2},{6,4},{7,6},{5,7},{3,5},{1,3},{8,9},{10,8},{12,1... | collective-permute-start | bytes 786440 | tf_op jit(solution)/shard_map/ppermute | solution.py:310
  7.7 11.5 %collective-permute-start.2 = (bf16[256,512]{1,0:T(8,128)(2,1)S(1)}, bf16[256,512]{1,0:T(8,128)(2,1)S(1)}, u32[]{:S(2)}, u32[]{:S(2)}) collective-permute-start(bf16[256,512]{1,0:T(8,128)(2,1)S(1)} %get-tuple-element.48.refs_3_), channel_id=1, source_target_pairs={{0,2},{2,4},{4,6},{6,7},{7,5},{5,3},{3,1},{1,0},{8,10},{10,12},{12... | collective-permute-start | bytes 786440 | tf_op jit(solution)/shard_map/ppermute | solution.py:309
  7.8 12.7 %collective-permute-start.10 = (bf16[256,512]{1,0:T(8,128)(2,1)S(1)}, bf16[256,512]{1,0:T(8,128)(2,1)S(1)}, u32[]{:S(2)}, u32[]{:S(2)}) collective-permute-start(bf16[256,512]{1,0:T(8,128)(2,1)S(1)} %get-tuple-element.49.refs_3_), channel_id=1, source_target_pairs={{0,1},{2,0},{4,2},{6,4},{7,6},{5,7},{3,5},{1,3},{8,9},{10,8},{12,1... | collective-permute-start | bytes 786440 | tf_op jit(solution)/shard_map/ppermute | solution.py:312
  9.7 12.5 %collective-permute-start.9 = (bf16[256,512]{1,0:T(8,128)(2,1)S(1)}, bf16[256,512]{1,0:T(8,128)(2,1)S(1)}, u32[]{:S(2)}, u32[]{:S(2)}) collective-permute-start(bf16[256,512]{1,0:T(8,128)(2,1)S(1)} %get-tuple-element.49.refs_3_), channel_id=1, source_target_pairs={{0,2},{2,4},{4,6},{6,7},{7,5},{5,3},{3,1},{1,0},{8,10},{10,12},{12... | collective-permute-start | bytes 786440 | tf_op jit(solution)/shard_map/ppermute | solution.py:311
  17.2 10.6 %collective-permute-start.7 = (bf16[256,512]{1,0:T(8,128)(2,1)S(1)}, bf16[256,512]{1,0:T(8,128)(2,1)S(1)}, u32[]{:S(2)}, u32[]{:S(2)}) collective-permute-start(bf16[256,512]{1,0:T(8,128)(2,1)S(1)} %collective-permute-done.6.refs_4_), channel_id=1, source_target_pairs={{0,1},{2,0},{4,2},{6,4},{7,6},{5,7},{3,5},{1,3},{8,9},{10,8},{12,1... | collective-permute-start | bytes 786440 | tf_op jit(solution)/shard_map/ppermute | solution.py:310
  19.2 10.4 %collective-permute-start.3 = (bf16[256,512]{1,0:T(8,128)(2,1)S(1)}, bf16[256,512]{1,0:T(8,128)(2,1)S(1)}, u32[]{:S(2)}, u32[]{:S(2)}) collective-permute-start(bf16[256,512]{1,0:T(8,128)(2,1)S(1)} %collective-permute-done.2.refs_3_), channel_id=1, source_target_pairs={{0,2},{2,4},{4,6},{6,7},{7,5},{5,3},{3,1},{1,0},{8,10},{10,12},{12... | collective-permute-start | bytes 786440 | tf_op jit(solution)/shard_map/ppermute | solution.py:309
  20.5 11.7 %collective-permute-start.13 = (bf16[256,512]{1,0:T(8,128)(2,1)S(1)}, bf16[256,512]{1,0:T(8,128)(2,1)S(1)}, u32[]{:S(2)}, u32[]{:S(2)}) collective-permute-start(bf16[256,512]{1,0:T(8,128)(2,1)S(1)} %collective-permute-done.10.refs_4_), channel_id=1, source_target_pairs={{0,1},{2,0},{4,2},{6,4},{7,6},{5,7},{3,5},{1,3},{8,9},{10,8},{12,1... | collective-permute-start | bytes 786440 | tf_op jit(solution)/shard_map/ppermute | solution.py:312
  22.2 11.8 %collective-permute-start.11 = (bf16[256,512]{1,0:T(8,128)(2,1)S(1)}, bf16[256,512]{1,0:T(8,128)(2,1)S(1)}, u32[]{:S(2)}, u32[]{:S(2)}) collective-permute-start(bf16[256,512]{1,0:T(8,128)(2,1)S(1)} %collective-permute-done.9.refs_3_), channel_id=1, source_target_pairs={{0,2},{2,4},{4,6},{6,7},{7,5},{5,3},{3,1},{1,0},{8,10},{10,12},{12... | collective-permute-start | bytes 786440 | tf_op jit(solution)/shard_map/ppermute | solution.py:311
  27.8 16.1 %collective-permute-start.8 = (bf16[256,512]{1,0:T(8,128)(2,1)S(1)}, bf16[256,512]{1,0:T(8,128)(2,1)S(1)}, u32[]{:S(2)}, u32[]{:S(2)}) collective-permute-start(bf16[256,512]{1,0:T(8,128)(2,1)S(1)} %collective-permute-done.7.refs_4_), channel_id=1, source_target_pairs={{0,1},{2,0},{4,2},{6,4},{7,6},{5,7},{3,5},{1,3},{8,9},{10,8},{12,1... | collective-permute-start | bytes 786440 | tf_op jit(solution)/shard_map/ppermute | solution.py:310
  29.6 10.1 %collective-permute-start.4 = (bf16[256,512]{1,0:T(8,128)(2,1)S(1)}, bf16[256,512]{1,0:T(8,128)(2,1)S(1)}, u32[]{:S(2)}, u32[]{:S(2)}) collective-permute-start(bf16[256,512]{1,0:T(8,128)(2,1)S(1)} %collective-permute-done.3.refs_3_), channel_id=1, source_target_pairs={{0,2},{2,4},{4,6},{6,7},{7,5},{5,3},{3,1},{1,0},{8,10},{10,12},{12... | collective-permute-start | bytes 786440 | tf_op jit(solution)/shard_map/ppermute | solution.py:309
  32.2 10.1 %collective-permute-start.14 = (bf16[256,512]{1,0:T(8,128)(2,1)S(1)}, bf16[256,512]{1,0:T(8,128)(2,1)S(1)}, u32[]{:S(2)}, u32[]{:S(2)}) collective-permute-start(bf16[256,512]{1,0:T(8,128)(2,1)S(1)} %collective-permute-done.13.refs_4_), channel_id=1, source_target_pairs={{0,1},{2,0},{4,2},{6,4},{7,6},{5,7},{3,5},{1,3},{8,9},{10,8},{12,1... | collective-permute-start | bytes 786440 | tf_op jit(solution)/shard_map/ppermute | solution.py:312
  34.1 12.5 %collective-permute-start.12 = (bf16[256,512]{1,0:T(8,128)(2,1)S(1)}, bf16[256,512]{1,0:T(8,128)(2,1)S(1)}, u32[]{:S(2)}, u32[]{:S(2)}) collective-permute-start(bf16[256,512]{1,0:T(8,128)(2,1)S(1)} %collective-permute-done.11.refs_3_), channel_id=1, source_target_pairs={{0,2},{2,4},{4,6},{6,7},{7,5},{5,3},{3,1},{1,0},{8,10},{10,12},{12... | collective-permute-start | bytes 786440 | tf_op jit(solution)/shard_map/ppermute | solution.py:311
  39.7 13.2 %collective-permute-start.5 = (bf16[256,512]{1,0:T(8,128)(2,1)S(1)}, bf16[256,512]{1,0:T(8,128)(2,1)S(1)}, u32[]{:S(2)}, u32[]{:S(2)}) collective-permute-start(bf16[256,512]{1,0:T(8,128)(2,1)S(1)} %collective-permute-done.4.refs_3_), channel_id=1, source_target_pairs={{0,2},{2,4},{4,6},{6,7},{7,5},{5,3},{3,1},{1,0},{8,10},{10,12},{12... | collective-permute-start | bytes 786440 | tf_op jit(solution)/shard_map/ppermute | solution.py:315
  54.7 9.3 %collective-permute-start.16 = (bf16[256,512]{1,0:T(8,128)(2,1)S(1)}, bf16[256,512]{1,0:T(8,128)(2,1)S(1)}, u32[]{:S(2)}, u32[]{:S(2)}) collective-permute-start(bf16[256,512]{1,0:T(8,128)(2,1)S(1)} %shard_map.79), channel_id=1, source_target_pairs={{0,2},{2,4},{4,6},{6,7},{7,5},{5,3},{3,1},{1,0},{8,10},{10,12},{12... | collective-permute-start | bytes 786440 | tf_op jit(solution)/shard_map/ppermute | solution.py:329
  55.9 13.7 %collective-permute-start.23 = (bf16[256,512]{1,0:T(8,128)(2,1)S(1)}, bf16[256,512]{1,0:T(8,128)(2,1)S(1)}, u32[]{:S(2)}, u32[]{:S(2)}) collective-permute-start(bf16[256,512]{1,0:T(8,128)(2,1)S(1)} %shard_map.86), channel_id=1, source_target_pairs={{0,2},{2,4},{4,6},{6,7},{7,5},{5,3},{3,1},{1,0},{8,10},{10,12},{12... | collective-permute-start | bytes 786440 | tf_op jit(solution)/shard_map/ppermute | solution.py:333
  58.1 12.7 %collective-permute-start.20 = (bf16[256,512]{1,0:T(8,128)(2,1)S(1)}, bf16[256,512]{1,0:T(8,128)(2,1)S(1)}, u32[]{:S(2)}, u32[]{:S(2)}) collective-permute-start(bf16[256,512]{1,0:T(8,128)(2,1)S(1)} %shard_map.83), channel_id=1, source_target_pairs={{0,1},{2,0},{4,2},{6,4},{7,6},{5,7},{3,5},{1,3},{8,9},{10,8},{12,1... | collective-permute-start | bytes 786440 | tf_op jit(solution)/shard_map/ppermute | solution.py:332
  59.4 13.7 %collective-permute-start.27 = (bf16[256,512]{1,0:T(8,128)(2,1)S(1)}, bf16[256,512]{1,0:T(8,128)(2,1)S(1)}, u32[]{:S(2)}, u32[]{:S(2)}) collective-permute-start(bf16[256,512]{1,0:T(8,128)(2,1)S(1)} %shard_map.90), channel_id=1, source_target_pairs={{0,1},{2,0},{4,2},{6,4},{7,6},{5,7},{3,5},{1,3},{8,9},{10,8},{12,1... | collective-permute-start | bytes 786440 | tf_op jit(solution)/shard_map/ppermute | solution.py:330
  64.6 10.7 %collective-permute-start.17 = (bf16[256,512]{1,0:T(8,128)(2,1)S(1)}, bf16[256,512]{1,0:T(8,128)(2,1)S(1)}, u32[]{:S(2)}, u32[]{:S(2)}) collective-permute-start(bf16[256,512]{1,0:T(8,128)(2,1)S(1)} %shard_map.80), channel_id=1, source_target_pairs={{0,2},{2,4},{4,6},{6,7},{7,5},{5,3},{3,1},{1,0},{8,10},{10,12},{12... | collective-permute-start | bytes 786440 | tf_op jit(solution)/shard_map/ppermute | solution.py:329
  70.2 10.6 %collective-permute-start.24 = (bf16[256,512]{1,0:T(8,128)(2,1)S(1)}, bf16[256,512]{1,0:T(8,128)(2,1)S(1)}, u32[]{:S(2)}, u32[]{:S(2)}) collective-permute-start(bf16[256,512]{1,0:T(8,128)(2,1)S(1)} %shard_map.87), channel_id=1, source_target_pairs={{0,2},{2,4},{4,6},{6,7},{7,5},{5,3},{3,1},{1,0},{8,10},{10,12},{12... | collective-permute-start | bytes 786440 | tf_op jit(solution)/shard_map/ppermute | solution.py:333
  71.5 10.6 %collective-permute-start.21 = (bf16[256,512]{1,0:T(8,128)(2,1)S(1)}, bf16[256,512]{1,0:T(8,128)(2,1)S(1)}, u32[]{:S(2)}, u32[]{:S(2)}) collective-permute-start(bf16[256,512]{1,0:T(8,128)(2,1)S(1)} %shard_map.84), channel_id=1, source_target_pairs={{0,1},{2,0},{4,2},{6,4},{7,6},{5,7},{3,5},{1,3},{8,9},{10,8},{12,1... | collective-permute-start | bytes 786440 | tf_op jit(solution)/shard_map/ppermute | solution.py:332
  73.7 10.6 %collective-permute-start.28 = (bf16[256,512]{1,0:T(8,128)(2,1)S(1)}, bf16[256,512]{1,0:T(8,128)(2,1)S(1)}, u32[]{:S(2)}, u32[]{:S(2)}) collective-permute-start(bf16[256,512]{1,0:T(8,128)(2,1)S(1)} %shard_map.91), channel_id=1, source_target_pairs={{0,1},{2,0},{4,2},{6,4},{7,6},{5,7},{3,5},{1,3},{8,9},{10,8},{12,1... | collective-permute-start | bytes 786440 | tf_op jit(solution)/shard_map/ppermute | solution.py:330
  75.9 10.6 %collective-permute-start.18 = (bf16[256,512]{1,0:T(8,128)(2,1)S(1)}, bf16[256,512]{1,0:T(8,128)(2,1)S(1)}, u32[]{:S(2)}, u32[]{:S(2)}) collective-permute-start(bf16[256,512]{1,0:T(8,128)(2,1)S(1)} %shard_map.81), channel_id=1, source_target_pairs={{0,2},{2,4},{4,6},{6,7},{7,5},{5,3},{3,1},{1,0},{8,10},{10,12},{12... | collective-permute-start | bytes 786440 | tf_op jit(solution)/shard_map/ppermute | solution.py:329
  81.5 10.5 %collective-permute-start.25 = (bf16[256,512]{1,0:T(8,128)(2,1)S(1)}, bf16[256,512]{1,0:T(8,128)(2,1)S(1)}, u32[]{:S(2)}, u32[]{:S(2)}) collective-permute-start(bf16[256,512]{1,0:T(8,128)(2,1)S(1)} %shard_map.88), channel_id=1, source_target_pairs={{0,2},{2,4},{4,6},{6,7},{7,5},{5,3},{3,1},{1,0},{8,10},{10,12},{12... | collective-permute-start | bytes 786440 | tf_op jit(solution)/shard_map/ppermute | solution.py:339
  82.7 9.3 %collective-permute-start.22 = (bf16[256,512]{1,0:T(8,128)(2,1)S(1)}, bf16[256,512]{1,0:T(8,128)(2,1)S(1)}, u32[]{:S(2)}, u32[]{:S(2)}) collective-permute-start(bf16[256,512]{1,0:T(8,128)(2,1)S(1)} %shard_map.85), channel_id=1, source_target_pairs={{0,1},{2,0},{4,2},{6,4},{7,6},{5,7},{3,5},{1,3},{8,9},{10,8},{12,1... | collective-permute-start | bytes 786440 | tf_op jit(solution)/shard_map/ppermute | solution.py:338
  (6 other events, 34.2 us)

commit v4 on v3

--- a/solution.py
+++ b/solution.py
@@ -228,7 +228,7 @@
         input_output_aliases=aliases,
         compiler_params=pltpu.CompilerParams(vmem_limit_bytes=4 * MIB),
         cost_estimate=pl.CostEstimate(
-            flops=4 * rows * width * len(xs) * hid, bytes_accessed=0, transcendentals=0
+            flops=12 * rows * width * len(xs) * hid, bytes_accessed=0, transcendentals=0
         ),
     )(*operands)
     held.update(zip(bring, out[outs:]))
@@ -251,7 +251,7 @@
         out_specs=IN_VMEM,
         compiler_params=pltpu.CompilerParams(vmem_limit_bytes=4 * MIB),
         cost_estimate=pl.CostEstimate(
-            flops=2 * h.size * weight.shape[1], bytes_accessed=0, transcendentals=0
+            flops=6 * h.size * weight.shape[1], bytes_accessed=0, transcendentals=0
         ),
     )(*operands)
 

time: 96 us -> 95 us (0.990)
  starting transfers between devices: 32.6 us -> 30.5 us
    ppermute x2, waiting for transfers between devices: 8.71 us -> 2.6 us  [body(): b_f = term_b(step - 1, lax.ppermute(b_f, 'tp', fwd))]
    ppermute x3, waiting for transfers between devices: 0.01 us -> 6.04 us  [body(): b_b = term_b(-step, lax.ppermute(b_b, 'tp', bwd))]
    ppermute x3, starting transfers between devices: 4.86 us -> 0.89 us  [body(): b_b = term_b(-step, lax.ppermute(b_b, 'tp', bwd))]
    ppermute x1, waiting for transfers between devices: 0.01 us -> 3.32 us  [body(): lax.ppermute(b_b, 'tp', bwd)]
    ppermute x1, waiting for transfers between devices: 3.01 us -> 0.01 us  [body(): lax.ppermute(b_f, 'tp', fwd)]
    ppermute x3, starting transfers between devices: 1.77 us -> 4.72 us  [body(): a_f = term_a(step, lax.ppermute(a_f, 'tp', fwd))]
    ppermute x1, waiting for transfers between devices: 2.8 us -> 0.01 us  [body(): lax.ppermute(a_f, 'tp', fwd)]
    ppermute x3, waiting for transfers between devices: 3.09 us -> 4.78 us  [body(): a_f = term_a(step, lax.ppermute(a_f, 'tp', fwd))]
  transfers between devices with their start and end apart: 30 -> 30, of which waited for: 10 -> 17; matrix products, arithmetic and copies ran while one was open for 0% -> 0% of each run, Pallas kernels for 39% -> 40%
where the time goes in v4:
time: 95 us; the launch traced here: 94.6 us
  Pallas kernels  40.7 us (43%)
  starting transfers between devices  30.5 us (32%)
  waiting for transfers between devices  23 us (24%)
    pallas_call x10, Pallas kernels, stage(): pl.pallas_call(functools.partial(stage_kernel, len(xs), bool(acc), last,...  22.3 us
    pallas_call x16, Pallas kernels, down(): pl.pallas_call(down_kernel, out_shape=jax.ShapeDtypeStruct((h.shape[0], w...  10.2 us
    ppermute x4, starting transfers between devices, body(): b_b = lax.ppermute(b_b, 'tp', bwd)  7.21 us
    ppermute x3, starting transfers between devices, body(): a_b = lax.ppermute(a_b, 'tp', bwd)  6.75 us
    ppermute x3, waiting for transfers between devices, body(): b_b = term_b(-step, lax.ppermute(b_b, 'tp', bwd))  6.04 us
    pallas_call x2, Pallas kernels, fetch(): pl.pallas_call(functools.partial(fetch_kernel, bring, n, len(more)), out_...  5.27 us
    ppermute x3, waiting for transfers between devices, body(): a_f = term_a(step, lax.ppermute(a_f, 'tp', fwd))  4.78 us
    ppermute x3, starting transfers between devices, body(): a_f = term_a(step, lax.ppermute(a_f, 'tp', fwd))  4.72 us
  transfers between devices with their start and end apart: 30, of which 17 were waited for; matrix products, arithmetic and copies ran while one was open for 0% of the time, Pallas kernels for 40%

profile of v4, /device:TPU:0, one launch (start us, length us, event | category | flops | bytes accessed | tf_op | source)
XLA Modules:
  0.0 94.6 jit_solution(10427705967203135441)
XLA Ops:
  0.5 2.1 %shard_map.64 = (bf16[512,1792]{1,0:T(8,128)(2,1)S(1)}, bf16[512,1792]{1,0:T(8,128)(2,1)S(1)}) custom-call(bf16[4096,1792]{1,0:T(8,128)(2,1)} %refs_0_.19, bf16[4096,1792]{1,0:T(8,128)(2,1)} %refs_1_.19, bf16[1792,4096]{1,0:T(8,128)(2,1)} %refs_2_.19), custom_call_target="tpu_custom_call" | custom-call | bytes 8388608 | tf_op jit(solution)/shard_map/pallas_call | solution.py:149
  2.6 2.0 %shard_map.65 = (bf16[256,512]{1,0:T(8,128)(2,1)S(1)}, bf16[256,512]{1,0:T(8,128)(2,1)S(1)}) custom-call(s32[2]{0:T(128)} %mine_c.1, s32[2]{0:T(128)S(1)} %collective-permute-done.other_c, s32[8]{0:T(128)} %order.1, bf16[768,512]{1,0:T(8,128)(2,1)} %mine.1, bf16[768,512]{1,0:T(8,128)(2,1)S(1)} %collective-permute-done.1.other, ...), custom_call_target="tpu_custom_call" | custom-call | tf_op jit(solution)/shard_map/pallas_call | solution.py:98
  4.6 3.0 %collective-permute-start.6 = (bf16[256,512]{1,0:T(8,128)(2,1)S(1)}, bf16[256,512]{1,0:T(8,128)(2,1)S(1)}, u32[]{:S(2)}, u32[]{:S(2)}) collective-permute-start(bf16[256,512]{1,0:T(8,128)(2,1)S(1)} %get-tuple-element.48.refs_3_), channel_id=1, source_target_pairs={{0,1},{2,0},{4,2},{6,4},{7,6},{5,7},{3,5},{1,3},{8,9},{10,8},{12,1... | collective-permute-start | bytes 786440 | tf_op jit(solution)/shard_map/ppermute | solution.py:310
  7.7 1.9 %collective-permute-start.10 = (bf16[256,512]{1,0:T(8,128)(2,1)S(1)}, bf16[256,512]{1,0:T(8,128)(2,1)S(1)}, u32[]{:S(2)}, u32[]{:S(2)}) collective-permute-start(bf16[256,512]{1,0:T(8,128)(2,1)S(1)} %get-tuple-element.49.refs_3_), channel_id=1, source_target_pairs={{0,1},{2,0},{4,2},{6,4},{7,6},{5,7},{3,5},{1,3},{8,9},{10,8},{12,1... | collective-permute-start | bytes 786440 | tf_op jit(solution)/shard_map/ppermute | solution.py:312
  9.8 2.1 %shard_map.66 = (f32[256,1792]{1,0:T(8,128)S(1)}, f32[256,1792]{1,0:T(8,128)S(1)}, bf16[512,1792]{1,0:T(8,128)(2,1)S(1)}, bf16[512,1792]{1,0:T(8,128)(2,1)S(1)}) custom-call(bf16[4096,1792]{1,0:T(8,128)(2,1)} %refs_0_.19, bf16[4096,1792]{1,0:T(8,128)(2,1)} %refs_1_.19, bf16[1792,4096]{1,0:T(8,128)(2,1)} %refs_2_.19, ...), custom_call_target="tpu_custom_call" | custom-call | flops 2818572288 | tf_op jit(solution)/shard_map/pallas_call | solution.py:222
  11.8 3.2 %shard_map.67 = (bf16[512,1792]{1,0:T(8,128)(2,1)S(1)}, bf16[512,1792]{1,0:T(8,128)(2,1)S(1)}, bf16[512,1792]{1,0:T(8,128)(2,1)S(1)}, bf16[512,1792]{1,0:T(8,128)(2,1)S(1)}) custom-call(bf16[4096,1792]{1,0:T(8,128)(2,1)} %refs_0_.19, bf16[4096,1792]{1,0:T(8,128)(2,1)} %refs_1_.19, bf16[1792,4096]{1,0:T(8,128)(2,1)} %refs_2_.19, ...), custom_call_target="tpu_custom_call" | custom-call | bytes 16777216 | tf_op jit(solution)/shard_map/pallas_call | solution.py:149
  15.0 2.1 %shard_map.68 = (f32[256,1792]{1,0:T(8,128)S(1)}, f32[256,1792]{1,0:T(8,128)S(1)}, bf16[512,1792]{1,0:T(8,128)(2,1)S(1)}, bf16[512,1792]{1,0:T(8,128)(2,1)S(1)}) custom-call(bf16[4096,1792]{1,0:T(8,128)(2,1)} %refs_0_.19, bf16[4096,1792]{1,0:T(8,128)(2,1)} %refs_1_.19, bf16[1792,4096]{1,0:T(8,128)(2,1)} %refs_2_.19, ...), custom_call_target="tpu_custom_call" | custom-call | flops 2818572288 | tf_op jit(solution)/shard_map/pallas_call | solution.py:222
  17.1 2.0 %collective-permute-start.7 = (bf16[256,512]{1,0:T(8,128)(2,1)S(1)}, bf16[256,512]{1,0:T(8,128)(2,1)S(1)}, u32[]{:S(2)}, u32[]{:S(2)}) collective-permute-start(bf16[256,512]{1,0:T(8,128)(2,1)S(1)} %collective-permute-done.6.refs_4_), channel_id=1, source_target_pairs={{0,1},{2,0},{4,2},{6,4},{7,6},{5,7},{3,5},{1,3},{8,9},{10,8},{12,1... | collective-permute-start | bytes 786440 | tf_op jit(solution)/shard_map/ppermute | solution.py:310
  22.4 2.6 %shard_map.69 = (f32[256,1792]{1,0:T(8,128)S(1)}, f32[256,1792]{1,0:T(8,128)S(1)}, bf16[512,1792]{1,0:T(8,128)(2,1)S(1)}, bf16[512,1792]{1,0:T(8,128)(2,1)S(1)}) custom-call(bf16[4096,1792]{1,0:T(8,128)(2,1)} %refs_0_.19, bf16[4096,1792]{1,0:T(8,128)(2,1)} %refs_1_.19, bf16[1792,4096]{1,0:T(8,128)(2,1)} %refs_2_.19, ...), custom_call_target="tpu_custom_call", output_to_operand_aliasing={{0}: (9, {}), {1}: (10, {})} | custom-call | flops 5637144576 | tf_op jit(solution)/shard_map/pallas_call | solution.py:222
  25.1 2.6 %shard_map.71 = (f32[256,1792]{1,0:T(8,128)S(1)}, f32[256,1792]{1,0:T(8,128)S(1)}, bf16[512,1792]{1,0:T(8,128)(2,1)S(1)}, bf16[512,1792]{1,0:T(8,128)(2,1)S(1)}) custom-call(bf16[4096,1792]{1,0:T(8,128)(2,1)} %refs_0_.19, bf16[4096,1792]{1,0:T(8,128)(2,1)} %refs_1_.19, bf16[1792,4096]{1,0:T(8,128)(2,1)} %refs_2_.19, ...), custom_call_target="tpu_custom_call", output_to_operand_aliasing={{0}: (9, {}), {1}: (10, {})} | custom-call | flops 5637144576 | tf_op jit(solution)/shard_map/pallas_call | solution.py:222
  27.7 1.8 %collective-permute-start.8 = (bf16[256,512]{1,0:T(8,128)(2,1)S(1)}, bf16[256,512]{1,0:T(8,128)(2,1)S(1)}, u32[]{:S(2)}, u32[]{:S(2)}) collective-permute-start(bf16[256,512]{1,0:T(8,128)(2,1)S(1)} %collective-permute-done.7.refs_4_), channel_id=1, source_target_pairs={{0,1},{2,0},{4,2},{6,4},{7,6},{5,7},{3,5},{1,3},{8,9},{10,8},{12,1... | collective-permute-start | bytes 786440 | tf_op jit(solution)/shard_map/ppermute | solution.py:310
  29.8 2.2 %collective-permute-done.13.refs_4_ = bf16[256,512]{1,0:T(8,128)(2,1)S(1)} collective-permute-done((bf16[256,512]{1,0:T(8,128)(2,1)S(1)}, bf16[256,512]{1,0:T(8,128)(2,1)S(1)}, u32[]{:S(2)}, u32[]{:S(2)}) %collective-permute-start.13) | collective-permute-done | bytes 262176 | tf_op jit(solution)/shard_map/ppermute | solution.py:312
  32.1 1.9 %collective-permute-start.14 = (bf16[256,512]{1,0:T(8,128)(2,1)S(1)}, bf16[256,512]{1,0:T(8,128)(2,1)S(1)}, u32[]{:S(2)}, u32[]{:S(2)}) collective-permute-start(bf16[256,512]{1,0:T(8,128)(2,1)S(1)} %collective-permute-done.13.refs_4_), channel_id=1, source_target_pairs={{0,1},{2,0},{4,2},{6,4},{7,6},{5,7},{3,5},{1,3},{8,9},{10,8},{12,1... | collective-permute-start | bytes 786440 | tf_op jit(solution)/shard_map/ppermute | solution.py:312
  34.1 2.6 %shard_map.74 = (f32[256,1792]{1,0:T(8,128)S(1)}, f32[256,1792]{1,0:T(8,128)S(1)}, bf16[1792,512]{1,0:T(8,128)(2,1)S(1)}, bf16[1792,512]{1,0:T(8,128)(2,1)S(1)}) custom-call(bf16[4096,1792]{1,0:T(8,128)(2,1)} %refs_0_.19, bf16[4096,1792]{1,0:T(8,128)(2,1)} %refs_1_.19, bf16[1792,4096]{1,0:T(8,128)(2,1)} %refs_2_.19, ...), custom_call_target="tpu_custom_call", output_to_operand_aliasing={{0}: (9, {}), {1}: (10, {})} | custom-call | flops 5637144576 | tf_op jit(solution)/shard_map/pallas_call | solution.py:222
  36.7 2.7 %shard_map.70 = (f32[256,1792]{1,0:T(8,128)S(1)}, f32[256,1792]{1,0:T(8,128)S(1)}, bf16[512,1792]{1,0:T(8,128)(2,1)S(1)}, bf16[512,1792]{1,0:T(8,128)(2,1)S(1)}, bf16[1792,512]{1,0:T(8,128)(2,1)S(1)}) custom-call(bf16[4096,1792]{1,0:T(8,128)(2,1)} %refs_0_.19, bf16[4096,1792]{1,0:T(8,128)(2,1)} %refs_1_.19, ...), custom_call_target="tpu_custom_call", output_to_operand_aliasing={{0}: (9, {}), {1}: (10, {})} | custom-call | flops 5637144576 | tf_op jit(solution)/shard_map/pallas_call | solution.py:222
  39.6 1.8 %collective-permute-start.5 = (bf16[256,512]{1,0:T(8,128)(2,1)S(1)}, bf16[256,512]{1,0:T(8,128)(2,1)S(1)}, u32[]{:S(2)}, u32[]{:S(2)}) collective-permute-start(bf16[256,512]{1,0:T(8,128)(2,1)S(1)} %collective-permute-done.4.refs_3_), channel_id=1, source_target_pairs={{0,2},{2,4},{4,6},{6,7},{7,5},{5,3},{3,1},{1,0},{8,10},{10,12},{12... | collective-permute-start | bytes 786440 | tf_op jit(solution)/shard_map/ppermute | solution.py:315
  43.8 2.6 %shard_map.72 = (f32[256,1792]{1,0:T(8,128)S(1)}, f32[256,1792]{1,0:T(8,128)S(1)}, bf16[1792,512]{1,0:T(8,128)(2,1)S(1)}, bf16[1792,512]{1,0:T(8,128)(2,1)S(1)}) custom-call(bf16[4096,1792]{1,0:T(8,128)(2,1)} %refs_0_.19, bf16[4096,1792]{1,0:T(8,128)(2,1)} %refs_1_.19, bf16[1792,4096]{1,0:T(8,128)(2,1)} %refs_2_.19, ...), custom_call_target="tpu_custom_call", output_to_operand_aliasing={{0}: (9, {}), {1}: (10, {})} | custom-call | flops 5637144576 | tf_op jit(solution)/shard_map/pallas_call | solution.py:222
  46.5 2.7 %shard_map.75 = (f32[256,1792]{1,0:T(8,128)S(1)}, f32[256,1792]{1,0:T(8,128)S(1)}, bf16[1792,512]{1,0:T(8,128)(2,1)S(1)}, bf16[1792,512]{1,0:T(8,128)(2,1)S(1)}, bf16[1792,512]{1,0:T(8,128)(2,1)S(1)}) custom-call(bf16[4096,1792]{1,0:T(8,128)(2,1)} %refs_0_.19, bf16[4096,1792]{1,0:T(8,128)(2,1)} %refs_1_.19, ...), custom_call_target="tpu_custom_call", output_to_operand_aliasing={{0}: (9, {}), {1}: (10, {})} | custom-call | flops 5637144576 | tf_op jit(solution)/shard_map/pallas_call | solution.py:222
  59.7 1.8 %collective-permute-start.24 = (bf16[256,512]{1,0:T(8,128)(2,1)S(1)}, bf16[256,512]{1,0:T(8,128)(2,1)S(1)}, u32[]{:S(2)}, u32[]{:S(2)}) collective-permute-start(bf16[256,512]{1,0:T(8,128)(2,1)S(1)} %shard_map.87), channel_id=1, source_target_pairs={{0,2},{2,4},{4,6},{6,7},{7,5},{5,3},{3,1},{1,0},{8,10},{10,12},{12... | collective-permute-start | bytes 786440 | tf_op jit(solution)/shard_map/ppermute | solution.py:333
  62.9 2.2 %collective-permute-done.16.refs_0_ = bf16[256,512]{1,0:T(8,128)(2,1)S(1)} collective-permute-done((bf16[256,512]{1,0:T(8,128)(2,1)S(1)}, bf16[256,512]{1,0:T(8,128)(2,1)S(1)}, u32[]{:S(2)}, u32[]{:S(2)}) %collective-permute-start.16) | collective-permute-done | bytes 262176 | tf_op jit(solution)/shard_map/ppermute | solution.py:329
  68.6 2.2 %collective-permute-done.24.refs_0_ = bf16[256,512]{1,0:T(8,128)(2,1)S(1)} collective-permute-done((bf16[256,512]{1,0:T(8,128)(2,1)S(1)}, bf16[256,512]{1,0:T(8,128)(2,1)S(1)}, u32[]{:S(2)}, u32[]{:S(2)}) %collective-permute-start.24) | collective-permute-done | bytes 262176 | tf_op jit(solution)/shard_map/ppermute | solution.py:333
  74.2 2.2 %collective-permute-done.17.refs_0_ = bf16[256,512]{1,0:T(8,128)(2,1)S(1)} collective-permute-done((bf16[256,512]{1,0:T(8,128)(2,1)S(1)}, bf16[256,512]{1,0:T(8,128)(2,1)S(1)}, u32[]{:S(2)}, u32[]{:S(2)}) %collective-permute-start.17) | collective-permute-done | bytes 262176 | tf_op jit(solution)/shard_map/ppermute | solution.py:329
  79.8 4.9 %collective-permute-done.28.refs_0_ = bf16[256,512]{1,0:T(8,128)(2,1)S(1)} collective-permute-done((bf16[256,512]{1,0:T(8,128)(2,1)S(1)}, bf16[256,512]{1,0:T(8,128)(2,1)S(1)}, u32[]{:S(2)}, u32[]{:S(2)}) %collective-permute-start.28) | collective-permute-done | bytes 262176 | tf_op jit(solution)/shard_map/ppermute | solution.py:330
  90.3 3.3 %collective-permute-done.29.b_b = bf16[256,512]{1,0:T(8,128)(2,1)S(1)} collective-permute-done((bf16[256,512]{1,0:T(8,128)(2,1)S(1)}, bf16[256,512]{1,0:T(8,128)(2,1)S(1)}, u32[]{:S(2)}, u32[]{:S(2)}) %collective-permute-start.29) | collective-permute-done | bytes 262176 | tf_op jit(solution)/shard_map/ppermute | solution.py:339
  (66 shorter events, 35.7 us)
Async XLA Ops:
  4.6 12.6 %collective-permute-start.6 = (bf16[256,512]{1,0:T(8,128)(2,1)S(1)}, bf16[256,512]{1,0:T(8,128)(2,1)S(1)}, u32[]{:S(2)}, u32[]{:S(2)}) collective-permute-start(bf16[256,512]{1,0:T(8,128)(2,1)S(1)} %get-tuple-element.48.refs_3_), channel_id=1, source_target_pairs={{0,1},{2,0},{4,2},{6,4},{7,6},{5,7},{3,5},{1,3},{8,9},{10,8},{12,1... | collective-permute-start | bytes 786440 | tf_op jit(solution)/shard_map/ppermute | solution.py:310
  7.6 11.5 %collective-permute-start.2 = (bf16[256,512]{1,0:T(8,128)(2,1)S(1)}, bf16[256,512]{1,0:T(8,128)(2,1)S(1)}, u32[]{:S(2)}, u32[]{:S(2)}) collective-permute-start(bf16[256,512]{1,0:T(8,128)(2,1)S(1)} %get-tuple-element.48.refs_3_), channel_id=1, source_target_pairs={{0,2},{2,4},{4,6},{6,7},{7,5},{5,3},{3,1},{1,0},{8,10},{10,12},{12... | collective-permute-start | bytes 786440 | tf_op jit(solution)/shard_map/ppermute | solution.py:309
  7.7 12.7 %collective-permute-start.10 = (bf16[256,512]{1,0:T(8,128)(2,1)S(1)}, bf16[256,512]{1,0:T(8,128)(2,1)S(1)}, u32[]{:S(2)}, u32[]{:S(2)}) collective-permute-start(bf16[256,512]{1,0:T(8,128)(2,1)S(1)} %get-tuple-element.49.refs_3_), channel_id=1, source_target_pairs={{0,1},{2,0},{4,2},{6,4},{7,6},{5,7},{3,5},{1,3},{8,9},{10,8},{12,1... | collective-permute-start | bytes 786440 | tf_op jit(solution)/shard_map/ppermute | solution.py:312
  9.6 12.5 %collective-permute-start.9 = (bf16[256,512]{1,0:T(8,128)(2,1)S(1)}, bf16[256,512]{1,0:T(8,128)(2,1)S(1)}, u32[]{:S(2)}, u32[]{:S(2)}) collective-permute-start(bf16[256,512]{1,0:T(8,128)(2,1)S(1)} %get-tuple-element.49.refs_3_), channel_id=1, source_target_pairs={{0,2},{2,4},{4,6},{6,7},{7,5},{5,3},{3,1},{1,0},{8,10},{10,12},{12... | collective-permute-start | bytes 786440 | tf_op jit(solution)/shard_map/ppermute | solution.py:311
  17.1 10.6 %collective-permute-start.7 = (bf16[256,512]{1,0:T(8,128)(2,1)S(1)}, bf16[256,512]{1,0:T(8,128)(2,1)S(1)}, u32[]{:S(2)}, u32[]{:S(2)}) collective-permute-start(bf16[256,512]{1,0:T(8,128)(2,1)S(1)} %collective-permute-done.6.refs_4_), channel_id=1, source_target_pairs={{0,1},{2,0},{4,2},{6,4},{7,6},{5,7},{3,5},{1,3},{8,9},{10,8},{12,1... | collective-permute-start | bytes 786440 | tf_op jit(solution)/shard_map/ppermute | solution.py:310
  19.1 10.4 %collective-permute-start.3 = (bf16[256,512]{1,0:T(8,128)(2,1)S(1)}, bf16[256,512]{1,0:T(8,128)(2,1)S(1)}, u32[]{:S(2)}, u32[]{:S(2)}) collective-permute-start(bf16[256,512]{1,0:T(8,128)(2,1)S(1)} %collective-permute-done.2.refs_3_), channel_id=1, source_target_pairs={{0,2},{2,4},{4,6},{6,7},{7,5},{5,3},{3,1},{1,0},{8,10},{10,12},{12... | collective-permute-start | bytes 786440 | tf_op jit(solution)/shard_map/ppermute | solution.py:309
  20.4 11.7 %collective-permute-start.13 = (bf16[256,512]{1,0:T(8,128)(2,1)S(1)}, bf16[256,512]{1,0:T(8,128)(2,1)S(1)}, u32[]{:S(2)}, u32[]{:S(2)}) collective-permute-start(bf16[256,512]{1,0:T(8,128)(2,1)S(1)} %collective-permute-done.10.refs_4_), channel_id=1, source_target_pairs={{0,1},{2,0},{4,2},{6,4},{7,6},{5,7},{3,5},{1,3},{8,9},{10,8},{12,1... | collective-permute-start | bytes 786440 | tf_op jit(solution)/shard_map/ppermute | solution.py:312
  22.1 11.8 %collective-permute-start.11 = (bf16[256,512]{1,0:T(8,128)(2,1)S(1)}, bf16[256,512]{1,0:T(8,128)(2,1)S(1)}, u32[]{:S(2)}, u32[]{:S(2)}) collective-permute-start(bf16[256,512]{1,0:T(8,128)(2,1)S(1)} %collective-permute-done.9.refs_3_), channel_id=1, source_target_pairs={{0,2},{2,4},{4,6},{6,7},{7,5},{5,3},{3,1},{1,0},{8,10},{10,12},{12... | collective-permute-start | bytes 786440 | tf_op jit(solution)/shard_map/ppermute | solution.py:311
  27.7 16.1 %collective-permute-start.8 = (bf16[256,512]{1,0:T(8,128)(2,1)S(1)}, bf16[256,512]{1,0:T(8,128)(2,1)S(1)}, u32[]{:S(2)}, u32[]{:S(2)}) collective-permute-start(bf16[256,512]{1,0:T(8,128)(2,1)S(1)} %collective-permute-done.7.refs_4_), channel_id=1, source_target_pairs={{0,1},{2,0},{4,2},{6,4},{7,6},{5,7},{3,5},{1,3},{8,9},{10,8},{12,1... | collective-permute-start | bytes 786440 | tf_op jit(solution)/shard_map/ppermute | solution.py:310
  29.5 10.1 %collective-permute-start.4 = (bf16[256,512]{1,0:T(8,128)(2,1)S(1)}, bf16[256,512]{1,0:T(8,128)(2,1)S(1)}, u32[]{:S(2)}, u32[]{:S(2)}) collective-permute-start(bf16[256,512]{1,0:T(8,128)(2,1)S(1)} %collective-permute-done.3.refs_3_), channel_id=1, source_target_pairs={{0,2},{2,4},{4,6},{6,7},{7,5},{5,3},{3,1},{1,0},{8,10},{10,12},{12... | collective-permute-start | bytes 786440 | tf_op jit(solution)/shard_map/ppermute | solution.py:309
  32.1 10.1 %collective-permute-start.14 = (bf16[256,512]{1,0:T(8,128)(2,1)S(1)}, bf16[256,512]{1,0:T(8,128)(2,1)S(1)}, u32[]{:S(2)}, u32[]{:S(2)}) collective-permute-start(bf16[256,512]{1,0:T(8,128)(2,1)S(1)} %collective-permute-done.13.refs_4_), channel_id=1, source_target_pairs={{0,1},{2,0},{4,2},{6,4},{7,6},{5,7},{3,5},{1,3},{8,9},{10,8},{12,1... | collective-permute-start | bytes 786440 | tf_op jit(solution)/shard_map/ppermute | solution.py:312
  34.0 12.5 %collective-permute-start.12 = (bf16[256,512]{1,0:T(8,128)(2,1)S(1)}, bf16[256,512]{1,0:T(8,128)(2,1)S(1)}, u32[]{:S(2)}, u32[]{:S(2)}) collective-permute-start(bf16[256,512]{1,0:T(8,128)(2,1)S(1)} %collective-permute-done.11.refs_3_), channel_id=1, source_target_pairs={{0,2},{2,4},{4,6},{6,7},{7,5},{5,3},{3,1},{1,0},{8,10},{10,12},{12... | collective-permute-start | bytes 786440 | tf_op jit(solution)/shard_map/ppermute | solution.py:311
  39.6 14.5 %collective-permute-start.5 = (bf16[256,512]{1,0:T(8,128)(2,1)S(1)}, bf16[256,512]{1,0:T(8,128)(2,1)S(1)}, u32[]{:S(2)}, u32[]{:S(2)}) collective-permute-start(bf16[256,512]{1,0:T(8,128)(2,1)S(1)} %collective-permute-done.4.refs_3_), channel_id=1, source_target_pairs={{0,2},{2,4},{4,6},{6,7},{7,5},{5,3},{3,1},{1,0},{8,10},{10,12},{12... | collective-permute-start | bytes 786440 | tf_op jit(solution)/shard_map/ppermute | solution.py:315
  53.3 8.9 %collective-permute-start.26 = (bf16[256,512]{1,0:T(8,128)(2,1)S(1)}, bf16[256,512]{1,0:T(8,128)(2,1)S(1)}, u32[]{:S(2)}, u32[]{:S(2)}) collective-permute-start(bf16[256,512]{1,0:T(8,128)(2,1)S(1)} %shard_map.89), channel_id=1, source_target_pairs={{0,1},{2,0},{4,2},{6,4},{7,6},{5,7},{3,5},{1,3},{8,9},{10,8},{12,1... | collective-permute-start | bytes 786440 | tf_op jit(solution)/shard_map/ppermute | solution.py:330
  55.8 9.3 %collective-permute-start.16 = (bf16[256,512]{1,0:T(8,128)(2,1)S(1)}, bf16[256,512]{1,0:T(8,128)(2,1)S(1)}, u32[]{:S(2)}, u32[]{:S(2)}) collective-permute-start(bf16[256,512]{1,0:T(8,128)(2,1)S(1)} %shard_map.79), channel_id=1, source_target_pairs={{0,2},{2,4},{4,6},{6,7},{7,5},{5,3},{3,1},{1,0},{8,10},{10,12},{12... | collective-permute-start | bytes 786440 | tf_op jit(solution)/shard_map/ppermute | solution.py:329
  58.1 9.8 %collective-permute-start.20 = (bf16[256,512]{1,0:T(8,128)(2,1)S(1)}, bf16[256,512]{1,0:T(8,128)(2,1)S(1)}, u32[]{:S(2)}, u32[]{:S(2)}) collective-permute-start(bf16[256,512]{1,0:T(8,128)(2,1)S(1)} %shard_map.83), channel_id=1, source_target_pairs={{0,1},{2,0},{4,2},{6,4},{7,6},{5,7},{3,5},{1,3},{8,9},{10,8},{12,1... | collective-permute-start | bytes 786440 | tf_op jit(solution)/shard_map/ppermute | solution.py:332
  59.7 11.1 %collective-permute-start.24 = (bf16[256,512]{1,0:T(8,128)(2,1)S(1)}, bf16[256,512]{1,0:T(8,128)(2,1)S(1)}, u32[]{:S(2)}, u32[]{:S(2)}) collective-permute-start(bf16[256,512]{1,0:T(8,128)(2,1)S(1)} %shard_map.87), channel_id=1, source_target_pairs={{0,2},{2,4},{4,6},{6,7},{7,5},{5,3},{3,1},{1,0},{8,10},{10,12},{12... | collective-permute-start | bytes 786440 | tf_op jit(solution)/shard_map/ppermute | solution.py:333
  62.8 10.6 %collective-permute-start.27 = (bf16[256,512]{1,0:T(8,128)(2,1)S(1)}, bf16[256,512]{1,0:T(8,128)(2,1)S(1)}, u32[]{:S(2)}, u32[]{:S(2)}) collective-permute-start(bf16[256,512]{1,0:T(8,128)(2,1)S(1)} %shard_map.90), channel_id=1, source_target_pairs={{0,1},{2,0},{4,2},{6,4},{7,6},{5,7},{3,5},{1,3},{8,9},{10,8},{12,1... | collective-permute-start | bytes 786440 | tf_op jit(solution)/shard_map/ppermute | solution.py:330
  65.8 10.6 %collective-permute-start.17 = (bf16[256,512]{1,0:T(8,128)(2,1)S(1)}, bf16[256,512]{1,0:T(8,128)(2,1)S(1)}, u32[]{:S(2)}, u32[]{:S(2)}) collective-permute-start(bf16[256,512]{1,0:T(8,128)(2,1)S(1)} %shard_map.80), channel_id=1, source_target_pairs={{0,2},{2,4},{4,6},{6,7},{7,5},{5,3},{3,1},{1,0},{8,10},{10,12},{12... | collective-permute-start | bytes 786440 | tf_op jit(solution)/shard_map/ppermute | solution.py:329
  68.5 10.6 %collective-permute-start.21 = (bf16[256,512]{1,0:T(8,128)(2,1)S(1)}, bf16[256,512]{1,0:T(8,128)(2,1)S(1)}, u32[]{:S(2)}, u32[]{:S(2)}) collective-permute-start(bf16[256,512]{1,0:T(8,128)(2,1)S(1)} %shard_map.84), channel_id=1, source_target_pairs={{0,1},{2,0},{4,2},{6,4},{7,6},{5,7},{3,5},{1,3},{8,9},{10,8},{12,1... | collective-permute-start | bytes 786440 | tf_op jit(solution)/shard_map/ppermute | solution.py:332
  71.4 18.0 %collective-permute-start.25 = (bf16[256,512]{1,0:T(8,128)(2,1)S(1)}, bf16[256,512]{1,0:T(8,128)(2,1)S(1)}, u32[]{:S(2)}, u32[]{:S(2)}) collective-permute-start(bf16[256,512]{1,0:T(8,128)(2,1)S(1)} %shard_map.88), channel_id=1, source_target_pairs={{0,2},{2,4},{4,6},{6,7},{7,5},{5,3},{3,1},{1,0},{8,10},{10,12},{12... | collective-permute-start | bytes 786440 | tf_op jit(solution)/shard_map/ppermute | solution.py:339
  74.1 10.6 %collective-permute-start.28 = (bf16[256,512]{1,0:T(8,128)(2,1)S(1)}, bf16[256,512]{1,0:T(8,128)(2,1)S(1)}, u32[]{:S(2)}, u32[]{:S(2)}) collective-permute-start(bf16[256,512]{1,0:T(8,128)(2,1)S(1)} %shard_map.91), channel_id=1, source_target_pairs={{0,1},{2,0},{4,2},{6,4},{7,6},{5,7},{3,5},{1,3},{8,9},{10,8},{12,1... | collective-permute-start | bytes 786440 | tf_op jit(solution)/shard_map/ppermute | solution.py:330
  77.0 8.7 %collective-permute-start.18 = (bf16[256,512]{1,0:T(8,128)(2,1)S(1)}, bf16[256,512]{1,0:T(8,128)(2,1)S(1)}, u32[]{:S(2)}, u32[]{:S(2)}) collective-permute-start(bf16[256,512]{1,0:T(8,128)(2,1)S(1)} %shard_map.81), channel_id=1, source_target_pairs={{0,2},{2,4},{4,6},{6,7},{7,5},{5,3},{3,1},{1,0},{8,10},{10,12},{12... | collective-permute-start | bytes 786440 | tf_op jit(solution)/shard_map/ppermute | solution.py:329
  79.7 10.6 %collective-permute-start.22 = (bf16[256,512]{1,0:T(8,128)(2,1)S(1)}, bf16[256,512]{1,0:T(8,128)(2,1)S(1)}, u32[]{:S(2)}, u32[]{:S(2)}) collective-permute-start(bf16[256,512]{1,0:T(8,128)(2,1)S(1)} %shard_map.85), channel_id=1, source_target_pairs={{0,1},{2,0},{4,2},{6,4},{7,6},{5,7},{3,5},{1,3},{8,9},{10,8},{12,1... | collective-permute-start | bytes 786440 | tf_op jit(solution)/shard_map/ppermute | solution.py:338
  (6 other events, 35.3 us)

commit v5 on v4

--- a/solution.py
+++ b/solution.py
@@ -235,17 +235,17 @@
     return out[:outs]
 
 
-def down_kernel(h, weight, *refs):
+def down_kernel(count, h, weight, *refs):
     total = jnp.dot(h[...], weight[...], preferred_element_type=F32)
-    for other in refs[:-1]:
+    for other in refs[:count]:
         total = total + other[...].astype(F32)
     refs[-1][...] = total.astype(refs[-1].dtype)
 
 
-def down(h, weight, *arrived, dtype=BF16):
-    operands = [h, weight, *arrived]
-    return pl.pallas_call(
-        down_kernel,
+def down(h, weight, *arrived, dtype=BF16, after=()):
+    operands = [h, weight, *arrived, *after]
+    return pl.pallas_call(
+        functools.partial(down_kernel, len(arrived)),
         out_shape=jax.ShapeDtypeStruct((h.shape[0], weight.shape[1]), dtype),
         in_specs=[IN_VMEM] * len(operands),
         out_specs=IN_VMEM,
@@ -272,6 +272,40 @@
         out_specs=IN_VMEM,
         compiler_params=pltpu.CompilerParams(vmem_limit_bytes=8 * MIB),
     )(own_a, own_b, *arrived_a, *arrived_b)
+
+
+def join_kernel(term, arrived, out):
+    out[...] = (term[...] + arrived[...].astype(F32)).astype(BF16)
+
+
+def join(term, arrived):
+    return pl.pallas_call(
+        join_kernel,
+        out_shape=jax.ShapeDtypeStruct(term.shape, BF16),
+        in_specs=[IN_VMEM] * 2,
+        out_specs=IN_VMEM,
+        compiler_params=pltpu.CompilerParams(vmem_limit_bytes=4 * MIB),
+        cost_estimate=pl.CostEstimate(flops=0, bytes_accessed=0, transcendentals=0),
+    )(term, arrived)
+
+
+def pair_kernel(h, *refs):
+    for weight, out in zip(refs[:2], refs[2:]):
+        out[...] = jnp.dot(h[...], weight[...], preferred_element_type=F32).astype(BF16)
+
+
+def down_pair(h, *weights):
+    width = weights[0].shape[1]
+    return pl.pallas_call(
+        pair_kernel,
+        out_shape=[jax.ShapeDtypeStruct((h.shape[0], width), BF16)] * 2,
+        in_specs=[IN_VMEM] * 3,
+        out_specs=[IN_VMEM] * 2,
+        compiler_params=pltpu.CompilerParams(vmem_limit_bytes=4 * MIB),
+        cost_estimate=pl.CostEstimate(
+            flops=12 * h.size * width, bytes_accessed=0, transcendentals=0
+        ),
+    )(h, *weights)
 
 
 def both(*steps):
@@ -317,22 +351,24 @@
     (h_a,) = run([a_f], [far], acc_a, last=True)
     (h_b,) = run([b_b], [far], acc_b, last=True)
 
-    def term_a(step, *arrived):
-        return down(h_a, held[DOWN, step], *arrived)
-
-    def term_b(step, *arrived):
-        return down(h_b, held[DOWN, step], *arrived)
-
-    a_f, b_b = term_a(far), term_b(far)
-    a_b, b_f = term_a(1 - far), term_b(far - 1)
+    def hop(h, step, sent, way, start):
+        arrived = lax.ppermute(sent, "tp", way)
+        weight = held[DOWN, step]
+        if start:
+            return down(h, weight, arrived)
+        return join(down(h, weight, dtype=F32, after=[sent]), arrived)
+
+    a_f, a_b = down_pair(h_a, held[DOWN, far], held[DOWN, 1 - far])
+    b_b, b_f = down_pair(h_b, held[DOWN, far], held[DOWN, far - 1])
     for step in range(far - 1, 0, -1):
-        a_f = term_a(step, lax.ppermute(a_f, "tp", fwd))
-        b_b = term_b(-step, lax.ppermute(b_b, "tp", bwd))
+        start = step == far - 1
+        a_f = hop(h_a, step, a_f, fwd, start)
+        b_b = hop(h_b, -step, b_b, bwd, start)
         if step > 1:
-            a_b = term_a(1 - step, lax.ppermute(a_b, "tp", bwd))
-            b_f = term_b(step - 1, lax.ppermute(b_f, "tp", fwd))
+            a_b = hop(h_a, 1 - step, a_b, bwd, start)
+            b_f = hop(h_b, step - 1, b_f, fwd, start)
     last = held[DOWN, 0]
-    own = down(h_a, last, dtype=F32), down(h_b, last, dtype=F32)
+    own = down(h_a, last, dtype=F32, after=[a_b]), down(h_b, last, dtype=F32, after=[b_f])
     return finish(
         *own,
         (lax.ppermute(a_f, "tp", fwd), lax.ppermute(a_b, "tp", bwd)),

time: 95 us -> 94.2 us (level)
  waiting for transfers between devices: 23 us -> 20.2 us
  starting transfers between devices: 30.5 us -> 32.6 us
    ppermute x1, waiting for transfers between devices: 3.32 us -> 0.01 us  [body(): lax.ppermute(b_b, 'tp', bwd)]
    ppermute x10, waiting for transfers between devices: 14.3 us -> 11.3 us  [hop(): arrived = lax.ppermute(sent, 'tp', way)]
    ppermute x1, waiting for transfers between devices: 0.01 us -> 2.81 us  [body(): lax.ppermute(a_f, 'tp', fwd)]
    ppermute x1, waiting for transfers between devices: 0.01 us -> 1.95 us  [body(): lax.ppermute(b_f, 'tp', fwd)]
    ppermute x1, starting transfers between devices: 0.09 us -> 1.67 us  [body(): lax.ppermute(b_b, 'tp', bwd)]
    ppermute x1, starting transfers between devices: 0.1 us -> 1.67 us  [body(): lax.ppermute(a_b, 'tp', bwd)]
    ppermute x1, starting transfers between devices: 1.69 us -> 0.46 us  [body(): lax.ppermute(a_f, 'tp', fwd)]
    ppermute x10, starting transfers between devices: 9.68 us -> 10.9 us  [hop(): arrived = lax.ppermute(sent, 'tp', way)]
  transfers between devices with their start and end apart: 30 -> 30, of which waited for: 17 -> 13; matrix products, arithmetic and copies ran while one was open for 0% -> 0% of each run, Pallas kernels for 40% -> 40%
where the time goes in v5:
time: 94.2 us; the launch traced here: 93.8 us
  Pallas kernels  40.7 us (43%)
  starting transfers between devices  32.6 us (35%)
  waiting for transfers between devices  20.2 us (21%)
    pallas_call x10, Pallas kernels, stage(): pl.pallas_call(functools.partial(stage_kernel, len(xs), bool(acc), last,...  22.3 us
    ppermute x10, waiting for transfers between devices, hop(): arrived = lax.ppermute(sent, 'tp', way)  11.3 us
    ppermute x10, starting transfers between devices, hop(): arrived = lax.ppermute(sent, 'tp', way)  10.9 us
    pallas_call x12, Pallas kernels, down(): pl.pallas_call(functools.partial(down_kernel, len(arrived)), out_shape=ja...  7.59 us
    ppermute x4, starting transfers between devices, body(): b_b = lax.ppermute(b_b, 'tp', bwd)  7.23 us
    ppermute x3, starting transfers between devices, body(): a_b = lax.ppermute(a_b, 'tp', bwd)  6.76 us
    pallas_call x2, Pallas kernels, fetch(): pl.pallas_call(functools.partial(fetch_kernel, bring, n, len(more)), out_...  5.27 us
    ppermute x4, waiting for transfers between devices, body(): b_b = lax.ppermute(b_b, 'tp', bwd)  3.9 us
  transfers between devices with their start and end apart: 30, of which 13 were waited for; matrix products, arithmetic and copies ran while one was open for 0% of the time, Pallas kernels for 40%

profile of v5, /device:TPU:0, one launch (start us, length us, event | category | flops | bytes accessed | tf_op | source)
XLA Modules:
  0.0 93.8 jit_solution(11360477030476981676)
XLA Ops:
  0.5 2.1 %shard_map.64 = (bf16[512,1792]{1,0:T(8,128)(2,1)S(1)}, bf16[512,1792]{1,0:T(8,128)(2,1)S(1)}) custom-call(bf16[4096,1792]{1,0:T(8,128)(2,1)} %refs_0_.19, bf16[4096,1792]{1,0:T(8,128)(2,1)} %refs_1_.19, bf16[1792,4096]{1,0:T(8,128)(2,1)} %refs_2_.19), custom_call_target="tpu_custom_call" | custom-call | bytes 8388608 | tf_op jit(solution)/shard_map/pallas_call | solution.py:149
  2.6 2.1 %shard_map.65 = (bf16[256,512]{1,0:T(8,128)(2,1)S(1)}, bf16[256,512]{1,0:T(8,128)(2,1)S(1)}) custom-call(s32[2]{0:T(128)} %mine_c.1, s32[2]{0:T(128)S(1)} %collective-permute-done.other_c, s32[8]{0:T(128)} %order.1, bf16[768,512]{1,0:T(8,128)(2,1)} %mine.1, bf16[768,512]{1,0:T(8,128)(2,1)S(1)} %collective-permute-done.1.other, ...), custom_call_target="tpu_custom_call" | custom-call | tf_op jit(solution)/shard_map/pallas_call | solution.py:98
  4.7 3.0 %collective-permute-start.6 = (bf16[256,512]{1,0:T(8,128)(2,1)S(1)}, bf16[256,512]{1,0:T(8,128)(2,1)S(1)}, u32[]{:S(2)}, u32[]{:S(2)}) collective-permute-start(bf16[256,512]{1,0:T(8,128)(2,1)S(1)} %get-tuple-element.52.refs_3_), channel_id=1, source_target_pairs={{0,1},{2,0},{4,2},{6,4},{7,6},{5,7},{3,5},{1,3},{8,9},{10,8},{12,1... | collective-permute-start | bytes 786440 | tf_op jit(solution)/shard_map/ppermute | solution.py:344
  7.8 1.9 %collective-permute-start.10 = (bf16[256,512]{1,0:T(8,128)(2,1)S(1)}, bf16[256,512]{1,0:T(8,128)(2,1)S(1)}, u32[]{:S(2)}, u32[]{:S(2)}) collective-permute-start(bf16[256,512]{1,0:T(8,128)(2,1)S(1)} %get-tuple-element.53.refs_3_), channel_id=1, source_target_pairs={{0,1},{2,0},{4,2},{6,4},{7,6},{5,7},{3,5},{1,3},{8,9},{10,8},{12,1... | collective-permute-start | bytes 786440 | tf_op jit(solution)/shard_map/ppermute | solution.py:346
  9.8 2.1 %shard_map.66 = (f32[256,1792]{1,0:T(8,128)S(1)}, f32[256,1792]{1,0:T(8,128)S(1)}, bf16[512,1792]{1,0:T(8,128)(2,1)S(1)}, bf16[512,1792]{1,0:T(8,128)(2,1)S(1)}) custom-call(bf16[4096,1792]{1,0:T(8,128)(2,1)} %refs_0_.19, bf16[4096,1792]{1,0:T(8,128)(2,1)} %refs_1_.19, bf16[1792,4096]{1,0:T(8,128)(2,1)} %refs_2_.19, ...), custom_call_target="tpu_custom_call" | custom-call | flops 2818572288 | tf_op jit(solution)/shard_map/pallas_call | solution.py:222
  11.9 3.2 %shard_map.67 = (bf16[512,1792]{1,0:T(8,128)(2,1)S(1)}, bf16[512,1792]{1,0:T(8,128)(2,1)S(1)}, bf16[512,1792]{1,0:T(8,128)(2,1)S(1)}, bf16[512,1792]{1,0:T(8,128)(2,1)S(1)}) custom-call(bf16[4096,1792]{1,0:T(8,128)(2,1)} %refs_0_.19, bf16[4096,1792]{1,0:T(8,128)(2,1)} %refs_1_.19, bf16[1792,4096]{1,0:T(8,128)(2,1)} %refs_2_.19, ...), custom_call_target="tpu_custom_call" | custom-call | bytes 16777216 | tf_op jit(solution)/shard_map/pallas_call | solution.py:149
  15.1 2.1 %shard_map.68 = (f32[256,1792]{1,0:T(8,128)S(1)}, f32[256,1792]{1,0:T(8,128)S(1)}, bf16[512,1792]{1,0:T(8,128)(2,1)S(1)}, bf16[512,1792]{1,0:T(8,128)(2,1)S(1)}) custom-call(bf16[4096,1792]{1,0:T(8,128)(2,1)} %refs_0_.19, bf16[4096,1792]{1,0:T(8,128)(2,1)} %refs_1_.19, bf16[1792,4096]{1,0:T(8,128)(2,1)} %refs_2_.19, ...), custom_call_target="tpu_custom_call" | custom-call | flops 2818572288 | tf_op jit(solution)/shard_map/pallas_call | solution.py:222
  17.2 2.0 %collective-permute-start.7 = (bf16[256,512]{1,0:T(8,128)(2,1)S(1)}, bf16[256,512]{1,0:T(8,128)(2,1)S(1)}, u32[]{:S(2)}, u32[]{:S(2)}) collective-permute-start(bf16[256,512]{1,0:T(8,128)(2,1)S(1)} %collective-permute-done.6.refs_4_), channel_id=1, source_target_pairs={{0,1},{2,0},{4,2},{6,4},{7,6},{5,7},{3,5},{1,3},{8,9},{10,8},{12,1... | collective-permute-start | bytes 786440 | tf_op jit(solution)/shard_map/ppermute | solution.py:344
  22.3 2.6 %shard_map.69 = (f32[256,1792]{1,0:T(8,128)S(1)}, f32[256,1792]{1,0:T(8,128)S(1)}, bf16[512,1792]{1,0:T(8,128)(2,1)S(1)}, bf16[512,1792]{1,0:T(8,128)(2,1)S(1)}) custom-call(bf16[4096,1792]{1,0:T(8,128)(2,1)} %refs_0_.19, bf16[4096,1792]{1,0:T(8,128)(2,1)} %refs_1_.19, bf16[1792,4096]{1,0:T(8,128)(2,1)} %refs_2_.19, ...), custom_call_target="tpu_custom_call", output_to_operand_aliasing={{0}: (9, {}), {1}: (10, {})} | custom-call | flops 5637144576 | tf_op jit(solution)/shard_map/pallas_call | solution.py:222
  24.9 2.6 %shard_map.71 = (f32[256,1792]{1,0:T(8,128)S(1)}, f32[256,1792]{1,0:T(8,128)S(1)}, bf16[512,1792]{1,0:T(8,128)(2,1)S(1)}, bf16[512,1792]{1,0:T(8,128)(2,1)S(1)}) custom-call(bf16[4096,1792]{1,0:T(8,128)(2,1)} %refs_0_.19, bf16[4096,1792]{1,0:T(8,128)(2,1)} %refs_1_.19, bf16[1792,4096]{1,0:T(8,128)(2,1)} %refs_2_.19, ...), custom_call_target="tpu_custom_call", output_to_operand_aliasing={{0}: (9, {}), {1}: (10, {})} | custom-call | flops 5637144576 | tf_op jit(solution)/shard_map/pallas_call | solution.py:222
  27.6 1.8 %collective-permute-start.8 = (bf16[256,512]{1,0:T(8,128)(2,1)S(1)}, bf16[256,512]{1,0:T(8,128)(2,1)S(1)}, u32[]{:S(2)}, u32[]{:S(2)}) collective-permute-start(bf16[256,512]{1,0:T(8,128)(2,1)S(1)} %collective-permute-done.7.refs_4_), channel_id=1, source_target_pairs={{0,1},{2,0},{4,2},{6,4},{7,6},{5,7},{3,5},{1,3},{8,9},{10,8},{12,1... | collective-permute-start | bytes 786440 | tf_op jit(solution)/shard_map/ppermute | solution.py:344
  29.7 2.5 %collective-permute-done.13.refs_4_ = bf16[256,512]{1,0:T(8,128)(2,1)S(1)} collective-permute-done((bf16[256,512]{1,0:T(8,128)(2,1)S(1)}, bf16[256,512]{1,0:T(8,128)(2,1)S(1)}, u32[]{:S(2)}, u32[]{:S(2)}) %collective-permute-start.13) | collective-permute-done | bytes 262176 | tf_op jit(solution)/shard_map/ppermute | solution.py:346
  32.2 1.9 %collective-permute-start.14 = (bf16[256,512]{1,0:T(8,128)(2,1)S(1)}, bf16[256,512]{1,0:T(8,128)(2,1)S(1)}, u32[]{:S(2)}, u32[]{:S(2)}) collective-permute-start(bf16[256,512]{1,0:T(8,128)(2,1)S(1)} %collective-permute-done.13.refs_4_), channel_id=1, source_target_pairs={{0,1},{2,0},{4,2},{6,4},{7,6},{5,7},{3,5},{1,3},{8,9},{10,8},{12,1... | collective-permute-start | bytes 786440 | tf_op jit(solution)/shard_map/ppermute | solution.py:346
  34.2 2.6 %shard_map.74 = (f32[256,1792]{1,0:T(8,128)S(1)}, f32[256,1792]{1,0:T(8,128)S(1)}, bf16[1792,512]{1,0:T(8,128)(2,1)S(1)}, bf16[1792,512]{1,0:T(8,128)(2,1)S(1)}) custom-call(bf16[4096,1792]{1,0:T(8,128)(2,1)} %refs_0_.19, bf16[4096,1792]{1,0:T(8,128)(2,1)} %refs_1_.19, bf16[1792,4096]{1,0:T(8,128)(2,1)} %refs_2_.19, ...), custom_call_target="tpu_custom_call", output_to_operand_aliasing={{0}: (9, {}), {1}: (10, {})} | custom-call | flops 5637144576 | tf_op jit(solution)/shard_map/pallas_call | solution.py:222
  36.8 2.7 %shard_map.70 = (f32[256,1792]{1,0:T(8,128)S(1)}, f32[256,1792]{1,0:T(8,128)S(1)}, bf16[512,1792]{1,0:T(8,128)(2,1)S(1)}, bf16[512,1792]{1,0:T(8,128)(2,1)S(1)}, bf16[1792,512]{1,0:T(8,128)(2,1)S(1)}) custom-call(bf16[4096,1792]{1,0:T(8,128)(2,1)} %refs_0_.19, bf16[4096,1792]{1,0:T(8,128)(2,1)} %refs_1_.19, ...), custom_call_target="tpu_custom_call", output_to_operand_aliasing={{0}: (9, {}), {1}: (10, {})} | custom-call | flops 5637144576 | tf_op jit(solution)/shard_map/pallas_call | solution.py:222
  39.7 1.8 %collective-permute-start.5 = (bf16[256,512]{1,0:T(8,128)(2,1)S(1)}, bf16[256,512]{1,0:T(8,128)(2,1)S(1)}, u32[]{:S(2)}, u32[]{:S(2)}) collective-permute-start(bf16[256,512]{1,0:T(8,128)(2,1)S(1)} %collective-permute-done.4.refs_3_), channel_id=1, source_target_pairs={{0,2},{2,4},{4,6},{6,7},{7,5},{5,3},{3,1},{1,0},{8,10},{10,12},{12... | collective-permute-start | bytes 786440 | tf_op jit(solution)/shard_map/ppermute | solution.py:349
  43.7 2.6 %shard_map.72 = (f32[256,1792]{1,0:T(8,128)S(1)}, f32[256,1792]{1,0:T(8,128)S(1)}, bf16[1792,512]{1,0:T(8,128)(2,1)S(1)}, bf16[1792,512]{1,0:T(8,128)(2,1)S(1)}) custom-call(bf16[4096,1792]{1,0:T(8,128)(2,1)} %refs_0_.19, bf16[4096,1792]{1,0:T(8,128)(2,1)} %refs_1_.19, bf16[1792,4096]{1,0:T(8,128)(2,1)} %refs_2_.19, ...), custom_call_target="tpu_custom_call", output_to_operand_aliasing={{0}: (9, {}), {1}: (10, {})} | custom-call | flops 5637144576 | tf_op jit(solution)/shard_map/pallas_call | solution.py:222
  46.3 2.7 %shard_map.75 = (f32[256,1792]{1,0:T(8,128)S(1)}, f32[256,1792]{1,0:T(8,128)S(1)}, bf16[1792,512]{1,0:T(8,128)(2,1)S(1)}, bf16[1792,512]{1,0:T(8,128)(2,1)S(1)}, bf16[1792,512]{1,0:T(8,128)(2,1)S(1)}) custom-call(bf16[4096,1792]{1,0:T(8,128)(2,1)} %refs_0_.19, bf16[4096,1792]{1,0:T(8,128)(2,1)} %refs_1_.19, ...), custom_call_target="tpu_custom_call", output_to_operand_aliasing={{0}: (9, {}), {1}: (10, {})} | custom-call | flops 5637144576 | tf_op jit(solution)/shard_map/pallas_call | solution.py:222
  59.8 1.9 %collective-permute-start.16 = (bf16[256,512]{1,0:T(8,128)(2,1)S(1)}, bf16[256,512]{1,0:T(8,128)(2,1)S(1)}, u32[]{:S(2)}, u32[]{:S(2)}) collective-permute-start(bf16[256,512]{1,0:T(8,128)(2,1)S(1)} %shard_map.77.refs_0_), channel_id=1, source_target_pairs={{0,1},{2,0},{4,2},{6,4},{7,6},{5,7},{3,5},{1,3},{8,9},{10,8},{12,1... | collective-permute-start | bytes 786440 | tf_op jit(solution)/shard_map/ppermute | solution.py:355
  63.3 2.0 %collective-permute-done.26.refs_0_ = bf16[256,512]{1,0:T(8,128)(2,1)S(1)} collective-permute-done((bf16[256,512]{1,0:T(8,128)(2,1)S(1)}, bf16[256,512]{1,0:T(8,128)(2,1)S(1)}, u32[]{:S(2)}, u32[]{:S(2)}) %collective-permute-start.26) | collective-permute-done | bytes 262176 | tf_op jit(solution)/shard_map/ppermute | solution.py:355
  76.3 2.6 %collective-permute-done.19.arrived = bf16[256,512]{1,0:T(8,128)(2,1)S(1)} collective-permute-done((bf16[256,512]{1,0:T(8,128)(2,1)S(1)}, bf16[256,512]{1,0:T(8,128)(2,1)S(1)}, u32[]{:S(2)}, u32[]{:S(2)}) %collective-permute-start.19) | collective-permute-done | bytes 262176 | tf_op jit(solution)/shard_map/ppermute | solution.py:355
  82.4 2.1 %collective-permute-done.22.arrived = bf16[256,512]{1,0:T(8,128)(2,1)S(1)} collective-permute-done((bf16[256,512]{1,0:T(8,128)(2,1)S(1)}, bf16[256,512]{1,0:T(8,128)(2,1)S(1)}, u32[]{:S(2)}, u32[]{:S(2)}) %collective-permute-start.22) | collective-permute-done | bytes 262176 | tf_op jit(solution)/shard_map/ppermute | solution.py:355
  88.0 1.9 %collective-permute-done.25.b_f = bf16[256,512]{1,0:T(8,128)(2,1)S(1)} collective-permute-done((bf16[256,512]{1,0:T(8,128)(2,1)S(1)}, bf16[256,512]{1,0:T(8,128)(2,1)S(1)}, u32[]{:S(2)}, u32[]{:S(2)}) %collective-permute-start.25) | collective-permute-done | bytes 262176 | tf_op jit(solution)/shard_map/ppermute | solution.py:375
  90.0 2.8 %collective-permute-done.23.a_f = bf16[256,512]{1,0:T(8,128)(2,1)S(1)} collective-permute-done((bf16[256,512]{1,0:T(8,128)(2,1)S(1)}, bf16[256,512]{1,0:T(8,128)(2,1)S(1)}, u32[]{:S(2)}, u32[]{:S(2)}) %collective-permute-start.23) | collective-permute-done | bytes 262176 | tf_op jit(solution)/shard_map/ppermute | solution.py:374
  (70 shorter events, 37.8 us)
Async XLA Ops:
  4.7 12.6 %collective-permute-start.6 = (bf16[256,512]{1,0:T(8,128)(2,1)S(1)}, bf16[256,512]{1,0:T(8,128)(2,1)S(1)}, u32[]{:S(2)}, u32[]{:S(2)}) collective-permute-start(bf16[256,512]{1,0:T(8,128)(2,1)S(1)} %get-tuple-element.52.refs_3_), channel_id=1, source_target_pairs={{0,1},{2,0},{4,2},{6,4},{7,6},{5,7},{3,5},{1,3},{8,9},{10,8},{12,1... | collective-permute-start | bytes 786440 | tf_op jit(solution)/shard_map/ppermute | solution.py:344
  7.7 11.5 %collective-permute-start.2 = (bf16[256,512]{1,0:T(8,128)(2,1)S(1)}, bf16[256,512]{1,0:T(8,128)(2,1)S(1)}, u32[]{:S(2)}, u32[]{:S(2)}) collective-permute-start(bf16[256,512]{1,0:T(8,128)(2,1)S(1)} %get-tuple-element.52.refs_3_), channel_id=1, source_target_pairs={{0,2},{2,4},{4,6},{6,7},{7,5},{5,3},{3,1},{1,0},{8,10},{10,12},{12... | collective-permute-start | bytes 786440 | tf_op jit(solution)/shard_map/ppermute | solution.py:343
  7.8 12.4 %collective-permute-start.10 = (bf16[256,512]{1,0:T(8,128)(2,1)S(1)}, bf16[256,512]{1,0:T(8,128)(2,1)S(1)}, u32[]{:S(2)}, u32[]{:S(2)}) collective-permute-start(bf16[256,512]{1,0:T(8,128)(2,1)S(1)} %get-tuple-element.53.refs_3_), channel_id=1, source_target_pairs={{0,1},{2,0},{4,2},{6,4},{7,6},{5,7},{3,5},{1,3},{8,9},{10,8},{12,1... | collective-permute-start | bytes 786440 | tf_op jit(solution)/shard_map/ppermute | solution.py:346
  9.7 12.3 %collective-permute-start.9 = (bf16[256,512]{1,0:T(8,128)(2,1)S(1)}, bf16[256,512]{1,0:T(8,128)(2,1)S(1)}, u32[]{:S(2)}, u32[]{:S(2)}) collective-permute-start(bf16[256,512]{1,0:T(8,128)(2,1)S(1)} %get-tuple-element.53.refs_3_), channel_id=1, source_target_pairs={{0,2},{2,4},{4,6},{6,7},{7,5},{5,3},{3,1},{1,0},{8,10},{10,12},{12... | collective-permute-start | bytes 786440 | tf_op jit(solution)/shard_map/ppermute | solution.py:345
  17.2 10.3 %collective-permute-start.7 = (bf16[256,512]{1,0:T(8,128)(2,1)S(1)}, bf16[256,512]{1,0:T(8,128)(2,1)S(1)}, u32[]{:S(2)}, u32[]{:S(2)}) collective-permute-start(bf16[256,512]{1,0:T(8,128)(2,1)S(1)} %collective-permute-done.6.refs_4_), channel_id=1, source_target_pairs={{0,1},{2,0},{4,2},{6,4},{7,6},{5,7},{3,5},{1,3},{8,9},{10,8},{12,1... | collective-permute-start | bytes 786440 | tf_op jit(solution)/shard_map/ppermute | solution.py:344
  19.2 10.2 %collective-permute-start.3 = (bf16[256,512]{1,0:T(8,128)(2,1)S(1)}, bf16[256,512]{1,0:T(8,128)(2,1)S(1)}, u32[]{:S(2)}, u32[]{:S(2)}) collective-permute-start(bf16[256,512]{1,0:T(8,128)(2,1)S(1)} %collective-permute-done.2.refs_3_), channel_id=1, source_target_pairs={{0,2},{2,4},{4,6},{6,7},{7,5},{5,3},{3,1},{1,0},{8,10},{10,12},{12... | collective-permute-start | bytes 786440 | tf_op jit(solution)/shard_map/ppermute | solution.py:343
  20.3 11.9 %collective-permute-start.13 = (bf16[256,512]{1,0:T(8,128)(2,1)S(1)}, bf16[256,512]{1,0:T(8,128)(2,1)S(1)}, u32[]{:S(2)}, u32[]{:S(2)}) collective-permute-start(bf16[256,512]{1,0:T(8,128)(2,1)S(1)} %collective-permute-done.10.refs_4_), channel_id=1, source_target_pairs={{0,1},{2,0},{4,2},{6,4},{7,6},{5,7},{3,5},{1,3},{8,9},{10,8},{12,1... | collective-permute-start | bytes 786440 | tf_op jit(solution)/shard_map/ppermute | solution.py:346
  22.0 12.1 %collective-permute-start.11 = (bf16[256,512]{1,0:T(8,128)(2,1)S(1)}, bf16[256,512]{1,0:T(8,128)(2,1)S(1)}, u32[]{:S(2)}, u32[]{:S(2)}) collective-permute-start(bf16[256,512]{1,0:T(8,128)(2,1)S(1)} %collective-permute-done.9.refs_3_), channel_id=1, source_target_pairs={{0,2},{2,4},{4,6},{6,7},{7,5},{5,3},{3,1},{1,0},{8,10},{10,12},{12... | collective-permute-start | bytes 786440 | tf_op jit(solution)/shard_map/ppermute | solution.py:345
  27.6 16.1 %collective-permute-start.8 = (bf16[256,512]{1,0:T(8,128)(2,1)S(1)}, bf16[256,512]{1,0:T(8,128)(2,1)S(1)}, u32[]{:S(2)}, u32[]{:S(2)}) collective-permute-start(bf16[256,512]{1,0:T(8,128)(2,1)S(1)} %collective-permute-done.7.refs_4_), channel_id=1, source_target_pairs={{0,1},{2,0},{4,2},{6,4},{7,6},{5,7},{3,5},{1,3},{8,9},{10,8},{12,1... | collective-permute-start | bytes 786440 | tf_op jit(solution)/shard_map/ppermute | solution.py:344
  29.4 10.3 %collective-permute-start.4 = (bf16[256,512]{1,0:T(8,128)(2,1)S(1)}, bf16[256,512]{1,0:T(8,128)(2,1)S(1)}, u32[]{:S(2)}, u32[]{:S(2)}) collective-permute-start(bf16[256,512]{1,0:T(8,128)(2,1)S(1)} %collective-permute-done.3.refs_3_), channel_id=1, source_target_pairs={{0,2},{2,4},{4,6},{6,7},{7,5},{5,3},{3,1},{1,0},{8,10},{10,12},{12... | collective-permute-start | bytes 786440 | tf_op jit(solution)/shard_map/ppermute | solution.py:343
  32.2 9.8 %collective-permute-start.14 = (bf16[256,512]{1,0:T(8,128)(2,1)S(1)}, bf16[256,512]{1,0:T(8,128)(2,1)S(1)}, u32[]{:S(2)}, u32[]{:S(2)}) collective-permute-start(bf16[256,512]{1,0:T(8,128)(2,1)S(1)} %collective-permute-done.13.refs_4_), channel_id=1, source_target_pairs={{0,1},{2,0},{4,2},{6,4},{7,6},{5,7},{3,5},{1,3},{8,9},{10,8},{12,1... | collective-permute-start | bytes 786440 | tf_op jit(solution)/shard_map/ppermute | solution.py:346
  34.1 12.3 %collective-permute-start.12 = (bf16[256,512]{1,0:T(8,128)(2,1)S(1)}, bf16[256,512]{1,0:T(8,128)(2,1)S(1)}, u32[]{:S(2)}, u32[]{:S(2)}) collective-permute-start(bf16[256,512]{1,0:T(8,128)(2,1)S(1)} %collective-permute-done.11.refs_3_), channel_id=1, source_target_pairs={{0,2},{2,4},{4,6},{6,7},{7,5},{5,3},{3,1},{1,0},{8,10},{10,12},{12... | collective-permute-start | bytes 786440 | tf_op jit(solution)/shard_map/ppermute | solution.py:345
  39.7 9.3 %collective-permute-start.5 = (bf16[256,512]{1,0:T(8,128)(2,1)S(1)}, bf16[256,512]{1,0:T(8,128)(2,1)S(1)}, u32[]{:S(2)}, u32[]{:S(2)}) collective-permute-start(bf16[256,512]{1,0:T(8,128)(2,1)S(1)} %collective-permute-done.4.refs_3_), channel_id=1, source_target_pairs={{0,2},{2,4},{4,6},{6,7},{7,5},{5,3},{3,1},{1,0},{8,10},{10,12},{12... | collective-permute-start | bytes 786440 | tf_op jit(solution)/shard_map/ppermute | solution.py:349
  42.0 11.4 %collective-permute-start.17 = (bf16[256,512]{1,0:T(8,128)(2,1)S(1)}, bf16[256,512]{1,0:T(8,128)(2,1)S(1)}, u32[]{:S(2)}, u32[]{:S(2)}) collective-permute-start(bf16[256,512]{1,0:T(8,128)(2,1)S(1)} %collective-permute-done.14.refs_4_), channel_id=1, source_target_pairs={{0,1},{2,0},{4,2},{6,4},{7,6},{5,7},{3,5},{1,3},{8,9},{10,8},{12,1... | collective-permute-start | bytes 786440 | tf_op jit(solution)/shard_map/ppermute | solution.py:350
  52.9 9.2 %collective-permute-start.20 = (bf16[256,512]{1,0:T(8,128)(2,1)S(1)}, bf16[256,512]{1,0:T(8,128)(2,1)S(1)}, u32[]{:S(2)}, u32[]{:S(2)}) collective-permute-start(bf16[256,512]{1,0:T(8,128)(2,1)S(1)} %get-tuple-element.95), channel_id=1, source_target_pairs={{0,2},{2,4},{4,6},{6,7},{7,5},{5,3},{3,1},{1,0},{8,10},{10,12},{12... | collective-permute-start | bytes 786440 | tf_op jit(solution)/shard_map/ppermute | solution.py:355
  55.7 13.3 %collective-permute-start.18 = (bf16[256,512]{1,0:T(8,128)(2,1)S(1)}, bf16[256,512]{1,0:T(8,128)(2,1)S(1)}, u32[]{:S(2)}, u32[]{:S(2)}) collective-permute-start(bf16[256,512]{1,0:T(8,128)(2,1)S(1)} %get-tuple-element.94), channel_id=1, source_target_pairs={{0,2},{2,4},{4,6},{6,7},{7,5},{5,3},{3,1},{1,0},{8,10},{10,12},{12... | collective-permute-start | bytes 786440 | tf_op jit(solution)/shard_map/ppermute | solution.py:355
  56.1 9.2 %collective-permute-start.26 = (bf16[256,512]{1,0:T(8,128)(2,1)S(1)}, bf16[256,512]{1,0:T(8,128)(2,1)S(1)}, u32[]{:S(2)}, u32[]{:S(2)}) collective-permute-start(bf16[256,512]{1,0:T(8,128)(2,1)S(1)} %get-tuple-element.96), channel_id=1, source_target_pairs={{0,1},{2,0},{4,2},{6,4},{7,6},{5,7},{3,5},{1,3},{8,9},{10,8},{12,1... | collective-permute-start | bytes 786440 | tf_op jit(solution)/shard_map/ppermute | solution.py:355
  59.8 19.6 %collective-permute-start.16 = (bf16[256,512]{1,0:T(8,128)(2,1)S(1)}, bf16[256,512]{1,0:T(8,128)(2,1)S(1)}, u32[]{:S(2)}, u32[]{:S(2)}) collective-permute-start(bf16[256,512]{1,0:T(8,128)(2,1)S(1)} %shard_map.77.refs_0_), channel_id=1, source_target_pairs={{0,1},{2,0},{4,2},{6,4},{7,6},{5,7},{3,5},{1,3},{8,9},{10,8},{12,1... | collective-permute-start | bytes 786440 | tf_op jit(solution)/shard_map/ppermute | solution.py:355
  62.8 9.7 %collective-permute-start.21 = (bf16[256,512]{1,0:T(8,128)(2,1)S(1)}, bf16[256,512]{1,0:T(8,128)(2,1)S(1)}, u32[]{:S(2)}, u32[]{:S(2)}) collective-permute-start(bf16[256,512]{1,0:T(8,128)(2,1)S(1)} %shard_map.87.refs_0_), channel_id=1, source_target_pairs={{0,2},{2,4},{4,6},{6,7},{7,5},{5,3},{3,1},{1,0},{8,10},{10,12},{12... | collective-permute-start | bytes 786440 | tf_op jit(solution)/shard_map/ppermute | solution.py:355
  69.6 9.3 %collective-permute-start.19 = (bf16[256,512]{1,0:T(8,128)(2,1)S(1)}, bf16[256,512]{1,0:T(8,128)(2,1)S(1)}, u32[]{:S(2)}, u32[]{:S(2)}) collective-permute-start(bf16[256,512]{1,0:T(8,128)(2,1)S(1)} %shard_map.83.refs_0_), channel_id=1, source_target_pairs={{0,2},{2,4},{4,6},{6,7},{7,5},{5,3},{3,1},{1,0},{8,10},{10,12},{12... | collective-permute-start | bytes 786440 | tf_op jit(solution)/shard_map/ppermute | solution.py:355
  72.5 12.0 %collective-permute-start.22 = (bf16[256,512]{1,0:T(8,128)(2,1)S(1)}, bf16[256,512]{1,0:T(8,128)(2,1)S(1)}, u32[]{:S(2)}, u32[]{:S(2)}) collective-permute-start(bf16[256,512]{1,0:T(8,128)(2,1)S(1)} %shard_map.89.refs_0_), channel_id=1, source_target_pairs={{0,2},{2,4},{4,6},{6,7},{7,5},{5,3},{3,1},{1,0},{8,10},{10,12},{12... | collective-permute-start | bytes 786440 | tf_op jit(solution)/shard_map/ppermute | solution.py:355
  74.7 10.3 %collective-permute-start.28 = (bf16[256,512]{1,0:T(8,128)(2,1)S(1)}, bf16[256,512]{1,0:T(8,128)(2,1)S(1)}, u32[]{:S(2)}, u32[]{:S(2)}) collective-permute-start(bf16[256,512]{1,0:T(8,128)(2,1)S(1)} %shard_map.94.refs_0_), channel_id=1, source_target_pairs={{0,1},{2,0},{4,2},{6,4},{7,6},{5,7},{3,5},{1,3},{8,9},{10,8},{12,1... | collective-permute-start | bytes 786440 | tf_op jit(solution)/shard_map/ppermute | solution.py:355
  79.0 11.0 %collective-permute-start.25 = (bf16[256,512]{1,0:T(8,128)(2,1)S(1)}, bf16[256,512]{1,0:T(8,128)(2,1)S(1)}, u32[]{:S(2)}, u32[]{:S(2)}) collective-permute-start(bf16[256,512]{1,0:T(8,128)(2,1)S(1)} %shard_map.85.refs_0_), channel_id=1, source_target_pairs={{0,2},{2,4},{4,6},{6,7},{7,5},{5,3},{3,1},{1,0},{8,10},{10,12},{12... | collective-permute-start | bytes 786440 | tf_op jit(solution)/shard_map/ppermute | solution.py:375
  79.5 10.5 %collective-permute-start.24 = (bf16[256,512]{1,0:T(8,128)(2,1)S(1)}, bf16[256,512]{1,0:T(8,128)(2,1)S(1)}, u32[]{:S(2)}, u32[]{:S(2)}) collective-permute-start(bf16[256,512]{1,0:T(8,128)(2,1)S(1)} %shard_map.79.refs_0_), channel_id=1, source_target_pairs={{0,1},{2,0},{4,2},{6,4},{7,6},{5,7},{3,5},{1,3},{8,9},{10,8},{12,1... | collective-permute-start | bytes 786440 | tf_op jit(solution)/shard_map/ppermute | solution.py:374
  (6 other events, 37.2 us)
